TPU v7x, 32 devices: a whole 2x2x4 slice. The times are simulated.
32 devices in a mesh: groups: 2 (over y), ctx: 4 (over z), dp: 2 (over x), mp: 2 (over core).
Axes of the slice: x: 2, y: 2, z: 4, core: 2. Of those that a mesh axis runs over, the one named last changes fastest.
Arguments:
- mixer_input: bfloat16 [4, 4096, 4096], P(('groups', 'dp'), 'ctx', 'mp'), parts along dimension 0, may hold values from -6 to 6
- gate_input: bfloat16 [4, 4096, 4096], P(('groups', 'dp'), 'ctx', 'mp'), parts along dimension 0, may hold values from -6 to 6
- input_proj: bfloat16 [4, 4096, 128], P(('groups', 'dp'), 'ctx'), parts along dimension 0, may hold values from -6 to 6
- output_proj: bfloat16 [4, 4096, 128], P(('groups', 'dp'), 'ctx'), parts along dimension 0, may hold values from -6 to 6
- step_raw: float32 [4, 32, 4096], P(('groups', 'dp'), 'mp', 'ctx'), parts along dimension 0, may hold values from -1 to 1
- decay_rate: float32 [32], P('mp'), may hold values from 2.4414063e-05 to 0.05
- norm_gain: float32 [4096], P('mp'), may hold values from 0.1 to 1.9
- doc_lengths: int32 [4, 16], P(('groups', 'dp')), parts along dimension 0, may hold values from 1 to 3072, 4096 in all within a row
- partner: int32 [64], P(('groups', 'dp')), parts along dimension 0, may hold values from 0 to 31, as said below
Outputs:
- mixed: bfloat16 [4, 4096, 4096], P(('groups', 'dp'), 'ctx', 'mp'), parts along dimension 0
- embedding: float32 [64, 4096], P(('groups', 'dp'), 'mp'), parts along dimension 0
- doc_loss: float32 [64], P(('groups', 'dp')), parts along dimension 0
There are 2 independent parts, one for each index of `groups`. A program takes and returns all parts, laid end to end along the dimension named above; an argument that names none is the same for every part. Nothing has to cross between parts.
Inputs may be any that keep to these rules, and one draw needn't show every extreme that they name: `doc_lengths`: each row's lengths sum to 4096; the largest of each row is exactly 3072. partner pairs the documents: partner[partner[i]] = i and partner[i] != i.
All inputs are finite; a program needn't handle non-finite values.
Results may differ from a plain program's by a relative error of at most 0.005.
Values sent between devices are 32-bit elements; how exact they have to be, the bound alone decides.
No kernel may reach another device: no remote copies, remote signals or barrier semaphores. Data moves between devices by JAX's collectives and lax.ppermute only.
A program may use at most 128 MiB of HBM per device.

v0:
```python
import jax
import jax.numpy as jnp
from jax import lax
from jax.sharding import PartitionSpec as P

SPAN = 256
WIDTH = 4096


HIGH = lax.Precision.HIGHEST


def shifted(x, axis, by):
    count = lax.axis_size(axis)
    pairs = [(i, i + by) for i in range(count) if 0 <= i + by < count]
    return lax.ppermute(x, axis, pairs)


def doc_index(places, ends):
    found = jnp.sum((places[:, None] >= ends[None, :]).astype(jnp.int32), axis=1)
    return jnp.where(places < 0, -1, found)


def advance(carry, items):
    state, decay_prod = carry
    block_state, block_decay = items
    return (
        (block_decay[:, None, None] * state + block_state, decay_prod * block_decay),
        (state, decay_prod),
    )


def on_device(
    mixer_input,
    gate_input,
    input_proj,
    output_proj,
    step_raw,
    decay_rate,
    norm_gain,
    doc_lengths,
    partner,
):
    tok_count = mixer_input.shape[1]
    local_heads = decay_rate.shape[0]
    head_size = mixer_input.shape[2] // local_heads
    state_size = input_proj.shape[2]
    nblocks = tok_count // SPAN
    ctx_place = lax.axis_index("ctx")
    lengths = doc_lengths[0]
    ends = jnp.cumsum(lengths)
    places = ctx_place * tok_count + jnp.arange(tok_count, dtype=jnp.int32)
    doc_ids = doc_index(places, ends)
    block_starts = ctx_place * tok_count + jnp.arange(nblocks, dtype=jnp.int32) * SPAN - 1
    before = doc_index(block_starts, ends)
    steps = jax.nn.softplus(step_raw[0])
    logdecay = -decay_rate[:, None] * steps
    cumlog = jnp.cumsum(logdecay.reshape(local_heads, nblocks, SPAN), axis=2)
    step_blocks = steps.reshape(local_heads, nblocks, SPAN)
    doc_blocks = doc_ids.reshape(nblocks, SPAN)
    lower = jnp.tril(jnp.ones((SPAN, SPAN), dtype=bool))
    same = (doc_blocks[:, :, None] == doc_blocks[:, None, :]) & lower[None]
    in_blocks = input_proj[0].reshape(nblocks, SPAN, state_size)
    out_blocks = output_proj[0].reshape(nblocks, SPAN, state_size)
    scores = jnp.einsum("cis,cjs->cij", out_blocks, in_blocks, preferred_element_type=jnp.float32)
    spread = cumlog[:, :, :, None] - cumlog[:, :, None, :]
    factor = jnp.where(same[None], jnp.exp(jnp.where(same[None], spread, 0.0)), 0.0)
    weights = (scores[None] * factor * step_blocks[:, :, None, :]).astype(jnp.bfloat16)
    inputs = mixer_input[0].reshape(nblocks, SPAN, local_heads, head_size)
    intra = jnp.einsum("hcij,cjhp->cihp", weights, inputs, preferred_element_type=jnp.float32)
    tail = (
        jnp.exp(cumlog[:, :, -1:] - cumlog)
        * (doc_blocks == doc_blocks[:, -1:])[None].astype(jnp.float32)
        * step_blocks
    )
    carried = (inputs * tail.transpose(1, 2, 0)[:, :, :, None]).astype(jnp.bfloat16)
    block_state = jnp.einsum(
        "cjs,cjhp->chsp", in_blocks, carried, preferred_element_type=jnp.float32
    )
    block_decay = jnp.exp(cumlog[:, :, -1]) * (doc_blocks[:, -1] == before)[None].astype(
        jnp.float32
    )
    start = (
        jnp.zeros((local_heads, state_size, head_size), jnp.float32),
        jnp.ones((local_heads,), jnp.float32),
    )
    (dev_state, dev_decay), (state_in, decay_before) = lax.scan(
        advance, start, (block_state, block_decay.T)
    )
    entry = jnp.exp(cumlog) * (doc_blocks == before[:, None])[None].astype(jnp.float32)
    out_float = out_blocks.astype(jnp.float32)
    local_part = (
        jnp.einsum("cis,chsp->cihp", out_float, state_in, precision=HIGH)
        * entry.transpose(1, 2, 0)[:, :, :, None]
    )
    empty_state = jnp.zeros((local_heads, state_size, head_size), jnp.float32)

    def relay(step_index, incoming):
        sent = dev_decay[:, None, None] * incoming + dev_state
        return shifted(sent, "ctx", 1)

    incoming = lax.fori_loop(0, lax.axis_size("ctx") - 1, relay, empty_state)
    reach = entry * decay_before.T[:, :, None]
    remote_part = (
        jnp.einsum("cis,hsp->cihp", out_float, incoming, precision=HIGH)
        * reach.transpose(1, 2, 0)[:, :, :, None]
    )
    output = (intra + local_part + remote_part).reshape(tok_count, local_heads, head_size)
    gated = output * jax.nn.silu(
        gate_input[0].reshape(tok_count, local_heads, head_size).astype(jnp.float32)
    )
    normed = (
        gated
        * lax.rsqrt(jnp.mean(gated * gated, axis=2, keepdims=True) + 1e-05)
        * norm_gain.reshape(local_heads, head_size)
    )
    mixed = normed.reshape(tok_count, local_heads * head_size).astype(jnp.bfloat16)
    doc_count = lengths.shape[0]
    member = (doc_ids[None, :] == jnp.arange(doc_count, dtype=jnp.int32)[:, None]).astype(
        jnp.bfloat16
    )
    partial_sums = jnp.dot(member, mixed, preferred_element_type=jnp.float32)
    doc_totals = lax.psum(partial_sums, "ctx")
    pooled = doc_totals / lengths[:, None].astype(jnp.float32)
    pooled_all = lax.all_gather(pooled, "dp", axis=0, tiled=True)
    part_dots = jnp.dot(pooled, pooled_all.T, precision=HIGH)
    part_squares = jnp.sum(pooled_all * pooled_all, axis=1)
    dots, squares = lax.psum((part_dots, part_squares), "mp")
    inverse_all = lax.rsqrt(squares / WIDTH + 1e-06)
    first_doc = lax.axis_index("dp") * doc_count
    inverse_mine = lax.dynamic_slice_in_dim(inverse_all, first_doc, doc_count)
    embedding = pooled * inverse_mine[:, None]
    similar = dots * inverse_mine[:, None] * inverse_all[None, :] / (WIDTH * 0.05)
    every_doc = jnp.arange(pooled_all.shape[0], dtype=jnp.int32)
    my_docs = first_doc + jnp.arange(doc_count, dtype=jnp.int32)
    others = every_doc[None, :] != my_docs[:, None]
    total = jnp.sum(jnp.where(others, jnp.exp(similar), 0.0), axis=1)
    picked = jnp.sum(jnp.where(every_doc[None, :] == partner[:, None], similar, 0.0), axis=1)
    doc_loss = jnp.log(total) - picked
    return (mixed[None], embedding, doc_loss)


def solution(mesh):
    in_specs = (
        P(("groups", "dp"), "ctx", "mp"),
        P(("groups", "dp"), "ctx", "mp"),
        P(("groups", "dp"), "ctx", None),
        P(("groups", "dp"), "ctx", None),
        P(("groups", "dp"), "mp", "ctx"),
        P("mp"),
        P("mp"),
        P(("groups", "dp"), None),
        P(("groups", "dp")),
    )
    out_specs = (P(("groups", "dp"), "ctx", "mp"), P(("groups", "dp"), "mp"), P(("groups", "dp")))
    return jax.shard_map(
        on_device, mesh=mesh, in_specs=in_specs, out_specs=out_specs, check_vma=False
    )
```

profile of v0, /device:TPU:0, one launch (start us, length us, event | category | flops | bytes accessed | tf_op | source)
XLA Modules:
  0.0 268.2 jit_solution(13232657588594777341)
XLA Ops:
  7.3 0.9 squeeze.14
  8.2 0.9 squeeze.15
  9.0 0.7 copy.119
  10.2 0.7 compare_convert_fusion
  11.2 0.6 compare_select_fusion.2
  11.8 0.7 neg.27
  12.6 2.3 reduce-window.19
  15.3 0.5 copy-done.7
  15.7 5.6 %copy.151 = bf16[128,8,16,128]{3,2,1,0:T(8,128)(2,1)} copy(bf16[128,8,16,128]{3,1,2,0:T(8,128)(2,1)} %bitcast.132) | data formatting | bytes 8388608
  21.3 7.5 %copy.131 = bf16[4,256,16,128]{1,3,2,0:T(8,128)(2,1)} copy(bf16[4,256,16,128]{3,2,1,0:T(8,128)(2,1)} %bitcast.131) | data formatting | bytes 8388608 | tf_op jit(solution)/shard_map/reshape;squeeze | solution.py:69
  28.8 0.7 multiply_bitcast_fusion.2
  29.5 0.7 compare_select_fusion
  30.2 5.4 %fusion.32 = f32[4,16,128,128]{2,3,1,0:T(8,128)} fusion(bf16[4,256,128,1]{2,1,3,0:T(8,128)(2,1)S(1)} %bitcast.134, bf16[4,256,16,128]{1,3,2,0:T(8,128)(2,1)} %copy.131, f32[4,256,16]{1,2,0:T(8,128)S(1)} %get-tuple-element.170), kind=kOutput, calls=%fused_computation.46 | convolution fusion | flops 543162368 | bytes 8716288 | tf_op jit(solution)/shard_map/cjs,cjhp->chsp/dot_general | solution.py:77
  35.5 21.5 %while.28 = (s32[]{:T(128)}, f32[16,128,128]{2,1,0:T(8,128)S(1)}, f32[16]{0:T(128)}, f32[4,16,128,128]{3,2,1,0:T(8,128)}, f32[4,16]{1,0:T(4,128)}, /*index=5*/f3...) while((s32[]{:T(128)}, f32[16,128,128]{2,1,0:T(8,128)S(1)}, f32[16]{0:T(128)}, ...), condition=%wide.region_6.7_spmd.clone, body=%wide.region_5.6_spmd.clone.sunk | while | flops 1048611 | bytes 9438325 | solution.py:87
  35.5 1.2 fusion.57
  36.7 1.0 bitcast_dynamic-update-slice_fusion.2
  37.8 1.3 constant_dynamic-slice_fusion.3
  39.1 0.3 copy.175
  39.6 1.3 dynamic_update_slice.14
  40.9 1.2 fusion.57
  42.1 1.0 bitcast_dynamic-update-slice_fusion.2
  43.2 1.3 constant_dynamic-slice_fusion.3
  44.5 0.3 copy.175
  45.0 1.3 dynamic_update_slice.14
  46.3 1.2 fusion.57
  47.5 1.0 bitcast_dynamic-update-slice_fusion.2
  48.5 1.3 constant_dynamic-slice_fusion.3
  49.8 0.3 copy.175
  50.4 1.3 dynamic_update_slice.14
  51.7 1.2 fusion.57
  52.9 1.0 bitcast_dynamic-update-slice_fusion.2
  53.9 1.3 constant_dynamic-slice_fusion.3
  55.2 0.3 copy.175
  55.8 1.3 dynamic_update_slice.14
  57.3 3.2 %convert_bitcast_fusion.1 = f32[128,8,16,128]{3,1,2,0:T(8,128)S(1)} fusion(bf16[1,1024,2048]{2,1,0:T(8,128)(2,1)} %param.14), kind=kLoop, calls=%fused_computation.11 | loop fusion | flops 2097152 | bytes 12582912
  60.5 5.2 %copy.152 = f32[128,8,16,128]{3,2,1,0:T(8,128)} copy(f32[128,8,16,128]{3,1,2,0:T(8,128)S(1)} %convert_bitcast_fusion.1) | data formatting | bytes 16777216
  65.7 9.9 %copy.138 = f32[4,256,16,128]{1,3,2,0:T(8,128)} copy(f32[4,256,16,128]{3,2,1,0:T(8,128)} %bitcast.130) | data formatting | bytes 16777216 | tf_op jit(solution)/shard_map/convert_element_type | solution.py:110
  75.7 9.0 %fusion.44 = f32[4,16,128,256]{3,2,1,0:T(8,128)} fusion(f32[4,16,128,128]{3,2,1,0:T(8,128)} %get-tuple-element.65, bf16[4,256,128,1]{2,1,3,0:T(8,128)(2,1)S(1)} %bitcast.125), kind=kOutput, calls=%fused_computation.93 | convolution fusion | flops 3221225472 | bytes 12845056 | tf_op jit(solution)/shard_map/cis,chsp->cihp/dot_general | solution.py:93
  84.7 0.7 fusion.35
  85.7 8.8 %fusion.5 = f32[4,16,256,128]{2,3,1,0:T(8,128)} fusion(bf16[4,256,16,128]{1,3,2,0:T(8,128)(2,1)S(1)} %copy-done.4, f32[16,4,256]{2,0,1:T(8,128)S(1)} %copy-done.10, f32[16,4,256]{2,0,1:T(8,128)S(1)} %copy-done.8, f32[4,256,256]{2,1,0:T(8,128)S(1)} %fusion.43, pred[4,256,256]{2,1,0:T(8,128)(4,1)S(1)} %compare_and_fusion), kind=kOutput, calls=%fused_computation.16 | convolution fusion | flops 1098907648 | bytes 14024704 | tf_op jit(solution)/shard_map/hcij,cjhp->cihp/dot_general | solution.py:70
  94.6 80.7 %while.27 = (s32[]{:T(128)}, f32[16,128,128]{2,1,0:T(8,128)S(1)}, f32[16]{0:T(128)}, f32[16,128,128]{2,1,0:T(8,128)S(1)}, s32[]{:T(128)}) while((s32[]{:T(128)}, f32[16,128,128]{2,1,0:T(8,128)S(1)}, f32[16]{0:T(128)}, f32[16,128,128]{2,1,0:T(8,128)S(1)}, s32[]{:T(128)}) %tuple.57), condition=%wide.region_8.9_spmd, body=%wide.region_7.8_spmd.sunk | while | flops 524290 | bytes 7340197 | solution.py:102
  94.6 0.8 multiply_add_fusion.2
  95.4 5.0 %collective-permute-start = (f32[16,128,128]{2,1,0:T(8,128)S(1)}, f32[16,128,128]{2,1,0:T(8,128)S(1)}, u32[]{:S(2)}, u32[]{:S(2)}) collective-permute-start(f32[16,128,128]{2,1,0:T(8,128)S(1)} %multiply_add_fusion.2), channel_id=1, source_target_pairs={{0,4},{4,8},{8,12},{1,5},{5,9},{9,13},{2,6},{6,10},{10,14},{3,7},{... | collective-permute-start | bytes 3145736 | tf_op jit(solution)/shard_map/while/body/eval_jaxpr/ppermute | solution.py:16
  100.4 22.3 %collective-permute-done = f32[16,128,128]{2,1,0:T(8,128)S(1)} collective-permute-done((f32[16,128,128]{2,1,0:T(8,128)S(1)}, f32[16,128,128]{2,1,0:T(8,128)S(1)}, u32[]{:S(2)}, u32[]{:S(2)}) %collective-permute-start) | collective-permute-done | bytes 1048608 | tf_op jit(solution)/shard_map/while/body/eval_jaxpr/ppermute | solution.py:16
  122.8 0.8 multiply_add_fusion.2
  123.6 4.5 %collective-permute-start = (f32[16,128,128]{2,1,0:T(8,128)S(1)}, f32[16,128,128]{2,1,0:T(8,128)S(1)}, u32[]{:S(2)}, u32[]{:S(2)}) collective-permute-start(f32[16,128,128]{2,1,0:T(8,128)S(1)} %multiply_add_fusion.2), channel_id=1, source_target_pairs={{0,4},{4,8},{8,12},{1,5},{5,9},{9,13},{2,6},{6,10},{10,14},{3,7},{... | collective-permute-start | bytes 3145736 | tf_op jit(solution)/shard_map/while/body/eval_jaxpr/ppermute | solution.py:16
  128.0 21.5 %collective-permute-done = f32[16,128,128]{2,1,0:T(8,128)S(1)} collective-permute-done((f32[16,128,128]{2,1,0:T(8,128)S(1)}, f32[16,128,128]{2,1,0:T(8,128)S(1)}, u32[]{:S(2)}, u32[]{:S(2)}) %collective-permute-start) | collective-permute-done | bytes 1048608 | tf_op jit(solution)/shard_map/while/body/eval_jaxpr/ppermute | solution.py:16
  149.5 0.8 multiply_add_fusion.2
  150.3 4.5 %collective-permute-start = (f32[16,128,128]{2,1,0:T(8,128)S(1)}, f32[16,128,128]{2,1,0:T(8,128)S(1)}, u32[]{:S(2)}, u32[]{:S(2)}) collective-permute-start(f32[16,128,128]{2,1,0:T(8,128)S(1)} %multiply_add_fusion.2), channel_id=1, source_target_pairs={{0,4},{4,8},{8,12},{1,5},{5,9},{9,13},{2,6},{6,10},{10,14},{3,7},{... | collective-permute-start | bytes 3145736 | tf_op jit(solution)/shard_map/while/body/eval_jaxpr/ppermute | solution.py:16
  154.8 20.6 %collective-permute-done = f32[16,128,128]{2,1,0:T(8,128)S(1)} collective-permute-done((f32[16,128,128]{2,1,0:T(8,128)S(1)}, f32[16,128,128]{2,1,0:T(8,128)S(1)}, u32[]{:S(2)}, u32[]{:S(2)}) %collective-permute-start) | collective-permute-done | bytes 1048608 | tf_op jit(solution)/shard_map/while/body/eval_jaxpr/ppermute | solution.py:16
  175.3 13.7 %multiply_reduce_fusion = (f32[4,256,16]{1,2,0:T(8,128)S(1)}, f32[4,256,16,128]{1,3,2,0:T(8,128)}) fusion(f32[4,256,16,128]{1,3,2,0:T(8,128)} %copy.138, f32[4,256,16]{1,2,0:T(8,128)S(1)} %copy-done.9, bf16[4,256,128,1]{2,1,3,0:T(8,128)(2,1)S(1)} %bitcast.126, f32[16,128,128]{2,1,0:T(8,128)S(1)} %get-tuple-element.68, ...), kind=kOutput, calls=%fused_computation.33 | convolution fusion | flops 3244277760 | bytes 35061760 | tf_op jit(solution)/shard_map/cis,hsp->cihp/dot_general | solution.py:105
  189.3 10.3 %copy.136 = f32[4,256,16,128]{3,2,1,0:T(8,128)} copy(f32[4,256,16,128]{1,3,2,0:T(8,128)} %get-tuple-element.172) | data formatting | bytes 16777216 | tf_op jit(solution)/shard_map/add | solution.py:108
  199.5 2.3 mul.236
  201.9 3.2 %copy-done.3 = f32[1024,16,128]{2,1,0:T(8,128)} copy-done((f32[1024,16,128]{2,1,0:T(8,128)}, f32[1024,16,128]{2,1,0:T(8,128)S(1)}, u32[]{:S(2)}) %copy-start.3) | copy-done | bytes 8388632
  205.1 7.4 %fusion.30 = f32[16,2048]{1,0:T(8,128)} fusion(f32[128,8,16,128]{3,2,1,0:T(8,128)S(1)} %bitcast.129, bf16[1,1024,2048]{2,1,0:T(8,128)(2,1)} %param.14, f32[128,8,16,128]{3,2,1,0:T(8,128)S(1)} %bitcast.128, f32[2048]{0:T(1024)S(1)} %copy-done.12, s32[1024]{0:T(1024)S(1)} %copy-done.13), kind=kOutput, calls=%fused_computation.45 | convolution fusion | flops 85999616 | bytes 21114880 | tf_op jit(solution)/shard_map/dot_general | solution.py:122
  212.5 9.3 %mul.237 = f32[1,1024,2048]{2,1,0:T(8,128)} reshape(f32[1024,16,128]{2,1,0:T(8,128)} %copy-done.3) | data formatting | bytes 16777216 | tf_op jit(solution)/shard_map/mul | solution.py:113
  221.8 9.3 %reshape.296 = f32[1,1024,2048]{2,1,0:T(8,128)} reshape(f32[4,256,16,128]{3,2,1,0:T(8,128)} %copy.136) | data formatting | bytes 16777216 | tf_op jit(solution)/shard_map/reshape | solution.py:108
  231.1 10.8 %fusion.25 = bf16[1,1024,2048]{2,1,0:T(8,128)(2,1)} fusion(f32[1,1024,2048]{2,1,0:T(8,128)} %mul.237, f32[1,1024,2048]{2,1,0:T(8,128)} %reshape.296, bf16[1,1024,2048]{2,1,0:T(8,128)(2,1)} %param.14, f32[2048]{0:T(1024)S(1)} %copy-done.12), kind=kLoop, calls=%fused_computation.40 | loop fusion | flops 18874368 | bytes 25174016 | tf_op jit(solution)/shard_map/convert_element_type | solution.py:117
  241.9 7.4 %all-reduce.3.cloned.1.call-done = f32[16,2048]{1,0:T(8,128)} async-done(((f32[16,2048]{1,0:T(8,128)}), f32[16,2048]{1,0:T(8,128)}) %all-reduce.3.cloned.1.call-update) | async-done | bytes 131088 | tf_op jit(solution)/shard_map/psum | solution.py:123
  249.3 1.0 broadcast_divide_fusion
  250.3 5.6 %all_gather.3 = f32[32,2048]{1,0:T(8,128)S(1)} all-gather(f32[16,2048]{1,0:T(8,128)S(1)} %broadcast_divide_fusion), channel_id=1, replica_groups=mesh['groups'=2,'ctx'=4,'dp'=2,'mp'=2] {'dp'}, dimensions={0}, use_global_device_ids=true | all-gather | bytes 393216 | tf_op jit(solution)/shard_map/all_gather | solution.py:125
  256.4 2.5 all-reduce
  259.2 0.5 log_subtract_fusion
  259.7 1.6 broadcast_multiply_fusion
  (72 shorter events, 3.7 us)
Async XLA Ops:
  7.2 68.5 %copy-start = (bf16[1,1024,128]{2,1,0:T(8,128)(2,1)S(1)}, bf16[1,1024,128]{2,1,0:T(8,128)(2,1)}, u32[]{:S(2)}) copy-start(bf16[1,1024,128]{2,1,0:T(8,128)(2,1)} %param.16) | copy-start | bytes 786436
  7.2 242.1 %all-reduce.3.cloned.1.call-start = ((), (), s32[]{:S(2)}) async-start(), calls=%async_computation | async-start | bytes 262144 | tf_op jit(solution)/shard_map/psum | solution.py:123
  15.1 0.6 copy-start.7
  15.7 14.4 %copy-start.5 = (bf16[1,1024,128]{2,1,0:T(8,128)(2,1)S(1)}, bf16[1,1024,128]{2,1,0:T(8,128)(2,1)}, u32[]{:S(2)}) copy-start(bf16[1,1024,128]{2,1,0:T(8,128)(2,1)} %param.15) | copy-start | bytes 786436
  75.6 9.1 %copy-start.11 = (f32[4,256]{1,0:T(4,128)S(1)}, f32[4,256]{1,0:T(4,128)}, u32[]{:S(2)}) copy-start(f32[4,256]{1,0:T(4,128)} %get-tuple-element.164) | copy-start | bytes 12292
  75.6 9.1 %copy-start.14 = (f32[4,16]{1,0:T(4,128)S(1)}, f32[4,16]{1,0:T(4,128)}, u32[]{:S(2)}) copy-start(f32[4,16]{1,0:T(4,128)} %get-tuple-element.69) | copy-start | bytes 772
  75.6 9.8 %copy-start.6 = (bf16[1,1024,128]{2,1,0:T(8,128)(2,1)S(1)}, bf16[1,1024,128]{2,1,0:T(8,128)(2,1)}, u32[]{:S(2)}) copy-start(bf16[1,1024,128]{2,1,0:T(8,128)(2,1)} %param.15) | copy-start | bytes 786436
  75.6 10.1 %copy-start.4 = (bf16[4,256,16,128]{1,3,2,0:T(8,128)(2,1)S(1)}, bf16[4,256,16,128]{1,3,2,0:T(8,128)(2,1)}, u32[]{:S(2)}) copy-start(bf16[4,256,16,128]{1,3,2,0:T(8,128)(2,1)} %copy.131) | copy-start | bytes 12582916
  75.6 10.1 %copy-start.8 = (f32[16,4,256]{2,0,1:T(8,128)S(1)}, f32[16,4,256]{2,0,1:T(8,128)}, u32[]{:S(2)}) copy-start(f32[16,4,256]{2,0,1:T(8,128)} %copy-done.7) | copy-start | bytes 196612
  75.6 10.1 %copy-start.10 = (f32[16,4,256]{2,0,1:T(8,128)S(1)}, f32[16,4,256]{2,0,1:T(8,128)}, u32[]{:S(2)}) copy-start(f32[16,4,256]{2,0,1:T(8,128)} %get-tuple-element.169) | copy-start | bytes 196612
  94.5 80.8 %copy-start.9 = (f32[4,256,16]{1,2,0:T(8,128)S(1)}, f32[4,256,16]{1,2,0:T(8,128)}, u32[]{:S(2)}) copy-start(f32[4,256,16]{1,2,0:T(8,128)} %get-tuple-element.168) | copy-start | bytes 196612
  95.4 27.4 %collective-permute-start = (f32[16,128,128]{2,1,0:T(8,128)S(1)}, f32[16,128,128]{2,1,0:T(8,128)S(1)}, u32[]{:S(2)}, u32[]{:S(2)}) collective-permute-start(f32[16,128,128]{2,1,0:T(8,128)S(1)} %multiply_add_fusion.2), channel_id=1, source_target_pairs={{0,4},{4,8},{8,12},{1,5},{5,9},{9,13},{2,6},{6,10},{10,14},{3,7},{... | collective-permute-start | bytes 3145736 | tf_op jit(solution)/shard_map/while/body/eval_jaxpr/ppermute | solution.py:16
  123.6 25.9 %collective-permute-start = (f32[16,128,128]{2,1,0:T(8,128)S(1)}, f32[16,128,128]{2,1,0:T(8,128)S(1)}, u32[]{:S(2)}, u32[]{:S(2)}) collective-permute-start(f32[16,128,128]{2,1,0:T(8,128)S(1)} %multiply_add_fusion.2), channel_id=1, source_target_pairs={{0,4},{4,8},{8,12},{1,5},{5,9},{9,13},{2,6},{6,10},{10,14},{3,7},{... | collective-permute-start | bytes 3145736 | tf_op jit(solution)/shard_map/while/body/eval_jaxpr/ppermute | solution.py:16
  150.3 25.0 %collective-permute-start = (f32[16,128,128]{2,1,0:T(8,128)S(1)}, f32[16,128,128]{2,1,0:T(8,128)S(1)}, u32[]{:S(2)}, u32[]{:S(2)}) collective-permute-start(f32[16,128,128]{2,1,0:T(8,128)S(1)} %multiply_add_fusion.2), channel_id=1, source_target_pairs={{0,4},{4,8},{8,12},{1,5},{5,9},{9,13},{2,6},{6,10},{10,14},{3,7},{... | collective-permute-start | bytes 3145736 | tf_op jit(solution)/shard_map/while/body/eval_jaxpr/ppermute | solution.py:16
  199.5 5.5 %copy-start.2 = (f32[4,256,16,128]{3,2,1,0:T(8,128)S(1)}, f32[4,256,16,128]{3,2,1,0:T(8,128)}, u32[]{:S(2)}) copy-start(f32[4,256,16,128]{3,2,1,0:T(8,128)} %copy.136) | copy-start | bytes 25165828
  199.5 5.5 %copy-start.12 = (f32[2048]{0:T(1024)S(1)}, f32[2048]{0:T(1024)}, u32[]{:S(2)}) copy-start(f32[2048]{0:T(1024)} %param.19) | copy-start | bytes 24580
  199.5 5.5 %copy-start.13 = (s32[1024]{0:T(1024)S(1)}, s32[1024]{0:T(1024)}, u32[]{:S(2)}) copy-start(s32[1024]{0:T(1024)} %compare_select_fusion.2) | copy-start | bytes 12292
  201.9 3.2 %copy-start.3 = (f32[1024,16,128]{2,1,0:T(8,128)}, f32[1024,16,128]{2,1,0:T(8,128)S(1)}, u32[]{:S(2)}) copy-start(f32[1024,16,128]{2,1,0:T(8,128)S(1)} %mul.236) | copy-start | bytes 25165828
  221.8 39.6 %copy-start.1 = (bf16[1,1024,128]{2,1,0:T(8,128)(2,1)S(1)}, bf16[1,1024,128]{2,1,0:T(8,128)(2,1)}, u32[]{:S(2)}) copy-start(bf16[1,1024,128]{2,1,0:T(8,128)(2,1)} %param.16) | copy-start | bytes 786436
  231.1 10.8 %copy-start.15 = (s32[1,16]{1,0:T(1,128)S(1)}, s32[1,16]{1,0:T(1,128)}, u32[]{:S(2)}) copy-start(s32[1,16]{1,0:T(1,128)} %param.20) | copy-start | bytes 196
  231.1 27.9 %copy-start.16 = (s32[16]{0:T(128)S(1)}, s32[16]{0:T(128)}, u32[]{:S(2)}) copy-start(s32[16]{0:T(128)} %param.21) | copy-start | bytes 196
Sparse Core Ops, SparseCore 0:
  212.6 36.6 all-reduce.2
where the time goes:
time: 270 us; the launch traced here: 268 us
  local copies, waits for them, and re-layouts  78.1 us (29%)
  waiting for transfers between devices  71.8 us (27%)
  matrix products  44.8 us (17%)
  other arithmetic  36.9 us (14%)
  between operations  14.3 us (5%)
  starting transfers between devices  13.9 us (5%)
  blocking collectives  8.16 us (3%)
    ppermute x3, waiting for transfers between devices, shifted(): return lax.ppermute(x, axis, pairs)  64.4 us
    unnamed x36, local copies, waits for them, and re-layouts  14.5 us
    ppermute x3, starting transfers between devices, shifted(): return lax.ppermute(x, axis, pairs)  13.9 us
    dot_general x1, matrix products, on_device(): jnp.einsum('cis,hsp->cihp', out_float, incoming, precision=HIGH)  13.7 us
    mul x2, local copies, waits for them, and re-layouts, on_device(): gated * lax.rsqrt(jnp.mean(gated * gated, axis=2, keepdims=True) + 1e-05)  11.6 us
    convert_element_type x1, other arithmetic, on_device(): normed.reshape(tok_count, local_heads * head_size).astype(jnp.bfloat16)  10.8 us
    add x1, local copies, waits for them, and re-layouts, on_device(): intra + local_part + remote_part  10.3 us
    convert_element_type x1, local copies, waits for them, and re-layouts, on_device(): gate_input[0].reshape(tok_count, local_heads, head_size).astype(jnp.float32)  9.9 us
  transfers between devices with their start and end apart: 4, of which 4 were waited for; matrix products, arithmetic and copies ran while one was open for 11% of the time, Pallas kernels for 0%

commit v1 on v0

v1 whole, which is shorter than its diff:
```python
import functools

import jax
import jax.numpy as jnp
from jax import lax
from jax.experimental import pallas as pl
from jax.experimental.pallas import tpu as pltpu
from jax.sharding import PartitionSpec as P

SPAN = 256
WIDTH = 4096
HIGH = lax.Precision.HIGHEST

CHUNKS = 8
DELAY = 2
GROUPS = 4


def dot(a, b, dims=((1,), (0,))):
    return lax.dot_general(a, b, (dims, ((), ())), preferred_element_type=jnp.float32)


def split3(v):
    hi = v.astype(jnp.bfloat16)
    rest = v - hi.astype(jnp.float32)
    mid = rest.astype(jnp.bfloat16)
    low = (rest - mid.astype(jnp.float32)).astype(jnp.bfloat16)
    return hi, mid, low


def first_end_from(ends_ref, docs, place):
    found = jnp.int32(1 << 30)
    for k in range(docs - 1, -1, -1):
        found = jnp.where(ends_ref[k] >= place, ends_ref[k], found)
    return found


def last_end_until(ends_ref, docs, place):
    found = jnp.int32(0)
    for k in range(docs):
        found = jnp.where(ends_ref[k] <= place, ends_ref[k], found)
    return found


def state_kernel(
    docs,
    ends_ref,
    off_ref,
    x_ref,
    b_ref,
    raw_ref,
    rate_ref,
    state_ref,
    e_ref,
    f_ref,
    decay_ref,
    dend_ref,
    docid_ref,
    bt_ref,
    g_ref,
):
    tokens, heads = e_ref.shape
    blocks = tokens // SPAN
    step = pl.program_id(0)
    per = state_ref.shape[0]

    @pl.when(step == 0)
    def _():
        off = off_ref[0]
        raw = raw_ref[...]
        steps = jnp.maximum(raw, 0.0) + jnp.log1p(jnp.exp(-jnp.abs(raw)))
        steps_t = steps.T
        logdecay = -rate_ref[...] * steps_t
        row = lax.broadcasted_iota(jnp.int32, (SPAN, SPAN), 0)
        col = lax.broadcasted_iota(jnp.int32, (SPAN, SPAN), 1)
        lower = jnp.where(row >= col, 1.0, 0.0).astype(jnp.bfloat16)
        cums = []
        for b in range(blocks):
            parts = split3(logdecay[b * SPAN : (b + 1) * SPAN])
            cums.append(dot(lower, parts[0]) + (dot(lower, parts[1]) + dot(lower, parts[2])))
        later = jnp.zeros((1, heads), jnp.float32)
        for b in range(blocks - 1, -1, -1):
            later = later + cums[b][SPAN - 1 :]
            rows = pl.ds(b * SPAN, SPAN)
            f = steps_t[b * SPAN : (b + 1) * SPAN] * jnp.exp(-cums[b])
            e_ref[rows, :] = jnp.exp(cums[b])
            f_ref[rows, :] = f
            g_ref[rows, :] = f * jnp.exp(later)
        start = last_end_until(ends_ref, docs, off + tokens - 1)
        through = jnp.where(start < off, 1.0, 0.0)
        decay_ref[...] = jnp.exp(later) * through
        place = lax.broadcasted_iota(jnp.int32, (tokens, 128), 0) + off
        masked = jnp.where(place >= start, b_ref[...].astype(jnp.float32), 0.0)
        bt_ref[...] = masked.T.astype(jnp.bfloat16)
        places = lax.broadcasted_iota(jnp.int32, (1, tokens), 1) + off
        dend = jnp.full((1, tokens), 1 << 30, jnp.int32)
        docid = jnp.zeros((1, tokens), jnp.int32)
        for k in range(docs - 1, -1, -1):
            dend = jnp.where(ends_ref[k] > places, ends_ref[k], dend)
            docid = docid + (places >= ends_ref[k]).astype(jnp.int32)
        dend_ref[...] = dend
        docid_ref[...] = docid

    g = g_ref[...]
    lane = lax.broadcasted_iota(jnp.int32, (1, heads), 1)
    scaled = []
    for h in range(per):
        column = jnp.sum(jnp.where(lane == step * per + h, g, 0.0), axis=1, keepdims=True)
        scaled.append((x_ref[:, h * 128 : (h + 1) * 128].astype(jnp.float32) * column).astype(jnp.bfloat16))
    total = dot(bt_ref[...], jnp.concatenate(scaled, axis=1))
    for h in range(per):
        state_ref[h] = total[:, h * 128 : (h + 1) * 128]


def finish_kernel(
    docs,
    group,
    ends_ref,
    off_ref,
    x_ref,
    z_ref,
    b_ref,
    c_ref,
    e_ref,
    f_ref,
    dend_ref,
    docid_ref,
    gain_ref,
    *rest,
):
    in_refs = rest[: CHUNKS // GROUPS]
    mixed_ref, sums_ref, right_ref, state_ref = rest[-4:]
    block = pl.program_id(0)
    per = x_ref.shape[1] // 128
    start = off_ref[0] + block * SPAN
    prior_end = jnp.where(start > 0, first_end_from(ends_ref, docs, start), 0)
    last_start = last_end_until(ends_ref, docs, start + SPAN - 1)
    each = per // len(in_refs)

    @pl.when(block == 0)
    def _():
        for h in range(per):
            state_ref[:, h * 128 : (h + 1) * 128] = in_refs[h // each][h % each]
        sums_ref[...] = jnp.zeros_like(sums_ref)

    row = lax.broadcasted_iota(jnp.int32, (SPAN, SPAN), 0)
    col = lax.broadcasted_iota(jnp.int32, (SPAN, SPAN), 1)
    same = (row >= col) & (row + start < dend_ref[...])
    scores = jnp.where(same, dot(c_ref[...], b_ref[...], ((1,), (1,))), 0.0).astype(jnp.bfloat16)
    place = lax.broadcasted_iota(jnp.int32, (SPAN, 128), 0) + start
    reach = jnp.where(place < prior_end, c_ref[...].astype(jnp.float32), 0.0).astype(jnp.bfloat16)
    tail = jnp.where(place >= last_start, b_ref[...].astype(jnp.float32), 0.0).astype(jnp.bfloat16)
    state = state_ref[...]
    high = state.astype(jnp.bfloat16)
    right_ref[SPAN : SPAN + 128] = high
    right_ref[SPAN + 128 :] = (state - high.astype(jnp.float32)).astype(jnp.bfloat16)
    for h in range(per):
        cols = slice(h * 128, (h + 1) * 128)
        head = group * per + h
        right_ref[0:SPAN, cols] = (
            x_ref[:, cols].astype(jnp.float32) * f_ref[:, head : head + 1]
        ).astype(jnp.bfloat16)
    left = jnp.concatenate([scores, reach, reach], axis=1)
    inner = dot(left, right_ref[...])
    added = dot(tail, right_ref[0:SPAN], ((0,), (0,)))
    keep = jnp.where(last_start < start, 1.0, 0.0)
    ones = jnp.full((128, 128), 1.0, jnp.bfloat16)
    for h in range(per):
        cols = slice(h * 128, (h + 1) * 128)
        head = group * per + h
        z = z_ref[:, cols].astype(jnp.float32)
        half = 0.5 * z
        e = e_ref[:, head : head + 1]
        gated = (inner[:, cols] * e) * (half + half * jnp.tanh(half))
        squares = dot((gated * gated).astype(jnp.bfloat16), ones)
        normed = gated * lax.rsqrt(squares * (1.0 / 128) + 1e-05) * gain_ref[:, cols]
        mixed_ref[:, cols] = normed.astype(jnp.bfloat16)
        state_ref[:, cols] = e[SPAN - 1 :] * (keep * state[:, cols] + added[:, cols])
    member = (
        docid_ref[...] == lax.broadcasted_iota(jnp.int32, (docs, SPAN), 0)
    ).astype(jnp.float32).astype(jnp.bfloat16)
    sums_ref[...] += dot(member, mixed_ref[...])


def on_device(
    mixer_input,
    gate_input,
    input_proj,
    output_proj,
    step_raw,
    decay_rate,
    norm_gain,
    doc_lengths,
    partner,
):
    tokens = mixer_input.shape[1]
    width = mixer_input.shape[2]
    heads = decay_rate.shape[0]
    docs = doc_lengths.shape[1]
    blocks = tokens // SPAN
    count = lax.axis_size("ctx")
    here = lax.axis_index("ctx")
    x, z = mixer_input[0], gate_input[0]
    lengths = doc_lengths[0]
    ends = jnp.cumsum(lengths).astype(jnp.int32)
    off = (here * tokens).astype(jnp.int32).reshape(1)
    per = heads // CHUNKS
    smem = pl.BlockSpec(memory_space=pltpu.SMEM)
    whole = lambda shape: pl.BlockSpec(shape, lambda i: (0,) * len(shape))
    f32 = jnp.float32
    state, e, f, decay, dend, docid = pl.pallas_call(
        functools.partial(state_kernel, docs),
        grid=(CHUNKS,),
        in_specs=[
            smem,
            smem,
            pl.BlockSpec((tokens, per * 128), lambda i: (0, i)),
            whole((tokens, 128)),
            whole((heads, tokens)),
            whole((1, heads)),
        ],
        out_specs=[
            pl.BlockSpec((per, 128, 128), lambda i: (i, 0, 0)),
            whole((tokens, heads)),
            whole((tokens, heads)),
            whole((1, heads)),
            whole((1, tokens)),
            whole((1, tokens)),
        ],
        out_shape=[
            jax.ShapeDtypeStruct((heads, 128, 128), f32),
            jax.ShapeDtypeStruct((tokens, heads), f32),
            jax.ShapeDtypeStruct((tokens, heads), f32),
            jax.ShapeDtypeStruct((1, heads), f32),
            jax.ShapeDtypeStruct((1, tokens), jnp.int32),
            jax.ShapeDtypeStruct((1, tokens), jnp.int32),
        ],
        scratch_shapes=[pltpu.VMEM((128, tokens), jnp.bfloat16), pltpu.VMEM((tokens, heads), f32)],
        compiler_params=pltpu.CompilerParams(vmem_limit_bytes=32 << 20),
        cost_estimate=pl.CostEstimate(flops=2 * tokens * 128 * width, bytes_accessed=6 << 20, transcendentals=0),
        name="states",
    )(ends, off, x, input_proj[0], step_raw[0], decay_rate.reshape(1, heads))

    pairs = [(i, (i + 1) % count) for i in range(count)]
    got = []
    for r in range(CHUNKS + DELAY * (count - 2)):
        at = jnp.clip(r - DELAY * here, 0, CHUNKS - 1) * per
        sent = lax.dynamic_slice_in_dim(state, at, per, 0)
        if r >= DELAY:
            rate = lax.dynamic_slice_in_dim(decay[0], at, per, 0)
            sent = sent + rate[:, None, None] * jnp.where(here == 0, 0.0, got[r - DELAY])
        got.append(lax.ppermute(sent, "ctx", pairs))

    def arrived(c):
        value = jnp.zeros((per, 128, 128), f32)
        for k in range(1, count):
            value = jnp.where(here == k, got[c + DELAY * (k - 1)], value)
        return value

    cols = width // GROUPS
    each = CHUNKS // GROUPS
    mixed = None
    sums = []
    for q in range(GROUPS):
        incoming = [arrived(q * each + i) for i in range(each)]
        operands = [ends, off, x, z, input_proj[0], output_proj[0], e, f, dend, docid, norm_gain.reshape(1, width)]
        specs = [
            smem,
            smem,
            pl.BlockSpec((SPAN, cols), lambda i, q=q: (i, q)),
            pl.BlockSpec((SPAN, cols), lambda i, q=q: (i, q)),
            pl.BlockSpec((SPAN, 128), lambda i: (i, 0)),
            pl.BlockSpec((SPAN, 128), lambda i: (i, 0)),
            pl.BlockSpec((SPAN, heads), lambda i: (i, 0)),
            pl.BlockSpec((SPAN, heads), lambda i: (i, 0)),
            pl.BlockSpec((1, SPAN), lambda i: (0, i)),
            pl.BlockSpec((1, SPAN), lambda i: (0, i)),
            pl.BlockSpec((1, cols), lambda i, q=q: (0, q)),
        ] + [whole((per, 128, 128))] * each
        operands += incoming
        aliases = {}
        if mixed is not None:
            aliases = {len(operands): 0}
            operands.append(mixed)
            specs.append(pl.BlockSpec(memory_space=pl.ANY))
        mixed, part = pl.pallas_call(
            functools.partial(finish_kernel, docs, q),
            grid=(blocks,),
            in_specs=specs,
            out_specs=[
                pl.BlockSpec((SPAN, cols), lambda i, q=q: (i, q)),
                whole((docs, cols)),
            ],
            out_shape=[
                jax.ShapeDtypeStruct((tokens, width), jnp.bfloat16),
                jax.ShapeDtypeStruct((docs, cols), f32),
            ],
            scratch_shapes=[pltpu.VMEM((SPAN + 256, cols), jnp.bfloat16), pltpu.VMEM((128, cols), f32)],
            input_output_aliases=aliases,
            compiler_params=pltpu.CompilerParams(vmem_limit_bytes=32 << 20),
            cost_estimate=pl.CostEstimate(
                flops=2 * tokens * cols * 1024, bytes_accessed=3 * tokens * cols * 2, transcendentals=2 * tokens * cols
            ),
            name=f"finish{q}",
        )(*operands)
        sums.append(part)

    totals = jnp.concatenate(sums, axis=1)
    reach = 1
    while reach < count:
        totals = totals + lax.ppermute(totals, "ctx", [(i, i ^ reach) for i in range(count)])
        reach *= 2
    pooled = totals / lengths[:, None].astype(f32)
    pooled_all = lax.all_gather(pooled, "dp", axis=0, tiled=True)
    part_dots = jnp.dot(pooled, pooled_all.T, precision=HIGH)
    part_squares = jnp.sum(pooled_all * pooled_all, axis=1)
    dots, squares = lax.psum((part_dots, part_squares), "mp")
    inverse_all = lax.rsqrt(squares / WIDTH + 1e-06)
    first_doc = lax.axis_index("dp") * docs
    inverse_mine = lax.dynamic_slice_in_dim(inverse_all, first_doc, docs)
    embedding = pooled * inverse_mine[:, None]
    similar = dots * inverse_mine[:, None] * inverse_all[None, :] / (WIDTH * 0.05)
    every_doc = jnp.arange(pooled_all.shape[0], dtype=jnp.int32)
    my_docs = first_doc + jnp.arange(docs, dtype=jnp.int32)
    others = every_doc[None, :] != my_docs[:, None]
    total = jnp.sum(jnp.where(others, jnp.exp(similar), 0.0), axis=1)
    picked = jnp.sum(jnp.where(every_doc[None, :] == partner[:, None], similar, 0.0), axis=1)
    doc_loss = jnp.log(total) - picked
    return (mixed[None], embedding, doc_loss)


def solution(mesh):
    in_specs = (
        P(("groups", "dp"), "ctx", "mp"),
        P(("groups", "dp"), "ctx", "mp"),
        P(("groups", "dp"), "ctx", None),
        P(("groups", "dp"), "ctx", None),
        P(("groups", "dp"), "mp", "ctx"),
        P("mp"),
        P("mp"),
        P(("groups", "dp"), None),
        P(("groups", "dp")),
    )
    out_specs = (P(("groups", "dp"), "ctx", "mp"), P(("groups", "dp"), "mp"), P(("groups", "dp")))
    return jax.shard_map(
        on_device, mesh=mesh, in_specs=in_specs, out_specs=out_specs, check_vma=False
    )
```

time: 270 us -> 145 us (0.54)
  local copies, waits for them, and re-layouts: 78.1 us -> 11.9 us
  matrix products: 44.8 us -> 0.28 us
  other arithmetic: 36.9 us -> 5.18 us
  Pallas kernels: 0 us -> 26.7 us
  waiting for transfers between devices: 71.8 us -> 87.7 us
  between operations: 14.3 us -> 0.91 us
  starting transfers between devices: 13.9 us -> 3.62 us
    dot_general x6 -> x0, matrix products: 44.5 us -> none  [the longest x1 13.7 us: on_device(): jnp.einsum('cis,hsp->cihp', out_float, incoming, precision=HIGH)]
    pallas_call x0 -> x5, Pallas kernels: none -> 26.7 us  [the longest x4 20.4 us: on_device(): pl.pallas_call(functools.partial(finish_kernel, docs, q), grid=(blocks,),...]
    ppermute x3 -> x14, waiting for transfers between devices: 64.4 us -> 87.7 us  [the longest x12 76.1 us: on_device(): got.append(lax.ppermute(sent, 'ctx', pairs))]
    convert_element_type x5 -> x1, other arithmetic: 11.5 us -> 0.01 us  [on_device(): pooled = totals / lengths[:, None].astype(f32)]
    mul x2 -> x1, local copies, waits for them, and re-layouts: 11.6 us -> 0.09 us  [on_device(): rate[:, None, None] * jnp.where(here == 0, 0.0, got[r - DELAY])]
    ppermute x3 -> x14, starting transfers between devices: 13.9 us -> 3.62 us  [the longest x12 3.55 us: on_device(): got.append(lax.ppermute(sent, 'ctx', pairs))]
    add x1 -> x0, local copies, waits for them, and re-layouts: 10.3 us -> none  [on_device(): intra + local_part + remote_part]
    convert_element_type x1 -> x0, local copies, waits for them, and re-layouts: 9.9 us -> none  [on_device(): gate_input[0].reshape(tok_count, local_heads, head_size).astype(jnp.float32)]
  transfers between devices with their start and end apart: 4 -> 14, of which waited for: 4 -> 14; matrix products, arithmetic and copies ran while one was open for 11% -> 0% of each run, Pallas kernels for 0% -> 0%
where the time goes in v1:
time: 145 us; the launch traced here: 144 us
  waiting for transfers between devices  87.7 us (60%)
  Pallas kernels  26.7 us (18%)
  local copies, waits for them, and re-layouts  11.9 us (8%)
  blocking collectives  8.19 us (6%)
  other arithmetic  5.18 us (4%)
  starting transfers between devices  3.62 us (2%)
    ppermute x12, waiting for transfers between devices, on_device(): got.append(lax.ppermute(sent, 'ctx', pairs))  76.1 us
    pallas_call x4, Pallas kernels, on_device(): pl.pallas_call(functools.partial(finish_kernel, docs, q), grid=(blocks,),...  20.4 us
    ppermute x2, waiting for transfers between devices, on_device(): lax.ppermute(totals, 'ctx', [(i, i ^ reach) for i in range(count)])  11.6 us
    unnamed x31, local copies, waits for them, and re-layouts  11 us
    pallas_call x1, Pallas kernels, on_device(): pl.pallas_call(functools.partial(state_kernel, docs), grid=(CHUNKS,), in_...  6.24 us
    all_gather x1, blocking collectives, on_device(): pooled_all = lax.all_gather(pooled, 'dp', axis=0, tiled=True)  5.64 us
    ppermute x12, starting transfers between devices, on_device(): got.append(lax.ppermute(sent, 'ctx', pairs))  3.55 us
  transfers between devices with their start and end apart: 14, of which 14 were waited for; matrix products, arithmetic and copies ran while one was open for 0% of the time, Pallas kernels for 0%

profile of v1, /device:TPU:0, one launch (start us, length us, event | category | flops | bytes accessed | tf_op | source)
XLA Modules:
  0.0 144.4 jit_solution(1331518456288825109)
XLA Ops:
  0.6 0.7 copy.16
  1.4 0.1 reduce.ends_ref
  1.5 2.2 %copy-done = bf16[1,1024,2048]{2,1,0:T(8,128)(2,1)S(1)} copy-done((bf16[1,1024,2048]{2,1,0:T(8,128)(2,1)S(1)}, bf16[1,1024,2048]{2,1,0:T(8,128)(2,1)}, u32[]{:S(2)}) %copy-start) | copy-done | bytes 4194328
  3.7 0.9 copy-done.3
  4.7 0.8 copy-done.7
  5.5 0.7 copy-done.8
  6.2 6.2 %states.1 = (f32[16,128,128]{2,1,0:T(8,128)S(1)}, f32[1024,16]{1,0:T(8,128)S(1)}, f32[1024,16]{1,0:T(8,128)S(1)}, f32[1,16]{1,0:T(1,128)S(1)}, s32[1,1024]{1,0:T(1,128)S(1)}, /*index=5*/s32[1,1024]{1,0:T(1,128)S(1)}) custom-call(s32[16]{0:T(128)S(1)} %reduce.ends_ref, s32[1]{0:T(128)} %bitcast.1.off_ref, bf16[1024,2048]{1,0:T(8,128)(2,1)S(1)} %bitcast.34, ...), custom_call_target="tpu_custom_call" | custom-call | flops 536870912 | bytes 6291456 | tf_op jit(solution)/shard_map/states/pallas_call | solution.py:211
  12.4 0.0 copy-start.4
  12.4 0.0 copy-start.5
  12.5 3.1 %collective-permute-start.6 = (f32[2,128,128]{2,1,0:T(8,128)S(1)}, f32[2,128,128]{2,1,0:T(8,128)S(1)}, u32[]{:S(2)}, u32[]{:S(2)}) collective-permute-start(f32[2,128,128]{2,1,0:T(8,128)S(1)} %constant_dynamic-slice_fusion), channel_id=1, source_target_pairs={{0,4},{4,8},{8,12},{12,0},{1,5},{5,9},{9,13},{13,1},{2,6},{6,10},{... | collective-permute-start | bytes 393224 | tf_op jit(solution)/shard_map/ppermute | solution.py:252
  15.5 0.1 fusion.5
  15.6 5.4 %collective-permute-done.6 = f32[2,128,128]{2,1,0:T(8,128)S(1)} collective-permute-done((f32[2,128,128]{2,1,0:T(8,128)S(1)}, f32[2,128,128]{2,1,0:T(8,128)S(1)}, u32[]{:S(2)}, u32[]{:S(2)}) %collective-permute-start.6) | collective-permute-done | bytes 131104 | tf_op jit(solution)/shard_map/ppermute | solution.py:252
  21.1 0.1 multiply_add_fusion.4
  21.2 0.1 collective-permute-start.7
  21.2 6.8 %collective-permute-done.7 = f32[2,128,128]{2,1,0:T(8,128)S(1)} collective-permute-done((f32[2,128,128]{2,1,0:T(8,128)S(1)}, f32[2,128,128]{2,1,0:T(8,128)S(1)}, u32[]{:S(2)}, u32[]{:S(2)}) %collective-permute-start.7) | collective-permute-done | bytes 131104 | tf_op jit(solution)/shard_map/ppermute | solution.py:252
  28.0 0.1 multiply_add_fusion.3
  28.1 0.1 collective-permute-start.8
  28.1 6.8 %collective-permute-done.8 = f32[2,128,128]{2,1,0:T(8,128)S(1)} collective-permute-done((f32[2,128,128]{2,1,0:T(8,128)S(1)}, f32[2,128,128]{2,1,0:T(8,128)S(1)}, u32[]{:S(2)}, u32[]{:S(2)}) %collective-permute-start.8) | collective-permute-done | bytes 131104 | tf_op jit(solution)/shard_map/ppermute | solution.py:252
  34.9 0.1 multiply_add_fusion.2
  35.0 0.1 collective-permute-start.9
  35.0 6.8 %collective-permute-done.9 = f32[2,128,128]{2,1,0:T(8,128)S(1)} collective-permute-done((f32[2,128,128]{2,1,0:T(8,128)S(1)}, f32[2,128,128]{2,1,0:T(8,128)S(1)}, u32[]{:S(2)}, u32[]{:S(2)}) %collective-permute-start.9) | collective-permute-done | bytes 131104 | tf_op jit(solution)/shard_map/ppermute | solution.py:252
  41.8 0.1 multiply_add_fusion.1
  41.9 0.1 collective-permute-start.10
  41.9 6.9 %collective-permute-done.10 = f32[2,128,128]{2,1,0:T(8,128)S(1)} collective-permute-done((f32[2,128,128]{2,1,0:T(8,128)S(1)}, f32[2,128,128]{2,1,0:T(8,128)S(1)}, u32[]{:S(2)}, u32[]{:S(2)}) %collective-permute-start.10) | collective-permute-done | bytes 131104 | tf_op jit(solution)/shard_map/ppermute | solution.py:252
  48.8 0.7 multiply_add_fusion
  49.6 7.7 %collective-permute-done = f32[2,128,128]{2,1,0:T(8,128)S(1)} collective-permute-done((f32[2,128,128]{2,1,0:T(8,128)S(1)}, f32[2,128,128]{2,1,0:T(8,128)S(1)}, u32[]{:S(2)}, u32[]{:S(2)}) %collective-permute-start) | collective-permute-done | bytes 131104 | tf_op jit(solution)/shard_map/ppermute | solution.py:252
  57.2 0.1 multiply_add_fusion.9
  57.3 0.1 collective-permute-start.1
  57.4 7.5 %collective-permute-done.1 = f32[2,128,128]{2,1,0:T(8,128)S(1)} collective-permute-done((f32[2,128,128]{2,1,0:T(8,128)S(1)}, f32[2,128,128]{2,1,0:T(8,128)S(1)}, u32[]{:S(2)}, u32[]{:S(2)}) %collective-permute-start.1) | collective-permute-done | bytes 131104 | tf_op jit(solution)/shard_map/ppermute | solution.py:252
  64.9 0.6 copy-done.9
  65.6 0.1 multiply_add_fusion.8
  65.6 0.1 collective-permute-start.2
  65.7 6.8 %collective-permute-done.2 = f32[2,128,128]{2,1,0:T(8,128)S(1)} collective-permute-done((f32[2,128,128]{2,1,0:T(8,128)S(1)}, f32[2,128,128]{2,1,0:T(8,128)S(1)}, u32[]{:S(2)}, u32[]{:S(2)}) %collective-permute-start.2) | collective-permute-done | bytes 131104 | tf_op jit(solution)/shard_map/ppermute | solution.py:252
  72.5 0.7 copy-done.10
  73.1 0.1 multiply_add_fusion.7
  73.2 0.1 collective-permute-start.3
  73.3 7.8 %collective-permute-done.3 = f32[2,128,128]{2,1,0:T(8,128)S(1)} collective-permute-done((f32[2,128,128]{2,1,0:T(8,128)S(1)}, f32[2,128,128]{2,1,0:T(8,128)S(1)}, u32[]{:S(2)}, u32[]{:S(2)}) %collective-permute-start.3) | collective-permute-done | bytes 131104 | tf_op jit(solution)/shard_map/ppermute | solution.py:252
  81.0 0.6 copy-done.11
  81.7 0.7 multiply_add_fusion.6
  82.4 7.1 %collective-permute-done.4 = f32[2,128,128]{2,1,0:T(8,128)} collective-permute-done((f32[2,128,128]{2,1,0:T(8,128)}, f32[2,128,128]{2,1,0:T(8,128)}, u32[]{:S(2)}, u32[]{:S(2)}) %collective-permute-start.4) | collective-permute-done | bytes 131104 | tf_op jit(solution)/shard_map/ppermute | solution.py:252
  89.5 0.1 multiply_add_fusion.5
  89.6 0.1 collective-permute-start.5
  89.6 1.1 collective-permute-done.11
  90.8 0.1 select_select_fusion
  90.9 5.5 %collective-permute-done.5 = f32[2,128,128]{2,1,0:T(8,128)S(1)} collective-permute-done((f32[2,128,128]{2,1,0:T(8,128)S(1)}, f32[2,128,128]{2,1,0:T(8,128)S(1)}, u32[]{:S(2)}, u32[]{:S(2)}) %collective-permute-start.5) | collective-permute-done | bytes 131104 | tf_op jit(solution)/shard_map/ppermute | solution.py:252
  96.4 1.2 select_select_fusion.1
  97.6 2.2 %copy-done.1 = bf16[1,1024,2048]{2,1,0:T(8,128)(2,1)S(1)} copy-done((bf16[1,1024,2048]{2,1,0:T(8,128)(2,1)S(1)}, bf16[1,1024,2048]{2,1,0:T(8,128)(2,1)}, u32[]{:S(2)}) %copy-start.1) | copy-done | bytes 4194328
  99.8 2.2 %copy-done.2 = bf16[1,1024,2048]{2,1,0:T(8,128)(2,1)S(1)} copy-done((bf16[1,1024,2048]{2,1,0:T(8,128)(2,1)S(1)}, bf16[1,1024,2048]{2,1,0:T(8,128)(2,1)}, u32[]{:S(2)}) %copy-start.2) | copy-done | bytes 4194328
  102.0 5.1 %finish0.1 = (bf16[1024,2048]{1,0:T(8,128)(2,1)}, f32[16,512]{1,0:T(8,128)S(1)}) custom-call(s32[16]{0:T(128)S(1)} %reduce.ends_ref, s32[1]{0:T(128)} %bitcast.1.off_ref, bf16[1024,2048]{1,0:T(8,128)(2,1)S(1)} %bitcast.35, bf16[1024,2048]{1,0:T(8,128)(2,1)S(1)} %bitcast.39, bf16[1024,128]{1,0:T(8,128)(2,1)S(1)} %bitcast.44, bf16[1024,128]{1,0:T(8,128)(2,1)S(1)} %bitcast.48, ...), custom_call_target="tpu_custom_call" | custom-call | flops 1073741824 | bytes 3145728 | tf_op jit(solution)/shard_map/finish0/pallas_call | solution.py:286
  107.1 5.1 %finish1.1 = (bf16[1024,2048]{1,0:T(8,128)(2,1)}, f32[16,512]{1,0:T(8,128)S(1)}) custom-call(s32[16]{0:T(128)S(1)} %reduce.ends_ref, s32[1]{0:T(128)} %bitcast.1.off_ref, bf16[1024,2048]{1,0:T(8,128)(2,1)S(1)} %bitcast.36, bf16[1024,2048]{1,0:T(8,128)(2,1)S(1)} %bitcast.40, bf16[1024,128]{1,0:T(8,128)(2,1)S(1)} %bitcast.45, ...), custom_call_target="tpu_custom_call", output_to_operand_aliasing={{0}: (13, {})} | custom-call | flops 1073741824 | bytes 3145728 | tf_op jit(solution)/shard_map/finish1/pallas_call | solution.py:286
  112.2 5.1 %finish2.1 = (bf16[1024,2048]{1,0:T(8,128)(2,1)}, f32[16,512]{1,0:T(8,128)S(1)}) custom-call(s32[16]{0:T(128)S(1)} %reduce.ends_ref, s32[1]{0:T(128)} %bitcast.1.off_ref, bf16[1024,2048]{1,0:T(8,128)(2,1)S(1)} %bitcast.37, bf16[1024,2048]{1,0:T(8,128)(2,1)S(1)} %bitcast.41, bf16[1024,128]{1,0:T(8,128)(2,1)S(1)} %bitcast.46, ...), custom_call_target="tpu_custom_call", output_to_operand_aliasing={{0}: (13, {})} | custom-call | flops 1073741824 | bytes 3145728 | tf_op jit(solution)/shard_map/finish2/pallas_call | solution.py:286
  117.3 5.1 %finish3.1 = (bf16[1024,2048]{1,0:T(8,128)(2,1)}, f32[16,512]{1,0:T(8,128)S(1)}) custom-call(s32[16]{0:T(128)S(1)} %reduce.ends_ref, s32[1]{0:T(128)} %bitcast.1.off_ref, bf16[1024,2048]{1,0:T(8,128)(2,1)S(1)} %bitcast.38, bf16[1024,2048]{1,0:T(8,128)(2,1)S(1)} %bitcast.42, bf16[1024,128]{1,0:T(8,128)(2,1)S(1)} %bitcast.47, ...), custom_call_target="tpu_custom_call", output_to_operand_aliasing={{0}: (13, {})} | custom-call | flops 1073741824 | bytes 3145728 | tf_op jit(solution)/shard_map/finish3/pallas_call | solution.py:286
  122.4 5.0 %collective-permute-done.12 = f32[16,2048]{1,0:T(8,128)S(1)} collective-permute-done((f32[16,2048]{1,0:T(8,128)S(1)}, f32[16,2048]{1,0:T(8,128)S(1)}, u32[]{:S(2)}, u32[]{:S(2)}) %collective-permute-start.12) | collective-permute-done | bytes 131104 | tf_op jit(solution)/shard_map/ppermute | solution.py:311
  127.4 0.1 collective-permute-start.13
  127.5 6.7 %collective-permute-done.13 = f32[16,2048]{1,0:T(8,128)S(1)} collective-permute-done((f32[16,2048]{1,0:T(8,128)S(1)}, f32[16,2048]{1,0:T(8,128)S(1)}, u32[]{:S(2)}, u32[]{:S(2)}) %collective-permute-start.13) | collective-permute-done | bytes 131104 | tf_op jit(solution)/shard_map/ppermute | solution.py:311
  134.2 0.1 add_divide_fusion
  134.3 5.6 %all_gather.3 = f32[32,2048]{1,0:T(8,128)S(1)} all-gather(f32[16,2048]{1,0:T(8,128)S(1)} %add_divide_fusion), channel_id=1, replica_groups=mesh['groups'=2,'ctx'=4,'dp'=2,'mp'=2] {'dp'}, dimensions={0}, use_global_device_ids=true | all-gather | bytes 393216 | tf_op jit(solution)/shard_map/all_gather | solution.py:314
  139.9 0.1 multiply_reduce_fusion
  140.0 0.3 fusion.10
  140.3 2.5 %all-reduce = (f32[32]{0:T(128)S(1)}, f32[16,32]{1,0:T(8,128)S(1)}) all-reduce(f32[32]{0:T(128)S(1)} %multiply_reduce_fusion, f32[16,32]{1,0:T(8,128)S(1)} %fusion.10), channel_id=1, replica_groups=mesh['groups'=2,'ctx'=4,'dp'=2,'mp'=2] {'mp'}, use_global_device_ids=true, to_apply=%region_2.3 | all-reduce | flops 544 | bytes 4352 | tf_op jit(solution)/shard_map/psum | solution.py:317
  142.9 0.1 dynamic_slice.91
  143.0 0.7 broadcast_multiply_fusion
  143.7 0.2 select_reduce_fusion.1
  143.9 0.5 log_subtract_fusion
  (31 shorter events, 0.1 us)
Async XLA Ops:
  1.5 2.2 %copy-start = (bf16[1,1024,2048]{2,1,0:T(8,128)(2,1)S(1)}, bf16[1,1024,2048]{2,1,0:T(8,128)(2,1)}, u32[]{:S(2)}) copy-start(bf16[1,1024,2048]{2,1,0:T(8,128)(2,1)} %param.9) | copy-start | bytes 12582916
  3.7 0.9 copy-start.3
  4.7 0.8 copy-start.7
  5.5 0.7 copy-start.8
  12.4 85.2 %copy-start.4 = (bf16[1,1024,128]{2,1,0:T(8,128)(2,1)S(1)}, bf16[1,1024,128]{2,1,0:T(8,128)(2,1)}, u32[]{:S(2)}) copy-start(bf16[1,1024,128]{2,1,0:T(8,128)(2,1)} %param.11) | copy-start | bytes 786436
  12.4 85.2 %copy-start.5 = (bf16[1,1024,128]{2,1,0:T(8,128)(2,1)S(1)}, bf16[1,1024,128]{2,1,0:T(8,128)(2,1)}, u32[]{:S(2)}) copy-start(bf16[1,1024,128]{2,1,0:T(8,128)(2,1)} %param.12) | copy-start | bytes 786436
  12.4 85.1 %copy-start.6 = (f32[2048]{0:T(1024)S(1)}, f32[2048]{0:T(1024)}, u32[]{:S(2)}) copy-start(f32[2048]{0:T(1024)} %param.15) | copy-start | bytes 24580
  12.5 8.6 %collective-permute-start.6 = (f32[2,128,128]{2,1,0:T(8,128)S(1)}, f32[2,128,128]{2,1,0:T(8,128)S(1)}, u32[]{:S(2)}, u32[]{:S(2)}) collective-permute-start(f32[2,128,128]{2,1,0:T(8,128)S(1)} %constant_dynamic-slice_fusion), channel_id=1, source_target_pairs={{0,4},{4,8},{8,12},{12,0},{1,5},{5,9},{9,13},{13,1},{2,6},{6,10},{... | collective-permute-start | bytes 393224 | tf_op jit(solution)/shard_map/ppermute | solution.py:252
  21.2 6.8 %collective-permute-start.7 = (f32[2,128,128]{2,1,0:T(8,128)S(1)}, f32[2,128,128]{2,1,0:T(8,128)S(1)}, u32[]{:S(2)}, u32[]{:S(2)}) collective-permute-start(f32[2,128,128]{2,1,0:T(8,128)S(1)} %multiply_add_fusion.4), channel_id=1, source_target_pairs={{0,4},{4,8},{8,12},{12,0},{1,5},{5,9},{9,13},{13,1},{2,6},{6,10},{... | collective-permute-start | bytes 393224 | tf_op jit(solution)/shard_map/ppermute | solution.py:252
  28.1 6.8 %collective-permute-start.8 = (f32[2,128,128]{2,1,0:T(8,128)S(1)}, f32[2,128,128]{2,1,0:T(8,128)S(1)}, u32[]{:S(2)}, u32[]{:S(2)}) collective-permute-start(f32[2,128,128]{2,1,0:T(8,128)S(1)} %multiply_add_fusion.3), channel_id=1, source_target_pairs={{0,4},{4,8},{8,12},{12,0},{1,5},{5,9},{9,13},{13,1},{2,6},{6,10},{... | collective-permute-start | bytes 393224 | tf_op jit(solution)/shard_map/ppermute | solution.py:252
  35.0 6.8 %collective-permute-start.9 = (f32[2,128,128]{2,1,0:T(8,128)S(1)}, f32[2,128,128]{2,1,0:T(8,128)S(1)}, u32[]{:S(2)}, u32[]{:S(2)}) collective-permute-start(f32[2,128,128]{2,1,0:T(8,128)S(1)} %multiply_add_fusion.2), channel_id=1, source_target_pairs={{0,4},{4,8},{8,12},{12,0},{1,5},{5,9},{9,13},{13,1},{2,6},{6,10},{... | collective-permute-start | bytes 393224 | tf_op jit(solution)/shard_map/ppermute | solution.py:252
  41.9 7.0 %collective-permute-start.10 = (f32[2,128,128]{2,1,0:T(8,128)S(1)}, f32[2,128,128]{2,1,0:T(8,128)S(1)}, u32[]{:S(2)}, u32[]{:S(2)}) collective-permute-start(f32[2,128,128]{2,1,0:T(8,128)S(1)} %multiply_add_fusion.1), channel_id=1, source_target_pairs={{0,4},{4,8},{8,12},{12,0},{1,5},{5,9},{9,13},{13,1},{2,6},{6,10},{... | collective-permute-start | bytes 393224 | tf_op jit(solution)/shard_map/ppermute | solution.py:252
  49.6 7.7 %collective-permute-start = (f32[2,128,128]{2,1,0:T(8,128)S(1)}, f32[2,128,128]{2,1,0:T(8,128)S(1)}, u32[]{:S(2)}, u32[]{:S(2)}) collective-permute-start(f32[2,128,128]{2,1,0:T(8,128)S(1)} %get-tuple-element.36), channel_id=1, source_target_pairs={{0,4},{4,8},{8,12},{12,0},{1,5},{5,9},{9,13},{13,1},{2,6},{6,10},{... | collective-permute-start | bytes 393224 | tf_op jit(solution)/shard_map/ppermute | solution.py:252
  57.3 7.6 %collective-permute-start.1 = (f32[2,128,128]{2,1,0:T(8,128)S(1)}, f32[2,128,128]{2,1,0:T(8,128)S(1)}, u32[]{:S(2)}, u32[]{:S(2)}) collective-permute-start(f32[2,128,128]{2,1,0:T(8,128)S(1)} %multiply_add_fusion.9), channel_id=1, source_target_pairs={{0,4},{4,8},{8,12},{12,0},{1,5},{5,9},{9,13},{13,1},{2,6},{6,10},{... | collective-permute-start | bytes 393224 | tf_op jit(solution)/shard_map/ppermute | solution.py:252
  64.9 0.6 copy-start.9
  65.6 6.8 %collective-permute-start.2 = (f32[2,128,128]{2,1,0:T(8,128)S(1)}, f32[2,128,128]{2,1,0:T(8,128)S(1)}, u32[]{:S(2)}, u32[]{:S(2)}) collective-permute-start(f32[2,128,128]{2,1,0:T(8,128)S(1)} %multiply_add_fusion.8), channel_id=1, source_target_pairs={{0,4},{4,8},{8,12},{12,0},{1,5},{5,9},{9,13},{13,1},{2,6},{6,10},{... | collective-permute-start | bytes 393224 | tf_op jit(solution)/shard_map/ppermute | solution.py:252
  72.5 0.7 copy-start.10
  73.2 7.8 %collective-permute-start.3 = (f32[2,128,128]{2,1,0:T(8,128)S(1)}, f32[2,128,128]{2,1,0:T(8,128)S(1)}, u32[]{:S(2)}, u32[]{:S(2)}) collective-permute-start(f32[2,128,128]{2,1,0:T(8,128)S(1)} %multiply_add_fusion.7), channel_id=1, source_target_pairs={{0,4},{4,8},{8,12},{12,0},{1,5},{5,9},{9,13},{13,1},{2,6},{6,10},{... | collective-permute-start | bytes 393224 | tf_op jit(solution)/shard_map/ppermute | solution.py:252
  81.0 0.7 copy-start.11
  82.4 7.1 %collective-permute-start.4 = (f32[2,128,128]{2,1,0:T(8,128)}, f32[2,128,128]{2,1,0:T(8,128)}, u32[]{:S(2)}, u32[]{:S(2)}) collective-permute-start(f32[2,128,128]{2,1,0:T(8,128)} %multiply_add_fusion.6), channel_id=1, source_target_pairs={{0,4},{4,8},{8,12},{12,0},{1,5},{5,9},{9,13},{13,1},{2,6},{6,10},{... | collective-permute-start | bytes 393224 | tf_op jit(solution)/shard_map/ppermute | solution.py:252
  82.4 8.4 %collective-permute-start.11 = (f32[2,128,128]{2,1,0:T(8,128)}, f32[2,128,128]{2,1,0:T(8,128)S(1)}, u32[]{:S(2)}, u32[]{:S(2)}) collective-permute-start(f32[2,128,128]{2,1,0:T(8,128)} %get-tuple-element.35), channel_id=1, source_target_pairs={{0,4},{4,8},{8,12},{12,0},{1,5},{5,9},{9,13},{13,1},{2,6},{6,10},{... | collective-permute-start | bytes 393224 | tf_op jit(solution)/shard_map/ppermute | solution.py:252
  89.6 6.8 %collective-permute-start.5 = (f32[2,128,128]{2,1,0:T(8,128)S(1)}, f32[2,128,128]{2,1,0:T(8,128)S(1)}, u32[]{:S(2)}, u32[]{:S(2)}) collective-permute-start(f32[2,128,128]{2,1,0:T(8,128)S(1)} %multiply_add_fusion.5), channel_id=1, source_target_pairs={{0,4},{4,8},{8,12},{12,0},{1,5},{5,9},{9,13},{13,1},{2,6},{6,10},{... | collective-permute-start | bytes 393224 | tf_op jit(solution)/shard_map/ppermute | solution.py:252
  97.6 2.2 %copy-start.1 = (bf16[1,1024,2048]{2,1,0:T(8,128)(2,1)S(1)}, bf16[1,1024,2048]{2,1,0:T(8,128)(2,1)}, u32[]{:S(2)}) copy-start(bf16[1,1024,2048]{2,1,0:T(8,128)(2,1)} %param.9) | copy-start | bytes 12582916
  99.8 2.2 %copy-start.2 = (bf16[1,1024,2048]{2,1,0:T(8,128)(2,1)S(1)}, bf16[1,1024,2048]{2,1,0:T(8,128)(2,1)}, u32[]{:S(2)}) copy-start(bf16[1,1024,2048]{2,1,0:T(8,128)(2,1)} %param.10) | copy-start | bytes 12582916
  117.3 10.2 %copy-start.12 = (s32[1,16]{1,0:T(1,128)S(1)}, s32[1,16]{1,0:T(1,128)}, u32[]{:S(2)}) copy-start(s32[1,16]{1,0:T(1,128)} %param.16) | copy-start | bytes 196
  117.3 26.4 %copy-start.13 = (s32[16]{0:T(128)S(1)}, s32[16]{0:T(128)}, u32[]{:S(2)}) copy-start(s32[16]{0:T(128)} %param.17) | copy-start | bytes 196
  122.4 5.0 %collective-permute-start.12 = (f32[16,2048]{1,0:T(8,128)S(1)}, f32[16,2048]{1,0:T(8,128)S(1)}, u32[]{:S(2)}, u32[]{:S(2)}) collective-permute-start(f32[16,2048]{1,0:T(8,128)S(1)} %constant_dynamic-update-slice_fusion), channel_id=1, source_target_pairs={{0,4},{4,0},{8,12},{12,8},{1,5},{5,1},{9,13},{13,9},{2,6},{6,2},{1... | collective-permute-start | bytes 393224 | tf_op jit(solution)/shard_map/ppermute | solution.py:311
  127.4 6.8 %collective-permute-start.13 = (f32[16,2048]{1,0:T(8,128)S(1)}, f32[16,2048]{1,0:T(8,128)S(1)}, u32[]{:S(2)}, u32[]{:S(2)}) collective-permute-start(f32[16,2048]{1,0:T(8,128)S(1)} %add.127), channel_id=1, source_target_pairs={{0,8},{4,12},{8,0},{12,4},{1,9},{5,13},{9,1},{13,5},{2,10},{6,14},... | collective-permute-start | bytes 393224 | tf_op jit(solution)/shard_map/ppermute | solution.py:311

commit v2 on v0

v2 whole, which is shorter than its diff:
```python
import functools

import jax
import jax.numpy as jnp
from jax import lax
from jax.experimental import pallas as pl
from jax.experimental.pallas import tpu as pltpu
from jax.sharding import PartitionSpec as P

SPAN = 256
WIDTH = 4096
HIGH = lax.Precision.HIGHEST

CHUNKS = 8
DELAY = 2
VMEM = 8 << 20
STEPS = 1


def dot(a, b, dims=((1,), (0,))):
    return lax.dot_general(a, b, (dims, ((), ())), preferred_element_type=jnp.float32)


def split3(v):
    hi = v.astype(jnp.bfloat16)
    rest = v - hi.astype(jnp.float32)
    mid = rest.astype(jnp.bfloat16)
    low = (rest - mid.astype(jnp.float32)).astype(jnp.bfloat16)
    return hi, mid, low


def first_end_from(ends, place):
    found = jnp.int32(1 << 30)
    for end in reversed(ends):
        found = jnp.where(end >= place, end, found)
    return found


def last_end_until(ends, place):
    found = jnp.int32(0)
    for end in ends:
        found = jnp.where(end <= place, end, found)
    return found


def prepare_kernel(
    lengths_ref,
    off_ref,
    b_ref,
    c_ref,
    raw_ref,
    rate_ref,
    e_ref,
    f_ref,
    last_ref,
    keep_ref,
    before_ref,
    rates_ref,
    left_ref,
    tail_ref,
    far_ref,
    member_ref,
    decay_ref,
):
    tokens, heads = e_ref.shape
    blocks = tokens // SPAN
    off = off_ref[0]
    docs = member_ref.shape[0]
    ends = [lengths_ref[0, 0]]
    for k in range(1, docs):
        ends.append(ends[-1] + lengths_ref[0, k])
    raw = raw_ref[...]
    steps = (jnp.maximum(raw, 0.0) + jnp.log1p(jnp.exp(-jnp.abs(raw)))).T
    logdecay = -rate_ref[...] * steps
    row = lax.broadcasted_iota(jnp.int32, (SPAN, SPAN), 0)
    col = lax.broadcasted_iota(jnp.int32, (SPAN, SPAN), 1)
    lower = jnp.where(row >= col, 1.0, 0.0).astype(jnp.bfloat16)
    places = lax.broadcasted_iota(jnp.int32, (1, tokens), 1) + off
    dend = jnp.full((1, tokens), 1 << 30, jnp.int32)
    docid = jnp.zeros((1, tokens), jnp.int32)
    for k in range(docs - 1, -1, -1):
        dend = jnp.where(ends[k] > places, ends[k], dend)
        docid = docid + (places >= ends[k]).astype(jnp.int32)
    member_ref[...] = (
        (docid == lax.broadcasted_iota(jnp.int32, (docs, tokens), 0)).astype(jnp.float32).astype(jnp.bfloat16)
    )
    device_end = jnp.where(off > 0, first_end_from(ends, off), 0)
    so_far = jnp.zeros((1, heads), jnp.float32)
    for b in range(blocks):
        rows = slice(b * SPAN, (b + 1) * SPAN)
        parts = split3(logdecay[rows])
        cum = dot(lower, parts[0]) + (dot(lower, parts[1]) + dot(lower, parts[2]))
        e_ref[rows, :] = jnp.exp(cum)
        f_ref[rows, :] = steps[rows] * jnp.exp(-cum)
        whole = cum[SPAN - 1 :]
        start = off + b * SPAN
        last_start = last_end_until(ends, start + SPAN - 1)
        prior_end = jnp.where(start > 0, first_end_from(ends, start), 0)
        before_ref[b : b + 1, :] = jnp.exp(so_far)
        so_far = so_far + whole
        last_ref[b : b + 1, :] = jnp.exp(whole)
        keep_ref[b : b + 1, :] = jnp.exp(whole) * jnp.where(last_start < start, 1.0, 0.0)
        bb, cc = b_ref[rows, :], c_ref[rows, :]
        same = (row >= col) & (row + start < dend[:, rows])
        left_ref[rows, 0:SPAN] = jnp.where(same, dot(cc, bb, ((1,), (1,))), 0.0).astype(jnp.bfloat16)
        place = lax.broadcasted_iota(jnp.int32, (SPAN, 128), 0) + start
        cf = cc.astype(jnp.float32)
        reach = jnp.where(place < prior_end, cf, 0.0).astype(jnp.bfloat16)
        left_ref[rows, SPAN : SPAN + 128] = reach
        left_ref[rows, SPAN + 128 :] = reach
        far_ref[rows, :] = jnp.where(place < device_end, cf, 0.0).astype(jnp.bfloat16)
        masked = jnp.where(place >= last_start, bb.astype(jnp.float32), 0.0)
        tail_ref[b * 128 : (b + 1) * 128, :] = masked.T.astype(jnp.bfloat16)
    through = jnp.where(last_end_until(ends, off + tokens - 1) < off, 1.0, 0.0)
    decay_ref[...] = jnp.broadcast_to(jnp.exp(so_far) * through, (128, heads)).T
    here = off // tokens
    per = heads // CHUNKS
    for r in range(rates_ref.shape[0] // per):
        chunk = jnp.clip(r - DELAY * here, 0, CHUNKS - 1)
        for h in range(per):
            rates_ref[r * per + h : r * per + h + 1, :] = decay_ref[pl.ds(chunk * per + h, 1), :]


def local_kernel(
    first,
    x_ref,
    z_ref,
    e_ref,
    f_ref,
    left_ref,
    tail_ref,
    last_ref,
    keep_ref,
    before_ref,
    local_ref,
    gate_ref,
    out_ref,
    right_ref,
    state_ref,
):
    block = pl.program_id(0)
    per = x_ref.shape[1] // 128

    @pl.when(block == 0)
    def _():
        state_ref[...] = jnp.zeros_like(state_ref)

    state = state_ref[...]
    high = state.astype(jnp.bfloat16)
    right_ref[SPAN : SPAN + 128] = high
    right_ref[SPAN + 128 :] = (state - high.astype(jnp.float32)).astype(jnp.bfloat16)
    for h in range(per):
        cols = slice(h * 128, (h + 1) * 128)
        head = first + h
        right_ref[0:SPAN, cols] = (
            x_ref[:, cols].astype(jnp.float32) * f_ref[:, head : head + 1]
        ).astype(jnp.bfloat16)
    inner = dot(left_ref[...], right_ref[...])
    added = dot(tail_ref[...], right_ref[0:SPAN])
    for h in range(per):
        cols = slice(h * 128, (h + 1) * 128)
        head = first + h
        half = 0.5 * z_ref[:, cols].astype(jnp.float32)
        gate = (half + half * jnp.tanh(half)) * e_ref[:, head : head + 1]
        gate_ref[:, cols] = (gate * before_ref[pl.ds(block, 1), head : head + 1]).astype(jnp.bfloat16)
        local_ref[:, cols] = inner[:, cols] * gate
        new = (
            keep_ref[pl.ds(block, 1), head : head + 1] * state[:, cols]
            + last_ref[pl.ds(block, 1), head : head + 1] * added[:, cols]
        )
        state_ref[:, cols] = new
        out_ref[h] = new


def finish_kernel(
    local_ref,
    gate_ref,
    far_ref,
    in_ref,
    gain_ref,
    member_ref,
    *rest,
):
    mixed_ref, sums_ref = rest[-2:]
    step = pl.program_id(0)
    cols = local_ref.shape[1]
    per = cols // 128
    row = lax.broadcasted_iota(jnp.int32, (cols, cols), 0)
    col = lax.broadcasted_iota(jnp.int32, (cols, cols), 1)
    mean = jnp.where(row // 128 == col // 128, 1.0 / 128, 0.0).astype(jnp.bfloat16)
    state = jnp.concatenate([in_ref[h] for h in range(per)], axis=1)
    high = state.astype(jnp.bfloat16)
    low = (state - high.astype(jnp.float32)).astype(jnp.bfloat16)
    right = jnp.concatenate([high, low], axis=0)
    gain = gain_ref[...]
    for b in range(local_ref.shape[0] // SPAN):
        rows = slice(b * SPAN, (b + 1) * SPAN)
        far = far_ref[rows, :]
        remote = dot(jnp.concatenate([far, far], axis=1), right)
        gated = local_ref[rows, :] + gate_ref[rows, :].astype(jnp.float32) * remote
        squares = dot((gated * gated).astype(jnp.bfloat16), mean)
        mixed_ref[rows, :] = (gated * lax.rsqrt(squares + 1e-05) * gain).astype(jnp.bfloat16)
    found = dot(member_ref[...], mixed_ref[...])

    @pl.when(step == 0)
    def _():
        sums_ref[...] = found

    @pl.when(step > 0)
    def _():
        sums_ref[...] += found


def after(value, *others):
    return lax.optimization_barrier((value, *others))[0]


def swapped(value, axis, by):
    return lax.ppermute(value, axis, [(i, i ^ by) for i in range(lax.axis_size(axis))])


def on_device(
    mixer_input,
    gate_input,
    input_proj,
    output_proj,
    step_raw,
    decay_rate,
    norm_gain,
    doc_lengths,
    partner,
):
    tokens = mixer_input.shape[1]
    width = mixer_input.shape[2]
    heads = decay_rate.shape[0]
    docs = doc_lengths.shape[1]
    blocks = tokens // SPAN
    count = lax.axis_size("ctx")
    here = lax.axis_index("ctx")
    x, z = mixer_input[0], gate_input[0]
    lengths = doc_lengths[0]
    row = lax.axis_index("dp")
    off = here * tokens
    places = [here == k for k in range(count)]
    firsts = [(row ^ j) * docs for j in range(lax.axis_size("dp"))]
    off, *rest = lax.optimization_barrier((off, *places, *firsts))
    places, firsts = rest[:count], rest[count:]
    off = off.astype(jnp.int32).reshape(1)
    per = heads // CHUNKS
    rounds = CHUNKS + DELAY * (count - 2)
    cols = per * 128
    f32, bf16 = jnp.float32, jnp.bfloat16
    smem = pl.BlockSpec(memory_space=pltpu.SMEM)
    whole = lambda *shape: pl.BlockSpec(shape, lambda *i: (0,) * len(shape))
    rows = lambda *shape: pl.BlockSpec(shape, lambda i: (i, 0))
    array = jax.ShapeDtypeStruct
    limit = pltpu.CompilerParams(vmem_limit_bytes=VMEM)

    shapes = [
        array((tokens, heads), f32),
        array((tokens, heads), f32),
        array((blocks, heads), f32),
        array((blocks, heads), f32),
        array((blocks, heads), f32),
        array((rounds * per, 128), f32),
        array((tokens, SPAN + 256), bf16),
        array((blocks * 128, SPAN), bf16),
        array((tokens, 128), bf16),
        array((docs, tokens), bf16),
    ]
    e, f, last, keep, before, rates, left, tails, far, member = pl.pallas_call(
        prepare_kernel,
        grid=(1,),
        in_specs=[smem, smem, whole(tokens, 128), whole(tokens, 128), whole(heads, tokens), whole(1, heads)],
        out_specs=[whole(*s.shape) for s in shapes],
        scratch_shapes=[pltpu.VMEM((heads, 128), f32)],
        out_shape=shapes,
        compiler_params=limit,
        cost_estimate=pl.CostEstimate(flops=1 << 28, bytes_accessed=4 << 20, transcendentals=0),
        name="prepare",
    )(doc_lengths, off, input_proj[0], output_proj[0], step_raw[0], decay_rate.reshape(1, heads))

    def local(c, last):
        block = pl.BlockSpec((SPAN, cols), lambda i: (i, c))
        return pl.pallas_call(
            functools.partial(local_kernel, c * per),
            grid=(blocks,),
            in_specs=[
                block,
                block,
                rows(SPAN, heads),
                rows(SPAN, heads),
                rows(SPAN, SPAN + 256),
                rows(128, SPAN),
                whole(blocks, heads),
                whole(blocks, heads),
                whole(blocks, heads),
            ],
            out_specs=[rows(SPAN, cols), rows(SPAN, cols), whole(per, 128, 128)],
            out_shape=[array((tokens, cols), f32), array((tokens, cols), bf16), array((per, 128, 128), f32)],
            scratch_shapes=[pltpu.VMEM((SPAN + 256, cols), bf16), pltpu.VMEM((128, cols), f32)],
            compiler_params=limit,
            cost_estimate=pl.CostEstimate(flops=1 << 20, bytes_accessed=1 << 16, transcendentals=0),
            name=f"local{c}",
        )(x, z, e, f, left, tails, last, keep, before)

    def finish(c, incoming, mixed):
        operands = [locals_[c], gates[c], far, incoming, norm_gain.reshape(1, width), member]
        specs = [
            rows(tokens // STEPS, cols),
            rows(tokens // STEPS, cols),
            rows(tokens // STEPS, 128),
            whole(per, 128, 128),
            pl.BlockSpec((1, cols), lambda i: (0, c)),
            pl.BlockSpec((docs, tokens // STEPS), lambda i: (0, i)),
        ]
        aliases = {}
        if mixed is not None:
            aliases = {len(operands): 0}
            operands.append(mixed)
            specs.append(pl.BlockSpec(memory_space=pl.ANY))
        return pl.pallas_call(
            finish_kernel,
            grid=(STEPS,),
            in_specs=specs,
            out_specs=[pl.BlockSpec((tokens // STEPS, cols), lambda i: (i, c)), whole(docs, cols)],
            out_shape=[array((tokens, width), bf16), array((docs, cols), f32)],
            input_output_aliases=aliases,
            compiler_params=limit,
            cost_estimate=pl.CostEstimate(flops=1 << 20, bytes_accessed=1 << 16, transcendentals=0),
            name=f"finish{c}",
        )(*operands)

    pairs = [(i, (i + 1) % count) for i in range(count)]
    locals_, gates, states, got, sums = [], [], [], [], []
    mixed = None
    sent = None

    def arrived(c, *ready):
        found = [got[c + DELAY * k] for k in range(count - 1)]
        found = lax.optimization_barrier((*found, *ready))
        value = jnp.zeros((per, 128, 128), f32)
        for k in range(1, count):
            value = jnp.where(places[k], found[k - 1], value)
        return value

    for r in range(rounds):
        ready = [] if sent is None else [sent]
        if r < CHUNKS:
            part, gate, state = local(r, after(last, *ready))
            locals_.append(part)
            gates.append(gate)
            states.append(state)
            ready.append(state)
        old = r - 1 - DELAY - DELAY * (count - 2)
        if old >= 0:
            mixed, part = finish(old, arrived(old, sent), mixed)
            sums.append(part)
            ready.append(part)
        mine = states[min(r, CHUNKS - 1)]
        for k in range(1, count):
            c = r - DELAY * k
            if 0 <= c < CHUNKS:
                mine = jnp.where(places[k], states[c], mine)
        if r >= DELAY:
            arriving = after(got[r - DELAY], *ready)
            mine = mine + rates[r * per : (r + 1) * per, None] * jnp.where(places[0], 0.0, arriving)
        elif r > 0:
            mine = after(mine, *ready)
        sent = mine
        got.append(lax.ppermute(sent, "ctx", pairs))
    for c in range(len(sums), CHUNKS):
        mixed, part = finish(c, arrived(c, *sums[-1:]), mixed)
        sums.append(part)

    totals = jnp.concatenate(sums, axis=1)
    if count <= 4:
        parts = [swapped(totals, "ctx", j) for j in range(1, count)]
        for part in parts:
            totals = totals + part
    else:
        reach = 1
        while reach < count:
            totals = totals + swapped(totals, "ctx", reach)
            reach *= 2
    pooled = totals / lengths[:, None].astype(f32)
    every = [pooled] + [swapped(pooled, "dp", j) for j in range(1, lax.axis_size("dp"))]
    found = [jnp.dot(pooled, one.T, precision=HIGH) for one in every]
    found += [jnp.sum(one * one, axis=1)[None] for one in every]
    found = jnp.concatenate(found, axis=0)
    for j in range(1, lax.axis_size("mp")):
        found = found + swapped(found, "mp", j)
    own = lax.rsqrt(found[len(every) * docs] / WIDTH + 1e-06)
    embedding = pooled * own[:, None]
    total = jnp.zeros((docs,), f32)
    picked = jnp.zeros((docs,), f32)
    ids = jnp.arange(docs, dtype=jnp.int32)
    for j in range(len(every)):
        other = lax.rsqrt(found[len(every) * docs + j] / WIDTH + 1e-06)
        similar = found[j * docs : (j + 1) * docs] * own[:, None] * other[None, :] / (WIDTH * 0.05)
        theirs = firsts[j] + ids
        others = theirs[None, :] != (firsts[0] + ids)[:, None]
        total = total + jnp.sum(jnp.where(others, jnp.exp(similar), 0.0), axis=1)
        picked = picked + jnp.sum(jnp.where(theirs[None, :] == partner[:, None], similar, 0.0), axis=1)
    doc_loss = jnp.log(total) - picked
    return (mixed[None], embedding, doc_loss)


def solution(mesh):
    in_specs = (
        P(("groups", "dp"), "ctx", "mp"),
        P(("groups", "dp"), "ctx", "mp"),
        P(("groups", "dp"), "ctx", None),
        P(("groups", "dp"), "ctx", None),
        P(("groups", "dp"), "mp", "ctx"),
        P("mp"),
        P("mp"),
        P(("groups", "dp"), None),
        P(("groups", "dp")),
    )
    out_specs = (P(("groups", "dp"), "ctx", "mp"), P(("groups", "dp"), "mp"), P(("groups", "dp")))
    return jax.shard_map(
        on_device, mesh=mesh, in_specs=in_specs, out_specs=out_specs, check_vma=False
    )
```

time: 270 us -> 82.4 us (0.31)
  local copies, waits for them, and re-layouts: 78.1 us -> 8.63 us
  waiting for transfers between devices: 71.8 us -> 25 us
  matrix products: 44.8 us -> 0.49 us
  other arithmetic: 36.9 us -> 2.75 us
  Pallas kernels: 0 us -> 28.5 us
  between operations: 14.3 us -> 0.89 us
  blocking collectives: 8.16 us -> 0 us
    dot_general x7 -> x2, matrix products: 44.8 us -> 0.49 us  [on_device(): found = [jnp.dot(pooled, one.T, precision=HIGH) for one in every]]
    ppermute x3 -> x17, waiting for transfers between devices: 64.4 us -> 25 us  [the longest x12 15.5 us: on_device(): got.append(lax.ppermute(sent, 'ctx', pairs))]
    pallas_call x0 -> x17, Pallas kernels: none -> 28.5 us  [the longest x8 15.7 us: local(): pl.pallas_call(functools.partial(local_kernel, c * per), grid=(blocks,),...]
    mul x2 -> x0, local copies, waits for them, and re-layouts: 11.6 us -> none  [on_device(): gated * lax.rsqrt(jnp.mean(gated * gated, axis=2, keepdims=True) + 1e-05)]
    convert_element_type x5 -> x1, other arithmetic: 11.5 us -> 0.01 us  [on_device(): pooled = totals / lengths[:, None].astype(f32)]
    add x1 -> x0, local copies, waits for them, and re-layouts: 10.3 us -> none  [on_device(): intra + local_part + remote_part]
    convert_element_type x1 -> x0, local copies, waits for them, and re-layouts: 9.9 us -> none  [on_device(): gate_input[0].reshape(tok_count, local_heads, head_size).astype(jnp.float32)]
    reshape x1 -> x0, local copies, waits for them, and re-layouts: 9.33 us -> none  [on_device(): (intra + local_part + remote_part).reshape(tok_count, local_heads, head_s...]
  transfers between devices with their start and end apart: 4 -> 17, of which waited for: 4 -> 14; matrix products, arithmetic and copies ran while one was open for 11% -> 1% of each run, Pallas kernels for 0% -> 29%
where the time goes in v2:
time: 82.4 us; the launch traced here: 82 us
  Pallas kernels  28.5 us (35%)
  waiting for transfers between devices  25 us (30%)
  starting transfers between devices  15.8 us (19%)
  local copies, waits for them, and re-layouts  8.63 us (10%)
  other arithmetic  2.75 us (3%)
  between operations  0.89 us (1%)
    pallas_call x8, Pallas kernels, local(): pl.pallas_call(functools.partial(local_kernel, c * per), grid=(blocks,),...  15.7 us
    ppermute x12, waiting for transfers between devices, on_device(): got.append(lax.ppermute(sent, 'ctx', pairs))  15.5 us
    pallas_call x8, Pallas kernels, finish(): pl.pallas_call(finish_kernel, grid=(STEPS,), in_specs=specs, out_specs=[p...  11.2 us
    ppermute x12, starting transfers between devices, on_device(): got.append(lax.ppermute(sent, 'ctx', pairs))  9.93 us
    ppermute x5, waiting for transfers between devices, swapped(): lax.ppermute(value, axis, [(i, i ^ by) for i in range(lax.axis_size(axis))])  9.49 us
    unnamed x29, local copies, waits for them, and re-layouts  8.45 us
    ppermute x5, starting transfers between devices, swapped(): lax.ppermute(value, axis, [(i, i ^ by) for i in range(lax.axis_size(axis))])  5.92 us
  transfers between devices with their start and end apart: 17, of which 14 were waited for; matrix products, arithmetic and copies ran while one was open for 1% of the time, Pallas kernels for 29%

profile of v2, /device:TPU:0, one launch (start us, length us, event | category | flops | bytes accessed | tf_op | source)
XLA Modules:
  0.0 82.0 jit_solution(5253720060579358802)
XLA Ops:
  0.7 0.9 %copy-done.4 = bf16[1,1024,128]{2,1,0:T(8,128)(2,1)S(1)} copy-done((bf16[1,1024,128]{2,1,0:T(8,128)(2,1)S(1)}, bf16[1,1024,128]{2,1,0:T(8,128)(2,1)}, u32[]{:S(2)}) %copy-start.4) | copy-done | bytes 262168
  1.6 0.9 %copy-done.5 = bf16[1,1024,128]{2,1,0:T(8,128)(2,1)S(1)} copy-done((bf16[1,1024,128]{2,1,0:T(8,128)(2,1)S(1)}, bf16[1,1024,128]{2,1,0:T(8,128)(2,1)}, u32[]{:S(2)}) %copy-start.5) | copy-done | bytes 262168
  2.6 0.8 %copy-done.6 = f32[1,16,1024]{2,1,0:T(8,128)S(1)} copy-done((f32[1,16,1024]{2,1,0:T(8,128)S(1)}, f32[1,16,1024]{2,1,0:T(8,128)}, u32[]{:S(2)}) %copy-start.6) | copy-done | bytes 65560
  3.4 0.7 copy-done.7
  4.0 0.7 copy-done.8
  4.7 1.5 %prepare.1 = (f32[1024,16]{1,0:T(8,128)S(1)}, f32[1024,16]{1,0:T(8,128)S(1)}, f32[4,16]{1,0:T(4,128)S(1)}, f32[4,16]{1,0:T(4,128)S(1)}, f32[4,16]{1,0:T(4,128)S(...) custom-call(s32[1,16]{1,0:T(1,128)S(1)} %copy-done.8, ...), custom_call_target="tpu_custom_call" | custom-call | flops 268435456 | bytes 4194304 | tf_op jit(solution)/shard_map/prepare/pallas_call | solution.py:271
  6.3 2.2 %copy-done = bf16[1,1024,2048]{2,1,0:T(8,128)(2,1)S(1)} copy-done((bf16[1,1024,2048]{2,1,0:T(8,128)(2,1)S(1)}, bf16[1,1024,2048]{2,1,0:T(8,128)(2,1)}, u32[]{:S(2)}) %copy-start) | copy-done | bytes 4194328
  8.4 2.2 %copy-done.2 = bf16[1,1024,2048]{2,1,0:T(8,128)(2,1)S(1)} copy-done((bf16[1,1024,2048]{2,1,0:T(8,128)(2,1)S(1)}, bf16[1,1024,2048]{2,1,0:T(8,128)(2,1)}, u32[]{:S(2)}) %copy-start.2) | copy-done | bytes 4194328
  10.6 2.0 %local0.1 = (f32[1024,256]{1,0:T(8,128)S(1)}, bf16[1024,256]{1,0:T(8,128)(2,1)S(1)}, f32[2,128,128]{2,1,0:T(8,128)S(1)}) custom-call(bf16[1024,2048]{1,0:T(8,128)(2,1)S(1)} %bitcast.17, bf16[1024,2048]{1,0:T(8,128)(2,1)S(1)} %bitcast.25, f32[1024,16]{1,0:T(8,128)S(1)} %get-tuple-element.103.e_ref, f32[1024,16]{1,0:T(8,128)S(1)} %get-tuple-element.104.f_ref, ...), custom_call_target="tpu_custom_call" | custom-call | flops 1048576 | bytes 65536 | tf_op jit(solution)/shard_map/local0/pallas_call | solution.py:285
  12.6 3.1 %collective-permute-start = (f32[2,128,128]{2,1,0:T(8,128)S(1)}, f32[2,128,128]{2,1,0:T(8,128)S(1)}, u32[]{:S(2)}, u32[]{:S(2)}) collective-permute-start(f32[2,128,128]{2,1,0:T(8,128)S(1)} %get-tuple-element.111), channel_id=1, source_target_pairs={{0,4},{4,8},{8,12},{12,0},{1,5},{5,9},{9,13},{13,1},{2,6},{6,10},{... | collective-permute-start | bytes 393224 | tf_op jit(solution)/shard_map/ppermute | solution.py:371
  15.7 2.0 %local1.1 = (f32[1024,256]{1,0:T(8,128)S(1)}, bf16[1024,256]{1,0:T(8,128)(2,1)S(1)}, f32[2,128,128]{2,1,0:T(8,128)S(1)}) custom-call(bf16[1024,2048]{1,0:T(8,128)(2,1)S(1)} %bitcast.18, bf16[1024,2048]{1,0:T(8,128)(2,1)S(1)} %bitcast.26, f32[1024,16]{1,0:T(8,128)S(1)} %get-tuple-element.103.e_ref, f32[1024,16]{1,0:T(8,128)S(1)} %get-tuple-element.104.f_ref, ...), custom_call_target="tpu_custom_call" | custom-call | flops 1048576 | bytes 65536 | tf_op jit(solution)/shard_map/local1/pallas_call | solution.py:285
  17.6 1.6 %collective-permute-start.1 = (f32[2,128,128]{2,1,0:T(8,128)S(1)}, f32[2,128,128]{2,1,0:T(8,128)S(1)}, u32[]{:S(2)}, u32[]{:S(2)}) collective-permute-start(f32[2,128,128]{2,1,0:T(8,128)S(1)} %get-tuple-element.115), channel_id=1, source_target_pairs={{0,4},{4,8},{8,12},{12,0},{1,5},{5,9},{9,13},{13,1},{2,6},{6,10},{... | collective-permute-start | bytes 393224 | tf_op jit(solution)/shard_map/ppermute | solution.py:371
  19.3 2.0 %local2.1 = (f32[1024,256]{1,0:T(8,128)S(1)}, bf16[1024,256]{1,0:T(8,128)(2,1)S(1)}, f32[2,128,128]{2,1,0:T(8,128)S(1)}) custom-call(bf16[1024,2048]{1,0:T(8,128)(2,1)S(1)} %bitcast.19, bf16[1024,2048]{1,0:T(8,128)(2,1)S(1)} %bitcast.27, f32[1024,16]{1,0:T(8,128)S(1)} %get-tuple-element.103.e_ref, f32[1024,16]{1,0:T(8,128)S(1)} %get-tuple-element.104.f_ref, ...), custom_call_target="tpu_custom_call" | custom-call | flops 1048576 | bytes 65536 | tf_op jit(solution)/shard_map/local2/pallas_call | solution.py:285
  21.3 1.6 %collective-permute-start.2 = (f32[2,128,128]{2,1,0:T(8,128)S(1)}, f32[2,128,128]{2,1,0:T(8,128)S(1)}, u32[]{:S(2)}, u32[]{:S(2)}) collective-permute-start(f32[2,128,128]{2,1,0:T(8,128)S(1)} %multiply_add_fusion.9), channel_id=1, source_target_pairs={{0,4},{4,8},{8,12},{12,0},{1,5},{5,9},{9,13},{13,1},{2,6},{6,10},{... | collective-permute-start | bytes 393224 | tf_op jit(solution)/shard_map/ppermute | solution.py:371
  22.9 2.0 %local3.1 = (f32[1024,256]{1,0:T(8,128)S(1)}, bf16[1024,256]{1,0:T(8,128)(2,1)S(1)}, f32[2,128,128]{2,1,0:T(8,128)S(1)}) custom-call(bf16[1024,2048]{1,0:T(8,128)(2,1)S(1)} %bitcast.20, bf16[1024,2048]{1,0:T(8,128)(2,1)S(1)} %bitcast.28, f32[1024,16]{1,0:T(8,128)S(1)} %get-tuple-element.103.e_ref, f32[1024,16]{1,0:T(8,128)S(1)} %get-tuple-element.104.f_ref, ...), custom_call_target="tpu_custom_call" | custom-call | flops 1048576 | bytes 65536 | tf_op jit(solution)/shard_map/local3/pallas_call | solution.py:285
  24.9 0.1 collective-permute-start.3
  25.0 2.0 %local4.1 = (f32[1024,256]{1,0:T(8,128)S(1)}, bf16[1024,256]{1,0:T(8,128)(2,1)S(1)}, f32[2,128,128]{2,1,0:T(8,128)S(1)}) custom-call(bf16[1024,2048]{1,0:T(8,128)(2,1)S(1)} %bitcast.21, bf16[1024,2048]{1,0:T(8,128)(2,1)S(1)} %bitcast.29, f32[1024,16]{1,0:T(8,128)S(1)} %get-tuple-element.103.e_ref, f32[1024,16]{1,0:T(8,128)S(1)} %get-tuple-element.104.f_ref, ...), custom_call_target="tpu_custom_call" | custom-call | flops 1048576 | bytes 65536 | tf_op jit(solution)/shard_map/local4/pallas_call | solution.py:285
  27.0 1.1 %collective-permute-done.2 = f32[2,128,128]{2,1,0:T(8,128)S(1)} collective-permute-done((f32[2,128,128]{2,1,0:T(8,128)S(1)}, f32[2,128,128]{2,1,0:T(8,128)S(1)}, u32[]{:S(2)}, u32[]{:S(2)}) %collective-permute-start.2) | collective-permute-done | bytes 131104 | tf_op jit(solution)/shard_map/ppermute | solution.py:371
  28.2 0.9 %collective-permute-start.4 = (f32[2,128,128]{2,1,0:T(8,128)S(1)}, f32[2,128,128]{2,1,0:T(8,128)S(1)}, u32[]{:S(2)}, u32[]{:S(2)}) collective-permute-start(f32[2,128,128]{2,1,0:T(8,128)S(1)} %multiply_add_fusion.7), channel_id=1, source_target_pairs={{0,4},{4,8},{8,12},{12,0},{1,5},{5,9},{9,13},{13,1},{2,6},{6,10},{... | collective-permute-start | bytes 393224 | tf_op jit(solution)/shard_map/ppermute | solution.py:371
  29.1 2.0 %local5.1 = (f32[1024,256]{1,0:T(8,128)S(1)}, bf16[1024,256]{1,0:T(8,128)(2,1)S(1)}, f32[2,128,128]{2,1,0:T(8,128)S(1)}) custom-call(bf16[1024,2048]{1,0:T(8,128)(2,1)S(1)} %bitcast.22, bf16[1024,2048]{1,0:T(8,128)(2,1)S(1)} %bitcast.30, f32[1024,16]{1,0:T(8,128)S(1)} %get-tuple-element.103.e_ref, f32[1024,16]{1,0:T(8,128)S(1)} %get-tuple-element.104.f_ref, ...), custom_call_target="tpu_custom_call" | custom-call | flops 1048576 | bytes 65536 | tf_op jit(solution)/shard_map/local5/pallas_call | solution.py:285
  31.0 1.8 %collective-permute-done.3 = f32[2,128,128]{2,1,0:T(8,128)S(1)} collective-permute-done((f32[2,128,128]{2,1,0:T(8,128)S(1)}, f32[2,128,128]{2,1,0:T(8,128)S(1)}, u32[]{:S(2)}, u32[]{:S(2)}) %collective-permute-start.3) | collective-permute-done | bytes 131104 | tf_op jit(solution)/shard_map/ppermute | solution.py:371
  32.9 0.1 collective-permute-start.5
  33.0 2.0 %local6.1 = (f32[1024,256]{1,0:T(8,128)S(1)}, bf16[1024,256]{1,0:T(8,128)(2,1)S(1)}, f32[2,128,128]{2,1,0:T(8,128)S(1)}) custom-call(bf16[1024,2048]{1,0:T(8,128)(2,1)S(1)} %bitcast.23, bf16[1024,2048]{1,0:T(8,128)(2,1)S(1)} %bitcast.31, f32[1024,16]{1,0:T(8,128)S(1)} %get-tuple-element.103.e_ref, f32[1024,16]{1,0:T(8,128)S(1)} %get-tuple-element.104.f_ref, ...), custom_call_target="tpu_custom_call" | custom-call | flops 1048576 | bytes 65536 | tf_op jit(solution)/shard_map/local6/pallas_call | solution.py:285
  35.0 1.0 %collective-permute-done.4 = f32[2,128,128]{2,1,0:T(8,128)S(1)} collective-permute-done((f32[2,128,128]{2,1,0:T(8,128)S(1)}, f32[2,128,128]{2,1,0:T(8,128)S(1)}, u32[]{:S(2)}, u32[]{:S(2)}) %collective-permute-start.4) | collective-permute-done | bytes 131104 | tf_op jit(solution)/shard_map/ppermute | solution.py:371
  36.0 0.2 collective-permute-start.7
  36.2 2.0 %local7.1 = (f32[1024,256]{1,0:T(8,128)S(1)}, bf16[1024,256]{1,0:T(8,128)(2,1)S(1)}, f32[2,128,128]{2,1,0:T(8,128)S(1)}) custom-call(bf16[1024,2048]{1,0:T(8,128)(2,1)S(1)} %bitcast.24, bf16[1024,2048]{1,0:T(8,128)(2,1)S(1)} %bitcast.32, f32[1024,16]{1,0:T(8,128)S(1)} %get-tuple-element.103.e_ref, f32[1024,16]{1,0:T(8,128)S(1)} %get-tuple-element.104.f_ref, ...), custom_call_target="tpu_custom_call" | custom-call | flops 1048576 | bytes 65536 | tf_op jit(solution)/shard_map/local7/pallas_call | solution.py:285
  38.2 1.4 %finish0.1 = (bf16[1024,2048]{1,0:T(8,128)(2,1)}, f32[16,256]{1,0:T(8,128)S(1)}) custom-call(f32[1024,256]{1,0:T(8,128)S(1)} %get-tuple-element.139.local_ref, bf16[1024,256]{1,0:T(8,128)(2,1)S(1)} %get-tuple-element.140.gate_ref, bf16[1024,128]{1,0:T(8,128)(2,1)S(1)} %get-tuple-element.137.far_ref, f32[2,128,128]{2,1,0:T(8,128)S(1)} %select_select_fusion.7.in_ref, ...), custom_call_target="tpu_custom_call" | custom-call | flops 1048576 | bytes 65536 | tf_op jit(solution)/shard_map/finish0/pallas_call | solution.py:322
  39.6 0.7 collective-permute-done.5
  40.3 0.5 collective-permute-start.6
  40.9 1.4 %finish1.1 = (bf16[1024,2048]{1,0:T(8,128)(2,1)}, f32[16,256]{1,0:T(8,128)S(1)}) custom-call(f32[1024,256]{1,0:T(8,128)S(1)} %get-tuple-element.147.local_ref, bf16[1024,256]{1,0:T(8,128)(2,1)S(1)} %get-tuple-element.148.gate_ref, bf16[1024,128]{1,0:T(8,128)(2,1)S(1)} %get-tuple-element.137.far_ref, ...), custom_call_target="tpu_custom_call", output_to_operand_aliasing={{0}: (6, {})} | custom-call | flops 1048576 | bytes 65536 | tf_op jit(solution)/shard_map/finish1/pallas_call | solution.py:322
  42.3 1.4 %collective-permute-done.7 = f32[2,128,128]{2,1,0:T(8,128)S(1)} collective-permute-done((f32[2,128,128]{2,1,0:T(8,128)S(1)}, f32[2,128,128]{2,1,0:T(8,128)S(1)}, u32[]{:S(2)}, u32[]{:S(2)}) %collective-permute-start.7) | collective-permute-done | bytes 131104 | tf_op jit(solution)/shard_map/ppermute | solution.py:371
  43.8 1.3 %collective-permute-start.9 = (f32[2,128,128]{2,1,0:T(8,128)S(1)}, f32[2,128,128]{2,1,0:T(8,128)S(1)}, u32[]{:S(2)}, u32[]{:S(2)}) collective-permute-start(f32[2,128,128]{2,1,0:T(8,128)S(1)} %multiply_add_fusion.3), channel_id=1, source_target_pairs={{0,4},{4,8},{8,12},{12,0},{1,5},{5,9},{9,13},{13,1},{2,6},{6,10},{... | collective-permute-start | bytes 393224 | tf_op jit(solution)/shard_map/ppermute | solution.py:371
  45.1 1.4 %finish2.1 = (bf16[1024,2048]{1,0:T(8,128)(2,1)}, f32[16,256]{1,0:T(8,128)S(1)}) custom-call(f32[1024,256]{1,0:T(8,128)S(1)} %get-tuple-element.155.local_ref, bf16[1024,256]{1,0:T(8,128)(2,1)S(1)} %get-tuple-element.156.gate_ref, bf16[1024,128]{1,0:T(8,128)(2,1)S(1)} %get-tuple-element.137.far_ref, ...), custom_call_target="tpu_custom_call", output_to_operand_aliasing={{0}: (6, {})} | custom-call | flops 1048576 | bytes 65536 | tf_op jit(solution)/shard_map/finish2/pallas_call | solution.py:322
  46.5 0.7 collective-permute-done.6
  47.2 0.4 collective-permute-start.8
  47.6 1.4 %finish3.1 = (bf16[1024,2048]{1,0:T(8,128)(2,1)}, f32[16,256]{1,0:T(8,128)S(1)}) custom-call(f32[1024,256]{1,0:T(8,128)S(1)} %get-tuple-element.163.local_ref, bf16[1024,256]{1,0:T(8,128)(2,1)S(1)} %get-tuple-element.164.gate_ref, bf16[1024,128]{1,0:T(8,128)(2,1)S(1)} %get-tuple-element.137.far_ref, ...), custom_call_target="tpu_custom_call", output_to_operand_aliasing={{0}: (6, {})} | custom-call | flops 1048576 | bytes 65536 | tf_op jit(solution)/shard_map/finish3/pallas_call | solution.py:322
  49.1 2.9 %collective-permute-done.9 = f32[2,128,128]{2,1,0:T(8,128)S(1)} collective-permute-done((f32[2,128,128]{2,1,0:T(8,128)S(1)}, f32[2,128,128]{2,1,0:T(8,128)S(1)}, u32[]{:S(2)}, u32[]{:S(2)}) %collective-permute-start.9) | collective-permute-done | bytes 131104 | tf_op jit(solution)/shard_map/ppermute | solution.py:371
  52.1 1.4 %finish4.1 = (bf16[1024,2048]{1,0:T(8,128)(2,1)}, f32[16,256]{1,0:T(8,128)S(1)}) custom-call(f32[1024,256]{1,0:T(8,128)S(1)} %get-tuple-element.171.local_ref, bf16[1024,256]{1,0:T(8,128)(2,1)S(1)} %get-tuple-element.172.gate_ref, bf16[1024,128]{1,0:T(8,128)(2,1)S(1)} %get-tuple-element.137.far_ref, ...), custom_call_target="tpu_custom_call", output_to_operand_aliasing={{0}: (6, {})} | custom-call | flops 1048576 | bytes 65536 | tf_op jit(solution)/shard_map/finish4/pallas_call | solution.py:322
  53.5 0.7 collective-permute-done.8
  54.2 0.1 collective-permute-start.10
  54.3 1.4 %finish5.1 = (bf16[1024,2048]{1,0:T(8,128)(2,1)}, f32[16,256]{1,0:T(8,128)S(1)}) custom-call(f32[1024,256]{1,0:T(8,128)S(1)} %get-tuple-element.181.local_ref, bf16[1024,256]{1,0:T(8,128)(2,1)S(1)} %get-tuple-element.182.gate_ref, bf16[1024,128]{1,0:T(8,128)(2,1)S(1)} %get-tuple-element.137.far_ref, ...), custom_call_target="tpu_custom_call", output_to_operand_aliasing={{0}: (6, {})} | custom-call | flops 1048576 | bytes 65536 | tf_op jit(solution)/shard_map/finish5/pallas_call | solution.py:322
  55.7 3.1 %collective-permute-done.11 = f32[2,128,128]{2,1,0:T(8,128)S(1)} collective-permute-done((f32[2,128,128]{2,1,0:T(8,128)S(1)}, f32[2,128,128]{2,1,0:T(8,128)S(1)}, u32[]{:S(2)}, u32[]{:S(2)}) %collective-permute-start.11) | collective-permute-done | bytes 131104 | tf_op jit(solution)/shard_map/ppermute | solution.py:371
  58.8 1.4 %finish6.1 = (bf16[1024,2048]{1,0:T(8,128)(2,1)}, f32[16,256]{1,0:T(8,128)S(1)}) custom-call(f32[1024,256]{1,0:T(8,128)S(1)} %get-tuple-element.179.local_ref, bf16[1024,256]{1,0:T(8,128)(2,1)S(1)} %get-tuple-element.180.gate_ref, bf16[1024,128]{1,0:T(8,128)(2,1)S(1)} %get-tuple-element.137.far_ref, ...), custom_call_target="tpu_custom_call", output_to_operand_aliasing={{0}: (6, {})} | custom-call | flops 1048576 | bytes 65536 | tf_op jit(solution)/shard_map/finish6/pallas_call | solution.py:322
  60.2 2.2 %collective-permute-done.10 = f32[2,128,128]{2,1,0:T(8,128)S(1)} collective-permute-done((f32[2,128,128]{2,1,0:T(8,128)S(1)}, f32[2,128,128]{2,1,0:T(8,128)S(1)}, u32[]{:S(2)}, u32[]{:S(2)}) %collective-permute-start.10) | collective-permute-done | bytes 131104 | tf_op jit(solution)/shard_map/ppermute | solution.py:371
  62.4 1.4 %finish7.1 = (bf16[1024,2048]{1,0:T(8,128)(2,1)}, f32[16,256]{1,0:T(8,128)S(1)}) custom-call(f32[1024,256]{1,0:T(8,128)S(1)} %get-tuple-element.135.local_ref, bf16[1024,256]{1,0:T(8,128)(2,1)S(1)} %get-tuple-element.136.gate_ref, bf16[1024,128]{1,0:T(8,128)(2,1)S(1)} %get-tuple-element.137.far_ref, ...), custom_call_target="tpu_custom_call", output_to_operand_aliasing={{0}: (6, {})} | custom-call | flops 1048576 | bytes 65536 | tf_op jit(solution)/shard_map/finish7/pallas_call | solution.py:322
  63.8 2.7 %collective-permute-start.13 = (f32[16,2048]{1,0:T(8,128)S(1)}, f32[16,2048]{1,0:T(8,128)S(1)}, u32[]{:S(2)}, u32[]{:S(2)}) collective-permute-start(f32[16,2048]{1,0:T(8,128)S(1)} %constant_dynamic-update-slice_fusion), channel_id=1, source_target_pairs={{0,8},{4,12},{8,0},{12,4},{1,9},{5,13},{9,1},{13,5},{2,10},{6,14},... | collective-permute-start | bytes 393224 | tf_op jit(solution)/shard_map/ppermute | solution.py:219
  66.5 1.7 %collective-permute-start.14 = (f32[16,2048]{1,0:T(8,128)S(1)}, f32[16,2048]{1,0:T(8,128)S(1)}, u32[]{:S(2)}, u32[]{:S(2)}) collective-permute-start(f32[16,2048]{1,0:T(8,128)S(1)} %constant_dynamic-update-slice_fusion), channel_id=1, source_target_pairs={{0,12},{4,8},{8,4},{12,0},{1,13},{5,9},{9,5},{13,1},{2,14},{6,10},... | collective-permute-start | bytes 393224 | tf_op jit(solution)/shard_map/ppermute | solution.py:219
  68.2 2.0 %collective-permute-done.12 = f32[16,2048]{1,0:T(8,128)S(1)} collective-permute-done((f32[16,2048]{1,0:T(8,128)S(1)}, f32[16,2048]{1,0:T(8,128)S(1)}, u32[]{:S(2)}, u32[]{:S(2)}) %collective-permute-start.12) | collective-permute-done | bytes 131104 | tf_op jit(solution)/shard_map/ppermute | solution.py:219
  70.2 3.2 %collective-permute-done.14 = f32[16,2048]{1,0:T(8,128)S(1)} collective-permute-done((f32[16,2048]{1,0:T(8,128)S(1)}, f32[16,2048]{1,0:T(8,128)S(1)}, u32[]{:S(2)}, u32[]{:S(2)}) %collective-permute-start.14) | collective-permute-done | bytes 131104 | tf_op jit(solution)/shard_map/ppermute | solution.py:219
  73.4 0.2 multiply_reduce_fusion.1
  73.6 1.5 %collective-permute-start.15 = (f32[16,2048]{1,0:T(8,128)S(1)}, f32[16,2048]{1,0:T(8,128)S(1)}, u32[]{:S(2)}, u32[]{:S(2)}) collective-permute-start(f32[16,2048]{1,0:T(8,128)S(1)} %get-tuple-element.208), channel_id=1, source_target_pairs={{0,2},{2,0},{1,3},{3,1},{4,6},{6,4},{5,7},{7,5},{8,10},{10,8},{9,1... | collective-permute-start | bytes 393224 | tf_op jit(solution)/shard_map/ppermute | solution.py:219
  75.1 0.1 copy.21
  75.2 0.2 fusion.11
  75.4 3.2 %collective-permute-done.15 = f32[16,2048]{1,0:T(8,128)S(1)} collective-permute-done((f32[16,2048]{1,0:T(8,128)S(1)}, f32[16,2048]{1,0:T(8,128)S(1)}, u32[]{:S(2)}, u32[]{:S(2)}) %collective-permute-start.15) | collective-permute-done | bytes 131104 | tf_op jit(solution)/shard_map/ppermute | solution.py:219
  78.6 0.1 multiply_reduce_fusion
  78.7 0.1 copy.22
  78.8 0.2 fusion.12
  79.1 0.1 pad_maximum_fusion
  79.3 1.1 %collective-permute-done.16 = f32[34,16]{0,1:T(8,128)S(1)} collective-permute-done((f32[34,16]{0,1:T(8,128)S(1)}, f32[34,16]{0,1:T(8,128)S(1)}, u32[]{:S(2)}, u32[]{:S(2)}) %collective-permute-start.16) | collective-permute-done | bytes 2208 | tf_op jit(solution)/shard_map/ppermute | solution.py:219
  80.4 0.1 fusion.17
  80.5 0.2 fusion.2
  80.7 0.7 broadcast_multiply_fusion
  81.4 0.1 select_reduce_fusion.2
  81.5 0.5 add_subtract_fusion
  (50 shorter events, 0.8 us)
Async XLA Ops:
  0.6 1.0 %copy-start.4 = (bf16[1,1024,128]{2,1,0:T(8,128)(2,1)S(1)}, bf16[1,1024,128]{2,1,0:T(8,128)(2,1)}, u32[]{:S(2)}) copy-start(bf16[1,1024,128]{2,1,0:T(8,128)(2,1)} %param.11) | copy-start | bytes 786436
  1.6 0.9 %copy-start.5 = (bf16[1,1024,128]{2,1,0:T(8,128)(2,1)S(1)}, bf16[1,1024,128]{2,1,0:T(8,128)(2,1)}, u32[]{:S(2)}) copy-start(bf16[1,1024,128]{2,1,0:T(8,128)(2,1)} %param.12) | copy-start | bytes 786436
  2.5 0.8 %copy-start.6 = (f32[1,16,1024]{2,1,0:T(8,128)S(1)}, f32[1,16,1024]{2,1,0:T(8,128)}, u32[]{:S(2)}) copy-start(f32[1,16,1024]{2,1,0:T(8,128)} %param.13) | copy-start | bytes 196612
  3.4 0.7 copy-start.7
  4.0 0.7 copy-start.8
  6.3 2.2 %copy-start = (bf16[1,1024,2048]{2,1,0:T(8,128)(2,1)S(1)}, bf16[1,1024,2048]{2,1,0:T(8,128)(2,1)}, u32[]{:S(2)}) copy-start(bf16[1,1024,2048]{2,1,0:T(8,128)(2,1)} %param.9) | copy-start | bytes 12582916
  8.4 2.2 %copy-start.2 = (bf16[1,1024,2048]{2,1,0:T(8,128)(2,1)S(1)}, bf16[1,1024,2048]{2,1,0:T(8,128)(2,1)}, u32[]{:S(2)}) copy-start(bf16[1,1024,2048]{2,1,0:T(8,128)(2,1)} %param.10) | copy-start | bytes 12582916
  12.6 8.7 %collective-permute-start = (f32[2,128,128]{2,1,0:T(8,128)S(1)}, f32[2,128,128]{2,1,0:T(8,128)S(1)}, u32[]{:S(2)}, u32[]{:S(2)}) collective-permute-start(f32[2,128,128]{2,1,0:T(8,128)S(1)} %get-tuple-element.111), channel_id=1, source_target_pairs={{0,4},{4,8},{8,12},{12,0},{1,5},{5,9},{9,13},{13,1},{2,6},{6,10},{... | collective-permute-start | bytes 393224 | tf_op jit(solution)/shard_map/ppermute | solution.py:371
  17.6 5.3 %copy-start.1 = (bf16[1,1024,2048]{2,1,0:T(8,128)(2,1)S(1)}, bf16[1,1024,2048]{2,1,0:T(8,128)(2,1)}, u32[]{:S(2)}) copy-start(bf16[1,1024,2048]{2,1,0:T(8,128)(2,1)} %param.9) | copy-start | bytes 12582916
  17.6 7.3 %collective-permute-start.1 = (f32[2,128,128]{2,1,0:T(8,128)S(1)}, f32[2,128,128]{2,1,0:T(8,128)S(1)}, u32[]{:S(2)}, u32[]{:S(2)}) collective-permute-start(f32[2,128,128]{2,1,0:T(8,128)S(1)} %get-tuple-element.115), channel_id=1, source_target_pairs={{0,4},{4,8},{8,12},{12,0},{1,5},{5,9},{9,13},{13,1},{2,6},{6,10},{... | collective-permute-start | bytes 393224 | tf_op jit(solution)/shard_map/ppermute | solution.py:371
  21.3 6.8 %collective-permute-start.2 = (f32[2,128,128]{2,1,0:T(8,128)S(1)}, f32[2,128,128]{2,1,0:T(8,128)S(1)}, u32[]{:S(2)}, u32[]{:S(2)}) collective-permute-start(f32[2,128,128]{2,1,0:T(8,128)S(1)} %multiply_add_fusion.9), channel_id=1, source_target_pairs={{0,4},{4,8},{8,12},{12,0},{1,5},{5,9},{9,13},{13,1},{2,6},{6,10},{... | collective-permute-start | bytes 393224 | tf_op jit(solution)/shard_map/ppermute | solution.py:371
  24.9 7.9 %collective-permute-start.3 = (f32[2,128,128]{2,1,0:T(8,128)S(1)}, f32[2,128,128]{2,1,0:T(8,128)S(1)}, u32[]{:S(2)}, u32[]{:S(2)}) collective-permute-start(f32[2,128,128]{2,1,0:T(8,128)S(1)} %multiply_add_fusion.8), channel_id=1, source_target_pairs={{0,4},{4,8},{8,12},{12,0},{1,5},{5,9},{9,13},{13,1},{2,6},{6,10},{... | collective-permute-start | bytes 393224 | tf_op jit(solution)/shard_map/ppermute | solution.py:371
  28.2 7.8 %collective-permute-start.4 = (f32[2,128,128]{2,1,0:T(8,128)S(1)}, f32[2,128,128]{2,1,0:T(8,128)S(1)}, u32[]{:S(2)}, u32[]{:S(2)}) collective-permute-start(f32[2,128,128]{2,1,0:T(8,128)S(1)} %multiply_add_fusion.7), channel_id=1, source_target_pairs={{0,4},{4,8},{8,12},{12,0},{1,5},{5,9},{9,13},{13,1},{2,6},{6,10},{... | collective-permute-start | bytes 393224 | tf_op jit(solution)/shard_map/ppermute | solution.py:371
  32.9 7.4 %collective-permute-start.5 = (f32[2,128,128]{2,1,0:T(8,128)S(1)}, f32[2,128,128]{2,1,0:T(8,128)S(1)}, u32[]{:S(2)}, u32[]{:S(2)}) collective-permute-start(f32[2,128,128]{2,1,0:T(8,128)S(1)} %multiply_add_fusion.6), channel_id=1, source_target_pairs={{0,4},{4,8},{8,12},{12,0},{1,5},{5,9},{9,13},{13,1},{2,6},{6,10},{... | collective-permute-start | bytes 393224 | tf_op jit(solution)/shard_map/ppermute | solution.py:371
  36.0 7.7 %collective-permute-start.7 = (f32[2,128,128]{2,1,0:T(8,128)S(1)}, f32[2,128,128]{2,1,0:T(8,128)S(1)}, u32[]{:S(2)}, u32[]{:S(2)}) collective-permute-start(f32[2,128,128]{2,1,0:T(8,128)S(1)} %multiply_add_fusion.5), channel_id=1, source_target_pairs={{0,4},{4,8},{8,12},{12,0},{1,5},{5,9},{9,13},{13,1},{2,6},{6,10},{... | collective-permute-start | bytes 393224 | tf_op jit(solution)/shard_map/ppermute | solution.py:371
  36.2 2.0 %copy-start.3 = (f32[2048]{0:T(1024)S(1)}, f32[2048]{0:T(1024)}, u32[]{:S(2)}) copy-start(f32[2048]{0:T(1024)} %param.15) | copy-start | bytes 24580
  40.3 6.8 %collective-permute-start.6 = (f32[2,128,128]{2,1,0:T(8,128)S(1)}, f32[2,128,128]{2,1,0:T(8,128)S(1)}, u32[]{:S(2)}, u32[]{:S(2)}) collective-permute-start(f32[2,128,128]{2,1,0:T(8,128)S(1)} %multiply_add_fusion.4), channel_id=1, source_target_pairs={{0,4},{4,8},{8,12},{12,0},{1,5},{5,9},{9,13},{13,1},{2,6},{6,10},{... | collective-permute-start | bytes 393224 | tf_op jit(solution)/shard_map/ppermute | solution.py:371
  43.8 8.2 %collective-permute-start.9 = (f32[2,128,128]{2,1,0:T(8,128)S(1)}, f32[2,128,128]{2,1,0:T(8,128)S(1)}, u32[]{:S(2)}, u32[]{:S(2)}) collective-permute-start(f32[2,128,128]{2,1,0:T(8,128)S(1)} %multiply_add_fusion.3), channel_id=1, source_target_pairs={{0,4},{4,8},{8,12},{12,0},{1,5},{5,9},{9,13},{13,1},{2,6},{6,10},{... | collective-permute-start | bytes 393224 | tf_op jit(solution)/shard_map/ppermute | solution.py:371
  47.2 6.9 %collective-permute-start.8 = (f32[2,128,128]{2,1,0:T(8,128)S(1)}, f32[2,128,128]{2,1,0:T(8,128)S(1)}, u32[]{:S(2)}, u32[]{:S(2)}) collective-permute-start(f32[2,128,128]{2,1,0:T(8,128)S(1)} %multiply_add_fusion.2), channel_id=1, source_target_pairs={{0,4},{4,8},{8,12},{12,0},{1,5},{5,9},{9,13},{13,1},{2,6},{6,10},{... | collective-permute-start | bytes 393224 | tf_op jit(solution)/shard_map/ppermute | solution.py:371
  52.0 6.8 %collective-permute-start.11 = (f32[2,128,128]{2,1,0:T(8,128)S(1)}, f32[2,128,128]{2,1,0:T(8,128)S(1)}, u32[]{:S(2)}, u32[]{:S(2)}) collective-permute-start(f32[2,128,128]{2,1,0:T(8,128)S(1)} %multiply_add_fusion.1), channel_id=1, source_target_pairs={{0,4},{4,8},{8,12},{12,0},{1,5},{5,9},{9,13},{13,1},{2,6},{6,10},{... | collective-permute-start | bytes 393224 | tf_op jit(solution)/shard_map/ppermute | solution.py:371
  54.2 8.2 %collective-permute-start.10 = (f32[2,128,128]{2,1,0:T(8,128)S(1)}, f32[2,128,128]{2,1,0:T(8,128)S(1)}, u32[]{:S(2)}, u32[]{:S(2)}) collective-permute-start(f32[2,128,128]{2,1,0:T(8,128)S(1)} %multiply_add_fusion), channel_id=1, source_target_pairs={{0,4},{4,8},{8,12},{12,0},{1,5},{5,9},{9,13},{13,1},{2,6},{6,10},{... | collective-permute-start | bytes 393224 | tf_op jit(solution)/shard_map/ppermute | solution.py:371
  60.2 8.0 %copy-start.9 = (s32[1,16]{1,0:T(1,128)S(1)}, s32[1,16]{1,0:T(1,128)}, u32[]{:S(2)}) copy-start(s32[1,16]{1,0:T(1,128)} %lengths_ref.1) | copy-start | bytes 196
  60.2 21.2 %copy-start.10 = (s32[16]{0:T(128)S(1)}, s32[16]{0:T(128)}, u32[]{:S(2)}) copy-start(s32[16]{0:T(128)} %param.17) | copy-start | bytes 196
  63.8 6.4 %collective-permute-start.12 = (f32[16,2048]{1,0:T(8,128)S(1)}, f32[16,2048]{1,0:T(8,128)S(1)}, u32[]{:S(2)}, u32[]{:S(2)}) collective-permute-start(f32[16,2048]{1,0:T(8,128)S(1)} %constant_dynamic-update-slice_fusion), channel_id=1, source_target_pairs={{0,4},{4,0},{8,12},{12,8},{1,5},{5,1},{9,13},{13,9},{2,6},{6,2},{1... | collective-permute-start | bytes 393224 | tf_op jit(solution)/shard_map/ppermute | solution.py:219
  63.8 6.4 %collective-permute-start.13 = (f32[16,2048]{1,0:T(8,128)S(1)}, f32[16,2048]{1,0:T(8,128)S(1)}, u32[]{:S(2)}, u32[]{:S(2)}) collective-permute-start(f32[16,2048]{1,0:T(8,128)S(1)} %constant_dynamic-update-slice_fusion), channel_id=1, source_target_pairs={{0,8},{4,12},{8,0},{12,4},{1,9},{5,13},{9,1},{13,5},{2,10},{6,14},... | collective-permute-start | bytes 393224 | tf_op jit(solution)/shard_map/ppermute | solution.py:219
  66.5 6.9 %collective-permute-start.14 = (f32[16,2048]{1,0:T(8,128)S(1)}, f32[16,2048]{1,0:T(8,128)S(1)}, u32[]{:S(2)}, u32[]{:S(2)}) collective-permute-start(f32[16,2048]{1,0:T(8,128)S(1)} %constant_dynamic-update-slice_fusion), channel_id=1, source_target_pairs={{0,12},{4,8},{8,4},{12,0},{1,13},{5,9},{9,5},{13,1},{2,14},{6,10},... | collective-permute-start | bytes 393224 | tf_op jit(solution)/shard_map/ppermute | solution.py:219
  73.6 5.0 %collective-permute-start.15 = (f32[16,2048]{1,0:T(8,128)S(1)}, f32[16,2048]{1,0:T(8,128)S(1)}, u32[]{:S(2)}, u32[]{:S(2)}) collective-permute-start(f32[16,2048]{1,0:T(8,128)S(1)} %get-tuple-element.208), channel_id=1, source_target_pairs={{0,2},{2,0},{1,3},{3,1},{4,6},{6,4},{5,7},{7,5},{8,10},{10,8},{9,1... | collective-permute-start | bytes 393224 | tf_op jit(solution)/shard_map/ppermute | solution.py:219
  79.2 1.2 %collective-permute-start.16 = (f32[34,16]{0,1:T(8,128)S(1)}, f32[34,16]{0,1:T(8,128)S(1)}, u32[]{:S(2)}, u32[]{:S(2)}) collective-permute-start(f32[34,16]{0,1:T(8,128)S(1)} %pad_maximum_fusion), channel_id=1, source_target_pairs={{0,1},{1,0},{2,3},{3,2},{4,5},{5,4},{6,7},{7,6},{8,9},{9,8},{10,11... | collective-permute-start | bytes 6536 | tf_op jit(solution)/shard_map/ppermute | solution.py:219

commit v3 on v2

--- a/solution.py
+++ b/solution.py
@@ -12,9 +12,9 @@
 HIGH = lax.Precision.HIGHEST
 
 CHUNKS = 8
-DELAY = 2
+DELAY = 3
 VMEM = 8 << 20
-STEPS = 1
+BATCHES = (8,)
 
 
 def dot(a, b, dims=((1,), (0,))):
@@ -135,55 +135,40 @@
     local_ref,
     gate_ref,
     out_ref,
-    right_ref,
-    state_ref,
 ):
-    block = pl.program_id(0)
-    per = x_ref.shape[1] // 128
-
-    @pl.when(block == 0)
-    def _():
-        state_ref[...] = jnp.zeros_like(state_ref)
-
-    state = state_ref[...]
-    high = state.astype(jnp.bfloat16)
-    right_ref[SPAN : SPAN + 128] = high
-    right_ref[SPAN + 128 :] = (state - high.astype(jnp.float32)).astype(jnp.bfloat16)
-    for h in range(per):
-        cols = slice(h * 128, (h + 1) * 128)
-        head = first + h
-        right_ref[0:SPAN, cols] = (
-            x_ref[:, cols].astype(jnp.float32) * f_ref[:, head : head + 1]
-        ).astype(jnp.bfloat16)
-    inner = dot(left_ref[...], right_ref[...])
-    added = dot(tail_ref[...], right_ref[0:SPAN])
-    for h in range(per):
-        cols = slice(h * 128, (h + 1) * 128)
-        head = first + h
-        half = 0.5 * z_ref[:, cols].astype(jnp.float32)
-        gate = (half + half * jnp.tanh(half)) * e_ref[:, head : head + 1]
-        gate_ref[:, cols] = (gate * before_ref[pl.ds(block, 1), head : head + 1]).astype(jnp.bfloat16)
-        local_ref[:, cols] = inner[:, cols] * gate
-        new = (
-            keep_ref[pl.ds(block, 1), head : head + 1] * state[:, cols]
-            + last_ref[pl.ds(block, 1), head : head + 1] * added[:, cols]
-        )
-        state_ref[:, cols] = new
-        out_ref[h] = new
-
-
-def finish_kernel(
-    local_ref,
-    gate_ref,
-    far_ref,
-    in_ref,
-    gain_ref,
-    member_ref,
-    *rest,
-):
-    mixed_ref, sums_ref = rest[-2:]
-    step = pl.program_id(0)
-    cols = local_ref.shape[1]
+    tokens, cols = local_ref.shape
+    heads = range(first // 128, (first + cols) // 128)
+    lanes = pl.ds(first, cols)
+
+    def spread(ref, rows, count):
+        return jnp.concatenate([jnp.broadcast_to(ref[rows, h : h + 1], (count, 128)) for h in heads], axis=1)
+
+    state = None
+    for b in range(tokens // SPAN):
+        rows = slice(b * SPAN, (b + 1) * SPAN)
+        one = slice(b, b + 1)
+        scaled = (x_ref[rows, lanes].astype(jnp.float32) * spread(f_ref, rows, SPAN)).astype(jnp.bfloat16)
+        added = dot(tail_ref[b * 128 : (b + 1) * 128, :], scaled)
+        inner = dot(left_ref[rows, 0:SPAN], scaled)
+        if state is not None:
+            high = state.astype(jnp.bfloat16)
+            low = (state - high.astype(jnp.float32)).astype(jnp.bfloat16)
+            inner = inner + dot(left_ref[rows, SPAN:], jnp.concatenate([high, low], axis=0))
+        half = 0.5 * z_ref[rows, lanes].astype(jnp.float32)
+        gate = (half + half * jnp.tanh(half)) * spread(e_ref, rows, SPAN)
+        local_ref[rows, :] = inner * gate
+        if b > 0:
+            gate = gate * spread(before_ref, one, 1)
+        gate_ref[rows, :] = gate.astype(jnp.bfloat16)
+        new = spread(last_ref, one, 1) * added
+        state = new if state is None else spread(keep_ref, one, 1) * state + new
+    for h in range(cols // 128):
+        out_ref[h] = state[:, h * 128 : (h + 1) * 128]
+
+
+def finish_kernel(first, local_ref, gate_ref, far_ref, in_ref, gain_ref, member_ref, *rest):
+    mixed_ref, sums_ref, held_ref, sems = rest[-4:]
+    tokens, cols = local_ref.shape
     per = cols // 128
     row = lax.broadcasted_iota(jnp.int32, (cols, cols), 0)
     col = lax.broadcasted_iota(jnp.int32, (cols, cols), 1)
@@ -192,23 +177,26 @@
     high = state.astype(jnp.bfloat16)
     low = (state - high.astype(jnp.float32)).astype(jnp.bfloat16)
     right = jnp.concatenate([high, low], axis=0)
-    gain = gain_ref[...]
-    for b in range(local_ref.shape[0] // SPAN):
+    gain = gain_ref[:, first : first + cols]
+    copies = []
+    for b in range(tokens // SPAN):
         rows = slice(b * SPAN, (b + 1) * SPAN)
         far = far_ref[rows, :]
         remote = dot(jnp.concatenate([far, far], axis=1), right)
-        gated = local_ref[rows, :] + gate_ref[rows, :].astype(jnp.float32) * remote
+        gated = local_ref[rows, :].astype(jnp.float32) + gate_ref[rows, :].astype(jnp.float32) * remote
         squares = dot((gated * gated).astype(jnp.bfloat16), mean)
-        mixed_ref[rows, :] = (gated * lax.rsqrt(squares + 1e-05) * gain).astype(jnp.bfloat16)
-    found = dot(member_ref[...], mixed_ref[...])
-
-    @pl.when(step == 0)
-    def _():
-        sums_ref[...] = found
-
-    @pl.when(step > 0)
-    def _():
-        sums_ref[...] += found
+        held_ref[rows, :] = (gated * lax.rsqrt(squares + 1e-05) * gain).astype(jnp.bfloat16)
+        copies.append(
+            pltpu.make_async_copy(
+                held_ref.at[pl.ds(b * SPAN, SPAN), :],
+                mixed_ref.at[pl.ds(b * SPAN, SPAN), pl.ds(first, cols)],
+                sems.at[b],
+            )
+        )
+        copies[-1].start()
+    sums_ref[...] = dot(member_ref[...], held_ref[...])
+    for copy in copies:
+        copy.wait()
 
 
 def after(value, *others):
@@ -252,8 +240,8 @@
     f32, bf16 = jnp.float32, jnp.bfloat16
     smem = pl.BlockSpec(memory_space=pltpu.SMEM)
     whole = lambda *shape: pl.BlockSpec(shape, lambda *i: (0,) * len(shape))
-    rows = lambda *shape: pl.BlockSpec(shape, lambda i: (i, 0))
     array = jax.ShapeDtypeStruct
+    VM = pl.BlockSpec(memory_space=pltpu.VMEM)
     limit = pltpu.CompilerParams(vmem_limit_bytes=VMEM)
 
     shapes = [
@@ -276,29 +264,16 @@
         scratch_shapes=[pltpu.VMEM((heads, 128), f32)],
         out_shape=shapes,
         compiler_params=limit,
-        cost_estimate=pl.CostEstimate(flops=1 << 28, bytes_accessed=4 << 20, transcendentals=0),
+        cost_estimate=pl.CostEstimate(flops=1 << 36, bytes_accessed=4 << 20, transcendentals=0),
         name="prepare",
     )(doc_lengths, off, input_proj[0], output_proj[0], step_raw[0], decay_rate.reshape(1, heads))
 
     def local(c, last):
-        block = pl.BlockSpec((SPAN, cols), lambda i: (i, c))
         return pl.pallas_call(
-            functools.partial(local_kernel, c * per),
-            grid=(blocks,),
-            in_specs=[
-                block,
-                block,
-                rows(SPAN, heads),
-                rows(SPAN, heads),
-                rows(SPAN, SPAN + 256),
-                rows(128, SPAN),
-                whole(blocks, heads),
-                whole(blocks, heads),
-                whole(blocks, heads),
-            ],
-            out_specs=[rows(SPAN, cols), rows(SPAN, cols), whole(per, 128, 128)],
+            functools.partial(local_kernel, c * cols),
+            in_specs=[VM] * 9,
+            out_specs=[VM] * 3,
             out_shape=[array((tokens, cols), f32), array((tokens, cols), bf16), array((per, 128, 128), f32)],
-            scratch_shapes=[pltpu.VMEM((SPAN + 256, cols), bf16), pltpu.VMEM((128, cols), f32)],
             compiler_params=limit,
             cost_estimate=pl.CostEstimate(flops=1 << 20, bytes_accessed=1 << 16, transcendentals=0),
             name=f"local{c}",
@@ -306,25 +281,18 @@
 
     def finish(c, incoming, mixed):
         operands = [locals_[c], gates[c], far, incoming, norm_gain.reshape(1, width), member]
-        specs = [
-            rows(tokens // STEPS, cols),
-            rows(tokens // STEPS, cols),
-            rows(tokens // STEPS, 128),
-            whole(per, 128, 128),
-            pl.BlockSpec((1, cols), lambda i: (0, c)),
-            pl.BlockSpec((docs, tokens // STEPS), lambda i: (0, i)),
-        ]
+        specs = [VM] * len(operands)
         aliases = {}
         if mixed is not None:
             aliases = {len(operands): 0}
             operands.append(mixed)
             specs.append(pl.BlockSpec(memory_space=pl.ANY))
         return pl.pallas_call(
-            finish_kernel,
-            grid=(STEPS,),
+            functools.partial(finish_kernel, c * cols),
             in_specs=specs,
-            out_specs=[pl.BlockSpec((tokens // STEPS, cols), lambda i: (i, c)), whole(docs, cols)],
+            out_specs=[pl.BlockSpec(memory_space=pl.ANY), VM],
             out_shape=[array((tokens, width), bf16), array((docs, cols), f32)],
+            scratch_shapes=[pltpu.VMEM((tokens, cols), bf16), pltpu.SemaphoreType.DMA((blocks,))],
             input_output_aliases=aliases,
             compiler_params=limit,
             cost_estimate=pl.CostEstimate(flops=1 << 20, bytes_accessed=1 << 16, transcendentals=0),
@@ -369,34 +337,46 @@
             mine = after(mine, *ready)
         sent = mine
         got.append(lax.ppermute(sent, "ctx", pairs))
-    for c in range(len(sums), CHUNKS):
-        mixed, part = finish(c, arrived(c, *sums[-1:]), mixed)
-        sums.append(part)
-
-    totals = jnp.concatenate(sums, axis=1)
-    if count <= 4:
-        parts = [swapped(totals, "ctx", j) for j in range(1, count)]
-        for part in parts:
-            totals = totals + part
-    else:
-        reach = 1
-        while reach < count:
-            totals = totals + swapped(totals, "ctx", reach)
-            reach *= 2
-    pooled = totals / lengths[:, None].astype(f32)
-    every = [pooled] + [swapped(pooled, "dp", j) for j in range(1, lax.axis_size("dp"))]
-    found = [jnp.dot(pooled, one.T, precision=HIGH) for one in every]
-    found += [jnp.sum(one * one, axis=1)[None] for one in every]
-    found = jnp.concatenate(found, axis=0)
+    spread = lengths[:, None].astype(f32)
+    pooled, found = [], []
+
+    def gather(low, high):
+        totals = jnp.concatenate(sums[low:high], axis=1)
+        if count <= 4:
+            parts = [swapped(totals, "ctx", j) for j in range(1, count)]
+            for part in parts:
+                totals = totals + part
+        else:
+            reach = 1
+            while reach < count:
+                totals = totals + swapped(totals, "ctx", reach)
+                reach *= 2
+        mean = totals / spread
+        every = [mean] + [swapped(mean, "dp", j) for j in range(1, lax.axis_size("dp"))]
+        part = [jnp.dot(mean, one.T, precision=HIGH) for one in every]
+        part += [jnp.sum(one * one, axis=1)[None] for one in every]
+        pooled.append(mean)
+        found.append(jnp.concatenate(part, axis=0))
+
+    low = 0
+    for high in BATCHES:
+        for c in range(len(sums), high):
+            mixed, part = finish(c, arrived(c, *sums[-1:]), mixed)
+            sums.append(part)
+        gather(low, high)
+        low = high
+    pooled = jnp.concatenate(pooled, axis=1)
+    found = sum(found)
+    count_dp = lax.axis_size("dp")
     for j in range(1, lax.axis_size("mp")):
         found = found + swapped(found, "mp", j)
-    own = lax.rsqrt(found[len(every) * docs] / WIDTH + 1e-06)
+    own = lax.rsqrt(found[count_dp * docs] / WIDTH + 1e-06)
     embedding = pooled * own[:, None]
     total = jnp.zeros((docs,), f32)
     picked = jnp.zeros((docs,), f32)
     ids = jnp.arange(docs, dtype=jnp.int32)
-    for j in range(len(every)):
-        other = lax.rsqrt(found[len(every) * docs + j] / WIDTH + 1e-06)
+    for j in range(count_dp):
+        other = lax.rsqrt(found[count_dp * docs + j] / WIDTH + 1e-06)
         similar = found[j * docs : (j + 1) * docs] * own[:, None] * other[None, :] / (WIDTH * 0.05)
         theirs = firsts[j] + ids
         others = theirs[None, :] != (firsts[0] + ids)[:, None]

time: 82.4 us -> 77.4 us (0.939)
  Pallas kernels: 28.5 us -> 20.3 us
  waiting for transfers between devices: 25 us -> 31.7 us
  local copies, waits for them, and re-layouts: 8.63 us -> 6.18 us
  starting transfers between devices: 15.8 us -> 14.8 us
    pallas_call x16, Pallas kernels: 26.9 us -> 18.7 us  [the longest x8 10.4 us: finish(): pl.pallas_call(functools.partial(finish_kernel, c * cols), in_specs=specs...]
    ppermute x12 -> x14, waiting for transfers between devices: 15.5 us -> 21.1 us  [on_device(): got.append(lax.ppermute(sent, 'ctx', pairs))]
    unnamed x29 -> x27, local copies, waits for them, and re-layouts: 8.45 us -> 6 us
    ppermute x12 -> x14, starting transfers between devices: 9.93 us -> 8.79 us  [on_device(): got.append(lax.ppermute(sent, 'ctx', pairs))]
    ppermute x5, waiting for transfers between devices: 9.49 us -> 10.5 us  [swapped(): lax.ppermute(value, axis, [(i, i ^ by) for i in range(lax.axis_size(axis))])]
  transfers between devices with their start and end apart: 17 -> 19, of which waited for: 14 -> 17; matrix products, arithmetic and copies ran while one was open for 1% -> 1% of each run, Pallas kernels for 29% -> 21%
where the time goes in v3:
time: 77.4 us; the launch traced here: 77.1 us
  waiting for transfers between devices  31.7 us (41%)
  Pallas kernels  20.3 us (26%)
  starting transfers between devices  14.8 us (19%)
  local copies, waits for them, and re-layouts  6.18 us (8%)
  other arithmetic  2.75 us (4%)
  between operations  1.01 us (1%)
    ppermute x14, waiting for transfers between devices, on_device(): got.append(lax.ppermute(sent, 'ctx', pairs))  21.1 us
    ppermute x5, waiting for transfers between devices, swapped(): lax.ppermute(value, axis, [(i, i ^ by) for i in range(lax.axis_size(axis))])  10.5 us
    pallas_call x8, Pallas kernels, finish(): pl.pallas_call(functools.partial(finish_kernel, c * cols), in_specs=specs...  10.4 us
    ppermute x14, starting transfers between devices, on_device(): got.append(lax.ppermute(sent, 'ctx', pairs))  8.79 us
    pallas_call x8, Pallas kernels, local(): pl.pallas_call(functools.partial(local_kernel, c * cols), in_specs=[VM] *...  8.31 us
    ppermute x5, starting transfers between devices, swapped(): lax.ppermute(value, axis, [(i, i ^ by) for i in range(lax.axis_size(axis))])  6.02 us
    unnamed x27, local copies, waits for them, and re-layouts  6 us
  transfers between devices with their start and end apart: 19, of which 17 were waited for; matrix products, arithmetic and copies ran while one was open for 1% of the time, Pallas kernels for 21%

profile of v3, /device:TPU:0, one launch (start us, length us, event | category | flops | bytes accessed | tf_op | source)
XLA Modules:
  0.0 77.1 jit_solution(9603267943116000411)
XLA Ops:
  0.7 0.9 %copy-done.3 = bf16[1,1024,128]{2,1,0:T(8,128)(2,1)S(1)} copy-done((bf16[1,1024,128]{2,1,0:T(8,128)(2,1)S(1)}, bf16[1,1024,128]{2,1,0:T(8,128)(2,1)}, u32[]{:S(2)}) %copy-start.3) | copy-done | bytes 262168
  1.6 0.9 %copy-done.4 = bf16[1,1024,128]{2,1,0:T(8,128)(2,1)S(1)} copy-done((bf16[1,1024,128]{2,1,0:T(8,128)(2,1)S(1)}, bf16[1,1024,128]{2,1,0:T(8,128)(2,1)}, u32[]{:S(2)}) %copy-start.4) | copy-done | bytes 262168
  2.6 0.8 %copy-done.5 = f32[1,16,1024]{2,1,0:T(8,128)S(1)} copy-done((f32[1,16,1024]{2,1,0:T(8,128)S(1)}, f32[1,16,1024]{2,1,0:T(8,128)}, u32[]{:S(2)}) %copy-start.5) | copy-done | bytes 65560
  3.4 0.7 copy-done.6
  4.0 0.7 copy-done.7
  4.7 1.5 %prepare.1 = (f32[1024,16]{1,0:T(8,128)S(1)}, f32[1024,16]{1,0:T(8,128)S(1)}, f32[4,16]{1,0:T(4,128)S(1)}, f32[4,16]{1,0:T(4,128)S(1)}, f32[4,16]{1,0:T(4,128)S(...) custom-call(s32[1,16]{1,0:T(1,128)S(1)} %copy-done.7, ...), custom_call_target="tpu_custom_call" | custom-call | flops 68719476736 | bytes 4194304 | tf_op jit(solution)/shard_map/prepare/pallas_call | solution.py:259
  6.3 0.6 copy-done
  6.9 1.3 %copy-done.1 = bf16[1,1024,2048]{2,1,0:T(8,128)(2,1)S(1)} copy-done((bf16[1,1024,2048]{2,1,0:T(8,128)(2,1)S(1)}, bf16[1,1024,2048]{2,1,0:T(8,128)(2,1)}, u32[]{:S(2)}) %copy-start.1) | copy-done | bytes 4194328
  8.2 1.0 %local0.1 = (f32[1024,256]{1,0:T(8,128)S(1)}, bf16[1024,256]{1,0:T(8,128)(2,1)S(1)}, f32[2,128,128]{2,1,0:T(8,128)S(1)}) custom-call(bf16[1024,2048]{1,0:T(8,128)(2,1)S(1)} %bitcast.17, bf16[1024,2048]{1,0:T(8,128)(2,1)S(1)} %bitcast.25, f32[1024,16]{1,0:T(8,128)S(1)} %get-tuple-element.105.e_ref, f32[1024,16]{1,0:T(8,128)S(1)} %get-tuple-element.106.f_ref, ...), custom_call_target="tpu_custom_call" | custom-call | flops 1048576 | bytes 65536 | tf_op jit(solution)/shard_map/local0/pallas_call | solution.py:272
  9.2 3.1 %collective-permute-start = (f32[2,128,128]{2,1,0:T(8,128)S(1)}, f32[2,128,128]{2,1,0:T(8,128)S(1)}, u32[]{:S(2)}, u32[]{:S(2)}) collective-permute-start(f32[2,128,128]{2,1,0:T(8,128)S(1)} %get-tuple-element.113), channel_id=1, source_target_pairs={{0,4},{4,8},{8,12},{12,0},{1,5},{5,9},{9,13},{13,1},{2,6},{6,10},{... | collective-permute-start | bytes 393224 | tf_op jit(solution)/shard_map/ppermute | solution.py:339
  12.3 1.0 %local1.1 = (f32[1024,256]{1,0:T(8,128)S(1)}, bf16[1024,256]{1,0:T(8,128)(2,1)S(1)}, f32[2,128,128]{2,1,0:T(8,128)S(1)}) custom-call(bf16[1024,2048]{1,0:T(8,128)(2,1)S(1)} %bitcast.18, bf16[1024,2048]{1,0:T(8,128)(2,1)S(1)} %bitcast.26, f32[1024,16]{1,0:T(8,128)S(1)} %get-tuple-element.105.e_ref, f32[1024,16]{1,0:T(8,128)S(1)} %get-tuple-element.106.f_ref, ...), custom_call_target="tpu_custom_call" | custom-call | flops 1048576 | bytes 65536 | tf_op jit(solution)/shard_map/local1/pallas_call | solution.py:272
  13.3 1.6 %collective-permute-start.1 = (f32[2,128,128]{2,1,0:T(8,128)S(1)}, f32[2,128,128]{2,1,0:T(8,128)S(1)}, u32[]{:S(2)}, u32[]{:S(2)}) collective-permute-start(f32[2,128,128]{2,1,0:T(8,128)S(1)} %get-tuple-element.117), channel_id=1, source_target_pairs={{0,4},{4,8},{8,12},{12,0},{1,5},{5,9},{9,13},{13,1},{2,6},{6,10},{... | collective-permute-start | bytes 393224 | tf_op jit(solution)/shard_map/ppermute | solution.py:339
  15.0 1.0 %local2.1 = (f32[1024,256]{1,0:T(8,128)S(1)}, bf16[1024,256]{1,0:T(8,128)(2,1)S(1)}, f32[2,128,128]{2,1,0:T(8,128)S(1)}) custom-call(bf16[1024,2048]{1,0:T(8,128)(2,1)S(1)} %bitcast.19, bf16[1024,2048]{1,0:T(8,128)(2,1)S(1)} %bitcast.27, f32[1024,16]{1,0:T(8,128)S(1)} %get-tuple-element.105.e_ref, f32[1024,16]{1,0:T(8,128)S(1)} %get-tuple-element.106.f_ref, ...), custom_call_target="tpu_custom_call" | custom-call | flops 1048576 | bytes 65536 | tf_op jit(solution)/shard_map/local2/pallas_call | solution.py:272
  16.0 1.6 %collective-permute-start.2 = (f32[2,128,128]{2,1,0:T(8,128)S(1)}, f32[2,128,128]{2,1,0:T(8,128)S(1)}, u32[]{:S(2)}, u32[]{:S(2)}) collective-permute-start(f32[2,128,128]{2,1,0:T(8,128)S(1)} %get-tuple-element.120), channel_id=1, source_target_pairs={{0,4},{4,8},{8,12},{12,0},{1,5},{5,9},{9,13},{13,1},{2,6},{6,10},{... | collective-permute-start | bytes 393224 | tf_op jit(solution)/shard_map/ppermute | solution.py:339
  17.6 1.0 %local3.1 = (f32[1024,256]{1,0:T(8,128)S(1)}, bf16[1024,256]{1,0:T(8,128)(2,1)S(1)}, f32[2,128,128]{2,1,0:T(8,128)S(1)}) custom-call(bf16[1024,2048]{1,0:T(8,128)(2,1)S(1)} %bitcast.20, bf16[1024,2048]{1,0:T(8,128)(2,1)S(1)} %bitcast.28, f32[1024,16]{1,0:T(8,128)S(1)} %get-tuple-element.105.e_ref, f32[1024,16]{1,0:T(8,128)S(1)} %get-tuple-element.106.f_ref, ...), custom_call_target="tpu_custom_call" | custom-call | flops 1048576 | bytes 65536 | tf_op jit(solution)/shard_map/local3/pallas_call | solution.py:272
  18.8 1.0 %local4.1 = (f32[1024,256]{1,0:T(8,128)S(1)}, bf16[1024,256]{1,0:T(8,128)(2,1)S(1)}, f32[2,128,128]{2,1,0:T(8,128)S(1)}) custom-call(bf16[1024,2048]{1,0:T(8,128)(2,1)S(1)} %bitcast.21, bf16[1024,2048]{1,0:T(8,128)(2,1)S(1)} %bitcast.29, f32[1024,16]{1,0:T(8,128)S(1)} %get-tuple-element.105.e_ref, f32[1024,16]{1,0:T(8,128)S(1)} %get-tuple-element.106.f_ref, ...), custom_call_target="tpu_custom_call" | custom-call | flops 1048576 | bytes 65536 | tf_op jit(solution)/shard_map/local4/pallas_call | solution.py:272
  19.9 1.6 %collective-permute-done.1 = f32[2,128,128]{2,1,0:T(8,128)S(1)} collective-permute-done((f32[2,128,128]{2,1,0:T(8,128)S(1)}, f32[2,128,128]{2,1,0:T(8,128)S(1)}, u32[]{:S(2)}, u32[]{:S(2)}) %collective-permute-start.1) | collective-permute-done | bytes 131104 | tf_op jit(solution)/shard_map/ppermute | solution.py:339
  21.5 0.2 collective-permute-start.4
  21.7 1.0 %local5.1 = (f32[1024,256]{1,0:T(8,128)S(1)}, bf16[1024,256]{1,0:T(8,128)(2,1)S(1)}, f32[2,128,128]{2,1,0:T(8,128)S(1)}) custom-call(bf16[1024,2048]{1,0:T(8,128)(2,1)S(1)} %bitcast.22, bf16[1024,2048]{1,0:T(8,128)(2,1)S(1)} %bitcast.30, f32[1024,16]{1,0:T(8,128)S(1)} %get-tuple-element.105.e_ref, f32[1024,16]{1,0:T(8,128)S(1)} %get-tuple-element.106.f_ref, ...), custom_call_target="tpu_custom_call" | custom-call | flops 1048576 | bytes 65536 | tf_op jit(solution)/shard_map/local5/pallas_call | solution.py:272
  22.8 1.5 %collective-permute-done.2 = f32[2,128,128]{2,1,0:T(8,128)S(1)} collective-permute-done((f32[2,128,128]{2,1,0:T(8,128)S(1)}, f32[2,128,128]{2,1,0:T(8,128)S(1)}, u32[]{:S(2)}, u32[]{:S(2)}) %collective-permute-start.2) | collective-permute-done | bytes 131104 | tf_op jit(solution)/shard_map/ppermute | solution.py:339
  24.3 0.1 collective-permute-start.7
  24.5 1.0 %local6.1 = (f32[1024,256]{1,0:T(8,128)S(1)}, bf16[1024,256]{1,0:T(8,128)(2,1)S(1)}, f32[2,128,128]{2,1,0:T(8,128)S(1)}) custom-call(bf16[1024,2048]{1,0:T(8,128)(2,1)S(1)} %bitcast.23, bf16[1024,2048]{1,0:T(8,128)(2,1)S(1)} %bitcast.31, f32[1024,16]{1,0:T(8,128)S(1)} %get-tuple-element.105.e_ref, f32[1024,16]{1,0:T(8,128)S(1)} %get-tuple-element.106.f_ref, ...), custom_call_target="tpu_custom_call" | custom-call | flops 1048576 | bytes 65536 | tf_op jit(solution)/shard_map/local6/pallas_call | solution.py:272
  25.5 1.6 %collective-permute-done.3 = f32[2,128,128]{2,1,0:T(8,128)S(1)} collective-permute-done((f32[2,128,128]{2,1,0:T(8,128)S(1)}, f32[2,128,128]{2,1,0:T(8,128)S(1)}, u32[]{:S(2)}, u32[]{:S(2)}) %collective-permute-start.3) | collective-permute-done | bytes 131104 | tf_op jit(solution)/shard_map/ppermute | solution.py:339
  27.2 1.0 %local7.1 = (f32[1024,256]{1,0:T(8,128)S(1)}, bf16[1024,256]{1,0:T(8,128)(2,1)S(1)}, f32[2,128,128]{2,1,0:T(8,128)S(1)}) custom-call(bf16[1024,2048]{1,0:T(8,128)(2,1)S(1)} %bitcast.24, bf16[1024,2048]{1,0:T(8,128)(2,1)S(1)} %bitcast.32, f32[1024,16]{1,0:T(8,128)S(1)} %get-tuple-element.105.e_ref, f32[1024,16]{1,0:T(8,128)S(1)} %get-tuple-element.106.f_ref, ...), custom_call_target="tpu_custom_call" | custom-call | flops 1048576 | bytes 65536 | tf_op jit(solution)/shard_map/local7/pallas_call | solution.py:272
  28.3 1.6 %collective-permute-done.4 = f32[2,128,128]{2,1,0:T(8,128)S(1)} collective-permute-done((f32[2,128,128]{2,1,0:T(8,128)S(1)}, f32[2,128,128]{2,1,0:T(8,128)S(1)}, u32[]{:S(2)}, u32[]{:S(2)}) %collective-permute-start.4) | collective-permute-done | bytes 131104 | tf_op jit(solution)/shard_map/ppermute | solution.py:339
  30.0 2.7 %collective-permute-done.7 = f32[2,128,128]{2,1,0:T(8,128)S(1)} collective-permute-done((f32[2,128,128]{2,1,0:T(8,128)S(1)}, f32[2,128,128]{2,1,0:T(8,128)S(1)}, u32[]{:S(2)}, u32[]{:S(2)}) %collective-permute-start.7) | collective-permute-done | bytes 131104 | tf_op jit(solution)/shard_map/ppermute | solution.py:339
  32.9 2.7 %collective-permute-done.6 = f32[2,128,128]{2,1,0:T(8,128)S(1)} collective-permute-done((f32[2,128,128]{2,1,0:T(8,128)S(1)}, f32[2,128,128]{2,1,0:T(8,128)S(1)}, u32[]{:S(2)}, u32[]{:S(2)}) %collective-permute-start.6) | collective-permute-done | bytes 131104 | tf_op jit(solution)/shard_map/ppermute | solution.py:339
  35.7 1.3 %finish0.1 = (bf16[1024,2048]{1,0:T(8,128)(2,1)}, f32[16,256]{1,0:T(8,128)S(1)}) custom-call(f32[1024,256]{1,0:T(8,128)S(1)} %get-tuple-element.144.local_ref, bf16[1024,256]{1,0:T(8,128)(2,1)S(1)} %get-tuple-element.145.gate_ref, bf16[1024,128]{1,0:T(8,128)(2,1)S(1)} %get-tuple-element.138.far_ref, f32[2,128,128]{2,1,0:T(8,128)S(1)} %select_select_fusion.7.in_ref, ...), custom_call_target="tpu_custom_call" | custom-call | flops 1048576 | bytes 65536 | tf_op jit(solution)/shard_map/finish0/pallas_call | solution.py:290
  37.0 1.3 %collective-permute-done.5 = f32[2,128,128]{2,1,0:T(8,128)S(1)} collective-permute-done((f32[2,128,128]{2,1,0:T(8,128)S(1)}, f32[2,128,128]{2,1,0:T(8,128)S(1)}, u32[]{:S(2)}, u32[]{:S(2)}) %collective-permute-start.5) | collective-permute-done | bytes 131104 | tf_op jit(solution)/shard_map/ppermute | solution.py:339
  38.4 0.2 collective-permute-start.8
  38.6 1.3 %finish1.1 = (bf16[1024,2048]{1,0:T(8,128)(2,1)}, f32[16,256]{1,0:T(8,128)S(1)}) custom-call(f32[1024,256]{1,0:T(8,128)S(1)} %get-tuple-element.152.local_ref, bf16[1024,256]{1,0:T(8,128)(2,1)S(1)} %get-tuple-element.153.gate_ref, bf16[1024,128]{1,0:T(8,128)(2,1)S(1)} %get-tuple-element.138.far_ref, ...), custom_call_target="tpu_custom_call", output_to_operand_aliasing={{0}: (6, {})} | custom-call | flops 1048576 | bytes 65536 | tf_op jit(solution)/shard_map/finish1/pallas_call | solution.py:290
  39.9 1.3 %collective-permute-done.10 = f32[2,128,128]{2,1,0:T(8,128)S(1)} collective-permute-done((f32[2,128,128]{2,1,0:T(8,128)S(1)}, f32[2,128,128]{2,1,0:T(8,128)S(1)}, u32[]{:S(2)}, u32[]{:S(2)}) %collective-permute-start.10) | collective-permute-done | bytes 131104 | tf_op jit(solution)/shard_map/ppermute | solution.py:339
  41.2 0.5 collective-permute-start.13
  41.7 1.3 %finish2.1 = (bf16[1024,2048]{1,0:T(8,128)(2,1)}, f32[16,256]{1,0:T(8,128)S(1)}) custom-call(f32[1024,256]{1,0:T(8,128)S(1)} %get-tuple-element.160.local_ref, bf16[1024,256]{1,0:T(8,128)(2,1)S(1)} %get-tuple-element.161.gate_ref, bf16[1024,128]{1,0:T(8,128)(2,1)S(1)} %get-tuple-element.138.far_ref, ...), custom_call_target="tpu_custom_call", output_to_operand_aliasing={{0}: (6, {})} | custom-call | flops 1048576 | bytes 65536 | tf_op jit(solution)/shard_map/finish2/pallas_call | solution.py:290
  43.1 0.9 %collective-permute-done.9 = f32[2,128,128]{2,1,0:T(8,128)S(1)} collective-permute-done((f32[2,128,128]{2,1,0:T(8,128)S(1)}, f32[2,128,128]{2,1,0:T(8,128)S(1)}, u32[]{:S(2)}, u32[]{:S(2)}) %collective-permute-start.9) | collective-permute-done | bytes 131104 | tf_op jit(solution)/shard_map/ppermute | solution.py:339
  44.0 1.1 %collective-permute-start.12 = (f32[2,128,128]{2,1,0:T(8,128)S(1)}, f32[2,128,128]{2,1,0:T(8,128)S(1)}, u32[]{:S(2)}, u32[]{:S(2)}) collective-permute-start(f32[2,128,128]{2,1,0:T(8,128)S(1)} %multiply_add_fusion.1), channel_id=1, source_target_pairs={{0,4},{4,8},{8,12},{12,0},{1,5},{5,9},{9,13},{13,1},{2,6},{6,10},{... | collective-permute-start | bytes 393224 | tf_op jit(solution)/shard_map/ppermute | solution.py:339
  45.2 1.3 %finish3.1 = (bf16[1024,2048]{1,0:T(8,128)(2,1)}, f32[16,256]{1,0:T(8,128)S(1)}) custom-call(f32[1024,256]{1,0:T(8,128)S(1)} %get-tuple-element.168.local_ref, bf16[1024,256]{1,0:T(8,128)(2,1)S(1)} %get-tuple-element.169.gate_ref, bf16[1024,128]{1,0:T(8,128)(2,1)S(1)} %get-tuple-element.138.far_ref, ...), custom_call_target="tpu_custom_call", output_to_operand_aliasing={{0}: (6, {})} | custom-call | flops 1048576 | bytes 65536 | tf_op jit(solution)/shard_map/finish3/pallas_call | solution.py:290
  46.5 0.3 collective-permute-done.8
  46.8 1.3 %finish4.1 = (bf16[1024,2048]{1,0:T(8,128)(2,1)}, f32[16,256]{1,0:T(8,128)S(1)}) custom-call(f32[1024,256]{1,0:T(8,128)S(1)} %get-tuple-element.180.local_ref, bf16[1024,256]{1,0:T(8,128)(2,1)S(1)} %get-tuple-element.181.gate_ref, bf16[1024,128]{1,0:T(8,128)(2,1)S(1)} %get-tuple-element.138.far_ref, ...), custom_call_target="tpu_custom_call", output_to_operand_aliasing={{0}: (6, {})} | custom-call | flops 1048576 | bytes 65536 | tf_op jit(solution)/shard_map/finish4/pallas_call | solution.py:290
  48.2 1.4 %collective-permute-done.13 = f32[2,128,128]{2,1,0:T(8,128)S(1)} collective-permute-done((f32[2,128,128]{2,1,0:T(8,128)S(1)}, f32[2,128,128]{2,1,0:T(8,128)S(1)}, u32[]{:S(2)}, u32[]{:S(2)}) %collective-permute-start.13) | collective-permute-done | bytes 131104 | tf_op jit(solution)/shard_map/ppermute | solution.py:339
  49.7 1.3 %finish5.1 = (bf16[1024,2048]{1,0:T(8,128)(2,1)}, f32[16,256]{1,0:T(8,128)S(1)}) custom-call(f32[1024,256]{1,0:T(8,128)S(1)} %get-tuple-element.178.local_ref, bf16[1024,256]{1,0:T(8,128)(2,1)S(1)} %get-tuple-element.179.gate_ref, bf16[1024,128]{1,0:T(8,128)(2,1)S(1)} %get-tuple-element.138.far_ref, ...), custom_call_target="tpu_custom_call", output_to_operand_aliasing={{0}: (6, {})} | custom-call | flops 1048576 | bytes 65536 | tf_op jit(solution)/shard_map/finish5/pallas_call | solution.py:290
  51.1 0.5 collective-permute-done.12
  51.5 1.3 %finish6.1 = (bf16[1024,2048]{1,0:T(8,128)(2,1)}, f32[16,256]{1,0:T(8,128)S(1)}) custom-call(f32[1024,256]{1,0:T(8,128)S(1)} %get-tuple-element.176.local_ref, bf16[1024,256]{1,0:T(8,128)(2,1)S(1)} %get-tuple-element.177.gate_ref, bf16[1024,128]{1,0:T(8,128)(2,1)S(1)} %get-tuple-element.138.far_ref, ...), custom_call_target="tpu_custom_call", output_to_operand_aliasing={{0}: (6, {})} | custom-call | flops 1048576 | bytes 65536 | tf_op jit(solution)/shard_map/finish6/pallas_call | solution.py:290
  52.9 3.6 %collective-permute-done.11 = f32[2,128,128]{2,1,0:T(8,128)S(1)} collective-permute-done((f32[2,128,128]{2,1,0:T(8,128)S(1)}, f32[2,128,128]{2,1,0:T(8,128)S(1)}, u32[]{:S(2)}, u32[]{:S(2)}) %collective-permute-start.11) | collective-permute-done | bytes 131104 | tf_op jit(solution)/shard_map/ppermute | solution.py:339
  56.5 1.3 %finish7.1 = (bf16[1024,2048]{1,0:T(8,128)(2,1)}, f32[16,256]{1,0:T(8,128)S(1)}) custom-call(f32[1024,256]{1,0:T(8,128)S(1)} %get-tuple-element.136.local_ref, bf16[1024,256]{1,0:T(8,128)(2,1)S(1)} %get-tuple-element.137.gate_ref, bf16[1024,128]{1,0:T(8,128)(2,1)S(1)} %get-tuple-element.138.far_ref, ...), custom_call_target="tpu_custom_call", output_to_operand_aliasing={{0}: (6, {})} | custom-call | flops 1048576 | bytes 65536 | tf_op jit(solution)/shard_map/finish7/pallas_call | solution.py:290
  57.9 0.7 collective-permute-start.15
  58.6 3.6 %collective-permute-start.16 = (f32[16,2048]{1,0:T(8,128)S(1)}, f32[16,2048]{1,0:T(8,128)S(1)}, u32[]{:S(2)}, u32[]{:S(2)}) collective-permute-start(f32[16,2048]{1,0:T(8,128)S(1)} %constant_dynamic-update-slice_fusion), channel_id=1, source_target_pairs={{0,12},{4,8},{8,4},{12,0},{1,13},{5,9},{9,5},{13,1},{2,14},{6,10},... | collective-permute-start | bytes 393224 | tf_op jit(solution)/shard_map/ppermute | solution.py:207
  62.3 2.0 %collective-permute-done.14 = f32[16,2048]{1,0:T(8,128)S(1)} collective-permute-done((f32[16,2048]{1,0:T(8,128)S(1)}, f32[16,2048]{1,0:T(8,128)S(1)}, u32[]{:S(2)}, u32[]{:S(2)}) %collective-permute-start.14) | collective-permute-done | bytes 131104 | tf_op jit(solution)/shard_map/ppermute | solution.py:207
  64.3 4.2 %collective-permute-done.15 = f32[16,2048]{1,0:T(8,128)S(1)} collective-permute-done((f32[16,2048]{1,0:T(8,128)S(1)}, f32[16,2048]{1,0:T(8,128)S(1)}, u32[]{:S(2)}, u32[]{:S(2)}) %collective-permute-start.15) | collective-permute-done | bytes 131104 | tf_op jit(solution)/shard_map/ppermute | solution.py:207
  68.5 0.2 multiply_reduce_fusion.1
  68.7 1.6 %collective-permute-start.17 = (f32[16,2048]{1,0:T(8,128)S(1)}, f32[16,2048]{1,0:T(8,128)S(1)}, u32[]{:S(2)}, u32[]{:S(2)}) collective-permute-start(f32[16,2048]{1,0:T(8,128)S(1)} %get-tuple-element.212), channel_id=1, source_target_pairs={{0,2},{2,0},{1,3},{3,1},{4,6},{6,4},{5,7},{7,5},{8,10},{10,8},{9,1... | collective-permute-start | bytes 393224 | tf_op jit(solution)/shard_map/ppermute | solution.py:207
  70.2 0.1 copy.21
  70.3 0.2 fusion.11
  70.6 3.2 %collective-permute-done.17 = f32[16,2048]{1,0:T(8,128)S(1)} collective-permute-done((f32[16,2048]{1,0:T(8,128)S(1)}, f32[16,2048]{1,0:T(8,128)S(1)}, u32[]{:S(2)}, u32[]{:S(2)}) %collective-permute-start.17) | collective-permute-done | bytes 131104 | tf_op jit(solution)/shard_map/ppermute | solution.py:207
  73.7 0.1 multiply_reduce_fusion
  73.9 0.1 copy.22
  73.9 0.2 fusion.12
  74.2 0.1 pad_maximum_fusion
  74.4 1.1 %collective-permute-done.18 = f32[34,16]{0,1:T(8,128)S(1)} collective-permute-done((f32[34,16]{0,1:T(8,128)S(1)}, f32[34,16]{0,1:T(8,128)S(1)}, u32[]{:S(2)}, u32[]{:S(2)}) %collective-permute-start.18) | collective-permute-done | bytes 2208 | tf_op jit(solution)/shard_map/ppermute | solution.py:207
  75.5 0.1 fusion.17
  75.6 0.2 fusion.2
  75.8 0.7 broadcast_multiply_fusion
  76.5 0.1 select_reduce_fusion.2
  76.6 0.5 add_subtract_fusion
  (53 shorter events, 1.2 us)
Async XLA Ops:
  0.6 1.0 %copy-start.3 = (bf16[1,1024,128]{2,1,0:T(8,128)(2,1)S(1)}, bf16[1,1024,128]{2,1,0:T(8,128)(2,1)}, u32[]{:S(2)}) copy-start(bf16[1,1024,128]{2,1,0:T(8,128)(2,1)} %param.11) | copy-start | bytes 786436
  1.6 0.9 %copy-start.4 = (bf16[1,1024,128]{2,1,0:T(8,128)(2,1)S(1)}, bf16[1,1024,128]{2,1,0:T(8,128)(2,1)}, u32[]{:S(2)}) copy-start(bf16[1,1024,128]{2,1,0:T(8,128)(2,1)} %param.12) | copy-start | bytes 786436
  2.5 0.8 %copy-start.5 = (f32[1,16,1024]{2,1,0:T(8,128)S(1)}, f32[1,16,1024]{2,1,0:T(8,128)}, u32[]{:S(2)}) copy-start(f32[1,16,1024]{2,1,0:T(8,128)} %param.13) | copy-start | bytes 196612
  3.4 0.7 copy-start.6
  4.0 0.7 copy-start.7
  4.7 2.2 %copy-start = (bf16[1,1024,2048]{2,1,0:T(8,128)(2,1)S(1)}, bf16[1,1024,2048]{2,1,0:T(8,128)(2,1)}, u32[]{:S(2)}) copy-start(bf16[1,1024,2048]{2,1,0:T(8,128)(2,1)} %param.9) | copy-start | bytes 12582916
  4.7 3.5 %copy-start.1 = (bf16[1,1024,2048]{2,1,0:T(8,128)(2,1)S(1)}, bf16[1,1024,2048]{2,1,0:T(8,128)(2,1)}, u32[]{:S(2)}) copy-start(bf16[1,1024,2048]{2,1,0:T(8,128)(2,1)} %param.10) | copy-start | bytes 12582916
  9.2 9.5 %collective-permute-start = (f32[2,128,128]{2,1,0:T(8,128)S(1)}, f32[2,128,128]{2,1,0:T(8,128)S(1)}, u32[]{:S(2)}, u32[]{:S(2)}) collective-permute-start(f32[2,128,128]{2,1,0:T(8,128)S(1)} %get-tuple-element.113), channel_id=1, source_target_pairs={{0,4},{4,8},{8,12},{12,0},{1,5},{5,9},{9,13},{13,1},{2,6},{6,10},{... | collective-permute-start | bytes 393224 | tf_op jit(solution)/shard_map/ppermute | solution.py:339
  13.3 8.2 %collective-permute-start.1 = (f32[2,128,128]{2,1,0:T(8,128)S(1)}, f32[2,128,128]{2,1,0:T(8,128)S(1)}, u32[]{:S(2)}, u32[]{:S(2)}) collective-permute-start(f32[2,128,128]{2,1,0:T(8,128)S(1)} %get-tuple-element.117), channel_id=1, source_target_pairs={{0,4},{4,8},{8,12},{12,0},{1,5},{5,9},{9,13},{13,1},{2,6},{6,10},{... | collective-permute-start | bytes 393224 | tf_op jit(solution)/shard_map/ppermute | solution.py:339
  16.0 8.3 %collective-permute-start.2 = (f32[2,128,128]{2,1,0:T(8,128)S(1)}, f32[2,128,128]{2,1,0:T(8,128)S(1)}, u32[]{:S(2)}, u32[]{:S(2)}) collective-permute-start(f32[2,128,128]{2,1,0:T(8,128)S(1)} %get-tuple-element.120), channel_id=1, source_target_pairs={{0,4},{4,8},{8,12},{12,0},{1,5},{5,9},{9,13},{13,1},{2,6},{6,10},{... | collective-permute-start | bytes 393224 | tf_op jit(solution)/shard_map/ppermute | solution.py:339
  18.7 8.4 %collective-permute-start.3 = (f32[2,128,128]{2,1,0:T(8,128)S(1)}, f32[2,128,128]{2,1,0:T(8,128)S(1)}, u32[]{:S(2)}, u32[]{:S(2)}) collective-permute-start(f32[2,128,128]{2,1,0:T(8,128)S(1)} %multiply_add_fusion.10), channel_id=1, source_target_pairs={{0,4},{4,8},{8,12},{12,0},{1,5},{5,9},{9,13},{13,1},{2,6},{6,10},{... | collective-permute-start | bytes 393224 | tf_op jit(solution)/shard_map/ppermute | solution.py:339
  21.5 8.4 %collective-permute-start.4 = (f32[2,128,128]{2,1,0:T(8,128)S(1)}, f32[2,128,128]{2,1,0:T(8,128)S(1)}, u32[]{:S(2)}, u32[]{:S(2)}) collective-permute-start(f32[2,128,128]{2,1,0:T(8,128)S(1)} %multiply_add_fusion.9), channel_id=1, source_target_pairs={{0,4},{4,8},{8,12},{12,0},{1,5},{5,9},{9,13},{13,1},{2,6},{6,10},{... | collective-permute-start | bytes 393224 | tf_op jit(solution)/shard_map/ppermute | solution.py:339
  24.3 8.4 %collective-permute-start.7 = (f32[2,128,128]{2,1,0:T(8,128)S(1)}, f32[2,128,128]{2,1,0:T(8,128)S(1)}, u32[]{:S(2)}, u32[]{:S(2)}) collective-permute-start(f32[2,128,128]{2,1,0:T(8,128)S(1)} %multiply_add_fusion.8), channel_id=1, source_target_pairs={{0,4},{4,8},{8,12},{12,0},{1,5},{5,9},{9,13},{13,1},{2,6},{6,10},{... | collective-permute-start | bytes 393224 | tf_op jit(solution)/shard_map/ppermute | solution.py:339
  27.2 8.5 %copy-start.2 = (f32[2048]{0:T(1024)S(1)}, f32[2048]{0:T(1024)}, u32[]{:S(2)}) copy-start(f32[2048]{0:T(1024)} %param.15) | copy-start | bytes 24580
  27.2 8.4 %collective-permute-start.6 = (f32[2,128,128]{2,1,0:T(8,128)S(1)}, f32[2,128,128]{2,1,0:T(8,128)S(1)}, u32[]{:S(2)}, u32[]{:S(2)}) collective-permute-start(f32[2,128,128]{2,1,0:T(8,128)S(1)} %multiply_add_fusion.7), channel_id=1, source_target_pairs={{0,4},{4,8},{8,12},{12,0},{1,5},{5,9},{9,13},{13,1},{2,6},{6,10},{... | collective-permute-start | bytes 393224 | tf_op jit(solution)/shard_map/ppermute | solution.py:339
  30.0 8.4 %collective-permute-start.5 = (f32[2,128,128]{2,1,0:T(8,128)S(1)}, f32[2,128,128]{2,1,0:T(8,128)S(1)}, u32[]{:S(2)}, u32[]{:S(2)}) collective-permute-start(f32[2,128,128]{2,1,0:T(8,128)S(1)} %multiply_add_fusion.6), channel_id=1, source_target_pairs={{0,4},{4,8},{8,12},{12,0},{1,5},{5,9},{9,13},{13,1},{2,6},{6,10},{... | collective-permute-start | bytes 393224 | tf_op jit(solution)/shard_map/ppermute | solution.py:339
  32.8 8.4 %collective-permute-start.10 = (f32[2,128,128]{2,1,0:T(8,128)S(1)}, f32[2,128,128]{2,1,0:T(8,128)S(1)}, u32[]{:S(2)}, u32[]{:S(2)}) collective-permute-start(f32[2,128,128]{2,1,0:T(8,128)S(1)} %multiply_add_fusion.5), channel_id=1, source_target_pairs={{0,4},{4,8},{8,12},{12,0},{1,5},{5,9},{9,13},{13,1},{2,6},{6,10},{... | collective-permute-start | bytes 393224 | tf_op jit(solution)/shard_map/ppermute | solution.py:339
  35.6 8.4 %collective-permute-start.9 = (f32[2,128,128]{2,1,0:T(8,128)S(1)}, f32[2,128,128]{2,1,0:T(8,128)S(1)}, u32[]{:S(2)}, u32[]{:S(2)}) collective-permute-start(f32[2,128,128]{2,1,0:T(8,128)S(1)} %multiply_add_fusion.4), channel_id=1, source_target_pairs={{0,4},{4,8},{8,12},{12,0},{1,5},{5,9},{9,13},{13,1},{2,6},{6,10},{... | collective-permute-start | bytes 393224 | tf_op jit(solution)/shard_map/ppermute | solution.py:339
  38.4 8.4 %collective-permute-start.8 = (f32[2,128,128]{2,1,0:T(8,128)S(1)}, f32[2,128,128]{2,1,0:T(8,128)S(1)}, u32[]{:S(2)}, u32[]{:S(2)}) collective-permute-start(f32[2,128,128]{2,1,0:T(8,128)S(1)} %multiply_add_fusion.3), channel_id=1, source_target_pairs={{0,4},{4,8},{8,12},{12,0},{1,5},{5,9},{9,13},{13,1},{2,6},{6,10},{... | collective-permute-start | bytes 393224 | tf_op jit(solution)/shard_map/ppermute | solution.py:339
  41.2 8.4 %collective-permute-start.13 = (f32[2,128,128]{2,1,0:T(8,128)S(1)}, f32[2,128,128]{2,1,0:T(8,128)S(1)}, u32[]{:S(2)}, u32[]{:S(2)}) collective-permute-start(f32[2,128,128]{2,1,0:T(8,128)S(1)} %multiply_add_fusion.2), channel_id=1, source_target_pairs={{0,4},{4,8},{8,12},{12,0},{1,5},{5,9},{9,13},{13,1},{2,6},{6,10},{... | collective-permute-start | bytes 393224 | tf_op jit(solution)/shard_map/ppermute | solution.py:339
  44.0 7.5 %collective-permute-start.12 = (f32[2,128,128]{2,1,0:T(8,128)S(1)}, f32[2,128,128]{2,1,0:T(8,128)S(1)}, u32[]{:S(2)}, u32[]{:S(2)}) collective-permute-start(f32[2,128,128]{2,1,0:T(8,128)S(1)} %multiply_add_fusion.1), channel_id=1, source_target_pairs={{0,4},{4,8},{8,12},{12,0},{1,5},{5,9},{9,13},{13,1},{2,6},{6,10},{... | collective-permute-start | bytes 393224 | tf_op jit(solution)/shard_map/ppermute | solution.py:339
  49.6 6.8 %collective-permute-start.11 = (f32[2,128,128]{2,1,0:T(8,128)S(1)}, f32[2,128,128]{2,1,0:T(8,128)S(1)}, u32[]{:S(2)}, u32[]{:S(2)}) collective-permute-start(f32[2,128,128]{2,1,0:T(8,128)S(1)} %multiply_add_fusion), channel_id=1, source_target_pairs={{0,4},{4,8},{8,12},{12,0},{1,5},{5,9},{9,13},{13,1},{2,6},{6,10},{... | collective-permute-start | bytes 393224 | tf_op jit(solution)/shard_map/ppermute | solution.py:339
  52.9 9.4 %copy-start.8 = (s32[1,16]{1,0:T(1,128)S(1)}, s32[1,16]{1,0:T(1,128)}, u32[]{:S(2)}) copy-start(s32[1,16]{1,0:T(1,128)} %lengths_ref.1) | copy-start | bytes 196
  52.9 23.6 %copy-start.9 = (s32[16]{0:T(128)S(1)}, s32[16]{0:T(128)}, u32[]{:S(2)}) copy-start(s32[16]{0:T(128)} %param.17) | copy-start | bytes 196
  57.8 6.5 %collective-permute-start.14 = (f32[16,2048]{1,0:T(8,128)S(1)}, f32[16,2048]{1,0:T(8,128)S(1)}, u32[]{:S(2)}, u32[]{:S(2)}) collective-permute-start(f32[16,2048]{1,0:T(8,128)S(1)} %constant_dynamic-update-slice_fusion), channel_id=1, source_target_pairs={{0,4},{4,0},{8,12},{12,8},{1,5},{5,1},{9,13},{13,9},{2,6},{6,2},{1... | collective-permute-start | bytes 393224 | tf_op jit(solution)/shard_map/ppermute | solution.py:207
  57.9 10.6 %collective-permute-start.15 = (f32[16,2048]{1,0:T(8,128)S(1)}, f32[16,2048]{1,0:T(8,128)S(1)}, u32[]{:S(2)}, u32[]{:S(2)}) collective-permute-start(f32[16,2048]{1,0:T(8,128)S(1)} %constant_dynamic-update-slice_fusion), channel_id=1, source_target_pairs={{0,8},{4,12},{8,0},{12,4},{1,9},{5,13},{9,1},{13,5},{2,10},{6,14},... | collective-permute-start | bytes 393224 | tf_op jit(solution)/shard_map/ppermute | solution.py:207
  58.6 9.9 %collective-permute-start.16 = (f32[16,2048]{1,0:T(8,128)S(1)}, f32[16,2048]{1,0:T(8,128)S(1)}, u32[]{:S(2)}, u32[]{:S(2)}) collective-permute-start(f32[16,2048]{1,0:T(8,128)S(1)} %constant_dynamic-update-slice_fusion), channel_id=1, source_target_pairs={{0,12},{4,8},{8,4},{12,0},{1,13},{5,9},{9,5},{13,1},{2,14},{6,10},... | collective-permute-start | bytes 393224 | tf_op jit(solution)/shard_map/ppermute | solution.py:207
  68.7 5.0 %collective-permute-start.17 = (f32[16,2048]{1,0:T(8,128)S(1)}, f32[16,2048]{1,0:T(8,128)S(1)}, u32[]{:S(2)}, u32[]{:S(2)}) collective-permute-start(f32[16,2048]{1,0:T(8,128)S(1)} %get-tuple-element.212), channel_id=1, source_target_pairs={{0,2},{2,0},{1,3},{3,1},{4,6},{6,4},{5,7},{7,5},{8,10},{10,8},{9,1... | collective-permute-start | bytes 393224 | tf_op jit(solution)/shard_map/ppermute | solution.py:207
  74.3 1.2 %collective-permute-start.18 = (f32[34,16]{0,1:T(8,128)S(1)}, f32[34,16]{0,1:T(8,128)S(1)}, u32[]{:S(2)}, u32[]{:S(2)}) collective-permute-start(f32[34,16]{0,1:T(8,128)S(1)} %pad_maximum_fusion), channel_id=1, source_target_pairs={{0,1},{1,0},{2,3},{3,2},{4,5},{5,4},{6,7},{7,6},{8,9},{9,8},{10,11... | collective-permute-start | bytes 6536 | tf_op jit(solution)/shard_map/ppermute | solution.py:207

commit v4 on v3

--- a/solution.py
+++ b/solution.py
@@ -14,7 +14,7 @@
 CHUNKS = 8
 DELAY = 3
 VMEM = 8 << 20
-BATCHES = (8,)
+BATCHES = (CHUNKS,)
 
 
 def dot(a, b, dims=((1,), (0,))):
@@ -43,18 +43,36 @@
     return found
 
 
-def prepare_kernel(
+def decay_kernel(raw_ref, rate_ref, e_ref, f_ref, last_ref, before_ref, total_ref):
+    tokens, heads = e_ref.shape
+    raw = raw_ref[...]
+    steps = (jnp.maximum(raw, 0.0) + jnp.log1p(jnp.exp(-jnp.abs(raw)))).T
+    logdecay = -rate_ref[...] * steps
+    row = lax.broadcasted_iota(jnp.int32, (SPAN, SPAN), 0)
+    col = lax.broadcasted_iota(jnp.int32, (SPAN, SPAN), 1)
+    lower = jnp.where(row >= col, 1.0, 0.0).astype(jnp.bfloat16)
+    so_far = jnp.zeros((1, heads), jnp.float32)
+    for b in range(tokens // SPAN):
+        rows = slice(b * SPAN, (b + 1) * SPAN)
+        parts = split3(logdecay[rows])
+        cum = dot(lower, parts[0]) + (dot(lower, parts[1]) + dot(lower, parts[2]))
+        e_ref[rows, :] = jnp.exp(cum)
+        f_ref[rows, :] = steps[rows] * jnp.exp(-cum)
+        whole = cum[SPAN - 1 :]
+        before_ref[b : b + 1, :] = jnp.exp(so_far)
+        so_far = so_far + whole
+        last_ref[b : b + 1, :] = jnp.exp(whole)
+    total_ref[...] = jnp.exp(so_far)
+
+
+def mask_kernel(
     lengths_ref,
     off_ref,
     b_ref,
     c_ref,
-    raw_ref,
-    rate_ref,
-    e_ref,
-    f_ref,
     last_ref,
+    total_ref,
     keep_ref,
-    before_ref,
     rates_ref,
     left_ref,
     tail_ref,
@@ -62,19 +80,14 @@
     member_ref,
     decay_ref,
 ):
-    tokens, heads = e_ref.shape
-    blocks = tokens // SPAN
+    docs, tokens = member_ref.shape
+    heads = last_ref.shape[1]
     off = off_ref[0]
-    docs = member_ref.shape[0]
     ends = [lengths_ref[0, 0]]
     for k in range(1, docs):
         ends.append(ends[-1] + lengths_ref[0, k])
-    raw = raw_ref[...]
-    steps = (jnp.maximum(raw, 0.0) + jnp.log1p(jnp.exp(-jnp.abs(raw)))).T
-    logdecay = -rate_ref[...] * steps
     row = lax.broadcasted_iota(jnp.int32, (SPAN, SPAN), 0)
     col = lax.broadcasted_iota(jnp.int32, (SPAN, SPAN), 1)
-    lower = jnp.where(row >= col, 1.0, 0.0).astype(jnp.bfloat16)
     places = lax.broadcasted_iota(jnp.int32, (1, tokens), 1) + off
     dend = jnp.full((1, tokens), 1 << 30, jnp.int32)
     docid = jnp.zeros((1, tokens), jnp.int32)
@@ -85,21 +98,12 @@
         (docid == lax.broadcasted_iota(jnp.int32, (docs, tokens), 0)).astype(jnp.float32).astype(jnp.bfloat16)
     )
     device_end = jnp.where(off > 0, first_end_from(ends, off), 0)
-    so_far = jnp.zeros((1, heads), jnp.float32)
-    for b in range(blocks):
+    for b in range(tokens // SPAN):
         rows = slice(b * SPAN, (b + 1) * SPAN)
-        parts = split3(logdecay[rows])
-        cum = dot(lower, parts[0]) + (dot(lower, parts[1]) + dot(lower, parts[2]))
-        e_ref[rows, :] = jnp.exp(cum)
-        f_ref[rows, :] = steps[rows] * jnp.exp(-cum)
-        whole = cum[SPAN - 1 :]
         start = off + b * SPAN
         last_start = last_end_until(ends, start + SPAN - 1)
         prior_end = jnp.where(start > 0, first_end_from(ends, start), 0)
-        before_ref[b : b + 1, :] = jnp.exp(so_far)
-        so_far = so_far + whole
-        last_ref[b : b + 1, :] = jnp.exp(whole)
-        keep_ref[b : b + 1, :] = jnp.exp(whole) * jnp.where(last_start < start, 1.0, 0.0)
+        keep_ref[b : b + 1, :] = last_ref[b : b + 1, :] * jnp.where(last_start < start, 1.0, 0.0)
         bb, cc = b_ref[rows, :], c_ref[rows, :]
         same = (row >= col) & (row + start < dend[:, rows])
         left_ref[rows, 0:SPAN] = jnp.where(same, dot(cc, bb, ((1,), (1,))), 0.0).astype(jnp.bfloat16)
@@ -112,7 +116,7 @@
         masked = jnp.where(place >= last_start, bb.astype(jnp.float32), 0.0)
         tail_ref[b * 128 : (b + 1) * 128, :] = masked.T.astype(jnp.bfloat16)
     through = jnp.where(last_end_until(ends, off + tokens - 1) < off, 1.0, 0.0)
-    decay_ref[...] = jnp.broadcast_to(jnp.exp(so_far) * through, (128, heads)).T
+    decay_ref[...] = jnp.broadcast_to(total_ref[...] * through, (128, heads)).T
     here = off // tokens
     per = heads // CHUNKS
     for r in range(rates_ref.shape[0] // per):
@@ -239,34 +243,37 @@
     cols = per * 128
     f32, bf16 = jnp.float32, jnp.bfloat16
     smem = pl.BlockSpec(memory_space=pltpu.SMEM)
-    whole = lambda *shape: pl.BlockSpec(shape, lambda *i: (0,) * len(shape))
     array = jax.ShapeDtypeStruct
     VM = pl.BlockSpec(memory_space=pltpu.VMEM)
     limit = pltpu.CompilerParams(vmem_limit_bytes=VMEM)
 
-    shapes = [
-        array((tokens, heads), f32),
-        array((tokens, heads), f32),
-        array((blocks, heads), f32),
-        array((blocks, heads), f32),
-        array((blocks, heads), f32),
-        array((rounds * per, 128), f32),
-        array((tokens, SPAN + 256), bf16),
-        array((blocks * 128, SPAN), bf16),
-        array((tokens, 128), bf16),
-        array((docs, tokens), bf16),
-    ]
-    e, f, last, keep, before, rates, left, tails, far, member = pl.pallas_call(
-        prepare_kernel,
-        grid=(1,),
-        in_specs=[smem, smem, whole(tokens, 128), whole(tokens, 128), whole(heads, tokens), whole(1, heads)],
-        out_specs=[whole(*s.shape) for s in shapes],
+    cost = pl.CostEstimate(flops=1 << 36, bytes_accessed=4 << 20, transcendentals=0)
+    e, f, last, before, decay = pl.pallas_call(
+        decay_kernel,
+        in_specs=[VM] * 2,
+        out_specs=[VM] * 5,
+        out_shape=[array((tokens, heads), f32)] * 2 + [array((blocks, heads), f32)] * 2 + [array((1, heads), f32)],
+        compiler_params=limit,
+        cost_estimate=cost,
+        name="decays",
+    )(step_raw[0], decay_rate.reshape(1, heads))
+    keep, rates, left, tails, far, member = pl.pallas_call(
+        mask_kernel,
+        in_specs=[smem, smem] + [VM] * 4,
+        out_specs=[VM] * 6,
+        out_shape=[
+            array((blocks, heads), f32),
+            array((rounds * per, 128), f32),
+            array((tokens, SPAN + 256), bf16),
+            array((blocks * 128, SPAN), bf16),
+            array((tokens, 128), bf16),
+            array((docs, tokens), bf16),
+        ],
         scratch_shapes=[pltpu.VMEM((heads, 128), f32)],
-        out_shape=shapes,
         compiler_params=limit,
-        cost_estimate=pl.CostEstimate(flops=1 << 36, bytes_accessed=4 << 20, transcendentals=0),
-        name="prepare",
-    )(doc_lengths, off, input_proj[0], output_proj[0], step_raw[0], decay_rate.reshape(1, heads))
+        cost_estimate=cost,
+        name="masks",
+    )(doc_lengths, off, input_proj[0], output_proj[0], last, decay)
 
     def local(c, last):
         return pl.pallas_call(
@@ -342,15 +349,10 @@
 
     def gather(low, high):
         totals = jnp.concatenate(sums[low:high], axis=1)
-        if count <= 4:
-            parts = [swapped(totals, "ctx", j) for j in range(1, count)]
-            for part in parts:
-                totals = totals + part
-        else:
-            reach = 1
-            while reach < count:
-                totals = totals + swapped(totals, "ctx", reach)
-                reach *= 2
+        reach = 1
+        while reach < count:
+            totals = totals + swapped(totals, "ctx", reach)
+            reach *= 2
         mean = totals / spread
         every = [mean] + [swapped(mean, "dp", j) for j in range(1, lax.axis_size("dp"))]
         part = [jnp.dot(mean, one.T, precision=HIGH) for one in every]
@@ -361,7 +363,7 @@
     low = 0
     for high in BATCHES:
         for c in range(len(sums), high):
-            mixed, part = finish(c, arrived(c, *sums[-1:]), mixed)
+            mixed, part = finish(c, arrived(c, sent, *sums[-1:]), mixed)
             sums.append(part)
         gather(low, high)
         low = high

time: 77.4 us -> 75 us (0.969)
  starting transfers between devices: 14.8 us -> 12.8 us
  local copies, waits for them, and re-layouts: 6.18 us -> 4.47 us
  waiting for transfers between devices: 31.7 us -> 32.8 us
    ppermute x5 -> x4, waiting for transfers between devices: 10.5 us -> 15.5 us  [swapped(): lax.ppermute(value, axis, [(i, i ^ by) for i in range(lax.axis_size(axis))])]
    ppermute x14, waiting for transfers between devices: 21.1 us -> 17.3 us  [on_device(): got.append(lax.ppermute(sent, 'ctx', pairs))]
    ppermute x5 -> x4, starting transfers between devices: 6.02 us -> 2.37 us  [swapped(): lax.ppermute(value, axis, [(i, i ^ by) for i in range(lax.axis_size(axis))])]
    unnamed x27 -> x25, local copies, waits for them, and re-layouts: 6 us -> 4.29 us
    ppermute x14, starting transfers between devices: 8.79 us -> 10.4 us  [on_device(): got.append(lax.ppermute(sent, 'ctx', pairs))]
    pallas_call x1 -> x2, Pallas kernels: 1.55 us -> 1.71 us  [the longest x1 1.02 us: on_device(): pl.pallas_call(mask_kernel, in_specs=[smem, smem] + [VM] * 4, out_specs=[...]
  transfers between devices with their start and end apart: 19 -> 18, of which waited for: 17 -> 17; matrix products, arithmetic and copies ran while one was open for 1% -> 1% of each run, Pallas kernels for 21% -> 22%
where the time goes in v4:
time: 75 us; the launch traced here: 74.8 us
  waiting for transfers between devices  32.8 us (44%)
  Pallas kernels  20.6 us (27%)
  starting transfers between devices  12.8 us (17%)
  local copies, waits for them, and re-layouts  4.47 us (6%)
  other arithmetic  2.78 us (4%)
  between operations  0.99 us (1%)
    ppermute x14, waiting for transfers between devices, on_device(): got.append(lax.ppermute(sent, 'ctx', pairs))  17.3 us
    ppermute x4, waiting for transfers between devices, swapped(): lax.ppermute(value, axis, [(i, i ^ by) for i in range(lax.axis_size(axis))])  15.5 us
    pallas_call x8, Pallas kernels, finish(): pl.pallas_call(functools.partial(finish_kernel, c * cols), in_specs=specs...  10.4 us
    ppermute x14, starting transfers between devices, on_device(): got.append(lax.ppermute(sent, 'ctx', pairs))  10.4 us
    pallas_call x8, Pallas kernels, local(): pl.pallas_call(functools.partial(local_kernel, c * cols), in_specs=[VM] *...  8.46 us
    unnamed x25, local copies, waits for them, and re-layouts  4.29 us
    ppermute x4, starting transfers between devices, swapped(): lax.ppermute(value, axis, [(i, i ^ by) for i in range(lax.axis_size(axis))])  2.37 us
  transfers between devices with their start and end apart: 18, of which 17 were waited for; matrix products, arithmetic and copies ran while one was open for 1% of the time, Pallas kernels for 22%

profile of v4, /device:TPU:0, one launch (start us, length us, event | category | flops | bytes accessed | tf_op | source)
XLA Modules:
  0.0 74.8 jit_solution(4948485146159467889)
XLA Ops:
  0.7 0.8 %copy-done.5 = f32[1,16,1024]{2,1,0:T(8,128)S(1)} copy-done((f32[1,16,1024]{2,1,0:T(8,128)S(1)}, f32[1,16,1024]{2,1,0:T(8,128)}, u32[]{:S(2)}) %copy-start.5) | copy-done | bytes 65560
  1.5 0.7 copy-done.6
  2.2 0.7 decays.1
  2.8 0.2 copy-done.3
  3.1 0.1 copy-done.4
  3.2 1.0 %masks.1 = (f32[4,16]{1,0:T(4,128)S(1)}, f32[28,128]{1,0:T(8,128)S(1)}, bf16[1024,512]{1,0:T(8,128)(2,1)S(1)}, bf16[512,256]{1,0:T(8,128)(2,1)S(1)}, bf16[1024,1...) custom-call(s32[1,16]{1,0:T(1,128)S(1)} %copy-done.7, s32[1]{0:T(128)} %bitcast.4.off_ref, ...), custom_call_target="tpu_custom_call" | custom-call | flops 68719476736 | bytes 4194304 | tf_op jit(solution)/shard_map/masks/pallas_call | solution.py:260
  4.2 1.2 %copy-done = bf16[1,1024,2048]{2,1,0:T(8,128)(2,1)S(1)} copy-done((bf16[1,1024,2048]{2,1,0:T(8,128)(2,1)S(1)}, bf16[1,1024,2048]{2,1,0:T(8,128)(2,1)}, u32[]{:S(2)}) %copy-start) | copy-done | bytes 4194328
  5.4 1.3 %copy-done.1 = bf16[1,1024,2048]{2,1,0:T(8,128)(2,1)S(1)} copy-done((bf16[1,1024,2048]{2,1,0:T(8,128)(2,1)S(1)}, bf16[1,1024,2048]{2,1,0:T(8,128)(2,1)}, u32[]{:S(2)}) %copy-start.1) | copy-done | bytes 4194328
  6.6 1.1 %local0.1 = (f32[1024,256]{1,0:T(8,128)S(1)}, bf16[1024,256]{1,0:T(8,128)(2,1)S(1)}, f32[2,128,128]{2,1,0:T(8,128)S(1)}) custom-call(bf16[1024,2048]{1,0:T(8,128)(2,1)S(1)} %bitcast.17, bf16[1024,2048]{1,0:T(8,128)(2,1)S(1)} %bitcast.25, f32[1024,16]{1,0:T(8,128)S(1)} %get-tuple-element.105.e_ref, f32[1024,16]{1,0:T(8,128)S(1)} %get-tuple-element.106.f_ref, ...), custom_call_target="tpu_custom_call" | custom-call | flops 1048576 | bytes 65536 | tf_op jit(solution)/shard_map/local0/pallas_call | solution.py:279
  7.7 3.1 %collective-permute-start = (f32[2,128,128]{2,1,0:T(8,128)S(1)}, f32[2,128,128]{2,1,0:T(8,128)S(1)}, u32[]{:S(2)}, u32[]{:S(2)}) collective-permute-start(f32[2,128,128]{2,1,0:T(8,128)S(1)} %get-tuple-element.115), channel_id=1, source_target_pairs={{0,4},{4,8},{8,12},{12,0},{1,5},{5,9},{9,13},{13,1},{2,6},{6,10},{... | collective-permute-start | bytes 393224 | tf_op jit(solution)/shard_map/ppermute | solution.py:346
  10.8 1.1 %local1.1 = (f32[1024,256]{1,0:T(8,128)S(1)}, bf16[1024,256]{1,0:T(8,128)(2,1)S(1)}, f32[2,128,128]{2,1,0:T(8,128)S(1)}) custom-call(bf16[1024,2048]{1,0:T(8,128)(2,1)S(1)} %bitcast.18, bf16[1024,2048]{1,0:T(8,128)(2,1)S(1)} %bitcast.26, f32[1024,16]{1,0:T(8,128)S(1)} %get-tuple-element.105.e_ref, f32[1024,16]{1,0:T(8,128)S(1)} %get-tuple-element.106.f_ref, ...), custom_call_target="tpu_custom_call" | custom-call | flops 1048576 | bytes 65536 | tf_op jit(solution)/shard_map/local1/pallas_call | solution.py:279
  11.9 1.6 %collective-permute-start.1 = (f32[2,128,128]{2,1,0:T(8,128)S(1)}, f32[2,128,128]{2,1,0:T(8,128)S(1)}, u32[]{:S(2)}, u32[]{:S(2)}) collective-permute-start(f32[2,128,128]{2,1,0:T(8,128)S(1)} %get-tuple-element.119), channel_id=1, source_target_pairs={{0,4},{4,8},{8,12},{12,0},{1,5},{5,9},{9,13},{13,1},{2,6},{6,10},{... | collective-permute-start | bytes 393224 | tf_op jit(solution)/shard_map/ppermute | solution.py:346
  13.5 1.1 %local2.1 = (f32[1024,256]{1,0:T(8,128)S(1)}, bf16[1024,256]{1,0:T(8,128)(2,1)S(1)}, f32[2,128,128]{2,1,0:T(8,128)S(1)}) custom-call(bf16[1024,2048]{1,0:T(8,128)(2,1)S(1)} %bitcast.19, bf16[1024,2048]{1,0:T(8,128)(2,1)S(1)} %bitcast.27, f32[1024,16]{1,0:T(8,128)S(1)} %get-tuple-element.105.e_ref, f32[1024,16]{1,0:T(8,128)S(1)} %get-tuple-element.106.f_ref, ...), custom_call_target="tpu_custom_call" | custom-call | flops 1048576 | bytes 65536 | tf_op jit(solution)/shard_map/local2/pallas_call | solution.py:279
  14.5 1.6 %collective-permute-start.2 = (f32[2,128,128]{2,1,0:T(8,128)S(1)}, f32[2,128,128]{2,1,0:T(8,128)S(1)}, u32[]{:S(2)}, u32[]{:S(2)}) collective-permute-start(f32[2,128,128]{2,1,0:T(8,128)S(1)} %get-tuple-element.122), channel_id=1, source_target_pairs={{0,4},{4,8},{8,12},{12,0},{1,5},{5,9},{9,13},{13,1},{2,6},{6,10},{... | collective-permute-start | bytes 393224 | tf_op jit(solution)/shard_map/ppermute | solution.py:346
  16.2 1.1 %local3.1 = (f32[1024,256]{1,0:T(8,128)S(1)}, bf16[1024,256]{1,0:T(8,128)(2,1)S(1)}, f32[2,128,128]{2,1,0:T(8,128)S(1)}) custom-call(bf16[1024,2048]{1,0:T(8,128)(2,1)S(1)} %bitcast.20, bf16[1024,2048]{1,0:T(8,128)(2,1)S(1)} %bitcast.28, f32[1024,16]{1,0:T(8,128)S(1)} %get-tuple-element.105.e_ref, f32[1024,16]{1,0:T(8,128)S(1)} %get-tuple-element.106.f_ref, ...), custom_call_target="tpu_custom_call" | custom-call | flops 1048576 | bytes 65536 | tf_op jit(solution)/shard_map/local3/pallas_call | solution.py:279
  17.4 1.1 %local4.1 = (f32[1024,256]{1,0:T(8,128)S(1)}, bf16[1024,256]{1,0:T(8,128)(2,1)S(1)}, f32[2,128,128]{2,1,0:T(8,128)S(1)}) custom-call(bf16[1024,2048]{1,0:T(8,128)(2,1)S(1)} %bitcast.21, bf16[1024,2048]{1,0:T(8,128)(2,1)S(1)} %bitcast.29, f32[1024,16]{1,0:T(8,128)S(1)} %get-tuple-element.105.e_ref, f32[1024,16]{1,0:T(8,128)S(1)} %get-tuple-element.106.f_ref, ...), custom_call_target="tpu_custom_call" | custom-call | flops 1048576 | bytes 65536 | tf_op jit(solution)/shard_map/local4/pallas_call | solution.py:279
  18.4 1.5 %collective-permute-done.1 = f32[2,128,128]{2,1,0:T(8,128)S(1)} collective-permute-done((f32[2,128,128]{2,1,0:T(8,128)S(1)}, f32[2,128,128]{2,1,0:T(8,128)S(1)}, u32[]{:S(2)}, u32[]{:S(2)}) %collective-permute-start.1) | collective-permute-done | bytes 131104 | tf_op jit(solution)/shard_map/ppermute | solution.py:346
  20.0 0.3 collective-permute-start.4
  20.3 1.1 %local5.1 = (f32[1024,256]{1,0:T(8,128)S(1)}, bf16[1024,256]{1,0:T(8,128)(2,1)S(1)}, f32[2,128,128]{2,1,0:T(8,128)S(1)}) custom-call(bf16[1024,2048]{1,0:T(8,128)(2,1)S(1)} %bitcast.22, bf16[1024,2048]{1,0:T(8,128)(2,1)S(1)} %bitcast.30, f32[1024,16]{1,0:T(8,128)S(1)} %get-tuple-element.105.e_ref, f32[1024,16]{1,0:T(8,128)S(1)} %get-tuple-element.106.f_ref, ...), custom_call_target="tpu_custom_call" | custom-call | flops 1048576 | bytes 65536 | tf_op jit(solution)/shard_map/local5/pallas_call | solution.py:279
  21.4 1.4 %collective-permute-done.2 = f32[2,128,128]{2,1,0:T(8,128)S(1)} collective-permute-done((f32[2,128,128]{2,1,0:T(8,128)S(1)}, f32[2,128,128]{2,1,0:T(8,128)S(1)}, u32[]{:S(2)}, u32[]{:S(2)}) %collective-permute-start.2) | collective-permute-done | bytes 131104 | tf_op jit(solution)/shard_map/ppermute | solution.py:346
  22.8 0.2 collective-permute-start.7
  23.1 1.1 %local6.1 = (f32[1024,256]{1,0:T(8,128)S(1)}, bf16[1024,256]{1,0:T(8,128)(2,1)S(1)}, f32[2,128,128]{2,1,0:T(8,128)S(1)}) custom-call(bf16[1024,2048]{1,0:T(8,128)(2,1)S(1)} %bitcast.23, bf16[1024,2048]{1,0:T(8,128)(2,1)S(1)} %bitcast.31, f32[1024,16]{1,0:T(8,128)S(1)} %get-tuple-element.105.e_ref, f32[1024,16]{1,0:T(8,128)S(1)} %get-tuple-element.106.f_ref, ...), custom_call_target="tpu_custom_call" | custom-call | flops 1048576 | bytes 65536 | tf_op jit(solution)/shard_map/local6/pallas_call | solution.py:279
  24.1 1.5 %collective-permute-done.3 = f32[2,128,128]{2,1,0:T(8,128)S(1)} collective-permute-done((f32[2,128,128]{2,1,0:T(8,128)S(1)}, f32[2,128,128]{2,1,0:T(8,128)S(1)}, u32[]{:S(2)}, u32[]{:S(2)}) %collective-permute-start.3) | collective-permute-done | bytes 131104 | tf_op jit(solution)/shard_map/ppermute | solution.py:346
  25.6 0.2 collective-permute-start.6
  25.8 1.1 %local7.1 = (f32[1024,256]{1,0:T(8,128)S(1)}, bf16[1024,256]{1,0:T(8,128)(2,1)S(1)}, f32[2,128,128]{2,1,0:T(8,128)S(1)}) custom-call(bf16[1024,2048]{1,0:T(8,128)(2,1)S(1)} %bitcast.24, bf16[1024,2048]{1,0:T(8,128)(2,1)S(1)} %bitcast.32, f32[1024,16]{1,0:T(8,128)S(1)} %get-tuple-element.105.e_ref, f32[1024,16]{1,0:T(8,128)S(1)} %get-tuple-element.106.f_ref, ...), custom_call_target="tpu_custom_call" | custom-call | flops 1048576 | bytes 65536 | tf_op jit(solution)/shard_map/local7/pallas_call | solution.py:279
  26.9 1.5 %collective-permute-done.4 = f32[2,128,128]{2,1,0:T(8,128)S(1)} collective-permute-done((f32[2,128,128]{2,1,0:T(8,128)S(1)}, f32[2,128,128]{2,1,0:T(8,128)S(1)}, u32[]{:S(2)}, u32[]{:S(2)}) %collective-permute-start.4) | collective-permute-done | bytes 131104 | tf_op jit(solution)/shard_map/ppermute | solution.py:346
  28.5 2.7 %collective-permute-done.7 = f32[2,128,128]{2,1,0:T(8,128)S(1)} collective-permute-done((f32[2,128,128]{2,1,0:T(8,128)S(1)}, f32[2,128,128]{2,1,0:T(8,128)S(1)}, u32[]{:S(2)}, u32[]{:S(2)}) %collective-permute-start.7) | collective-permute-done | bytes 131104 | tf_op jit(solution)/shard_map/ppermute | solution.py:346
  31.3 2.7 %collective-permute-done.6 = f32[2,128,128]{2,1,0:T(8,128)S(1)} collective-permute-done((f32[2,128,128]{2,1,0:T(8,128)S(1)}, f32[2,128,128]{2,1,0:T(8,128)S(1)}, u32[]{:S(2)}, u32[]{:S(2)}) %collective-permute-start.6) | collective-permute-done | bytes 131104 | tf_op jit(solution)/shard_map/ppermute | solution.py:346
  34.2 1.3 %finish0.1 = (bf16[1024,2048]{1,0:T(8,128)(2,1)}, f32[16,256]{1,0:T(8,128)S(1)}) custom-call(f32[1024,256]{1,0:T(8,128)S(1)} %get-tuple-element.146.local_ref, bf16[1024,256]{1,0:T(8,128)(2,1)S(1)} %get-tuple-element.147.gate_ref, bf16[1024,128]{1,0:T(8,128)(2,1)S(1)} %get-tuple-element.140.far_ref, f32[2,128,128]{2,1,0:T(8,128)S(1)} %select_select_fusion.7.in_ref, ...), custom_call_target="tpu_custom_call" | custom-call | flops 1048576 | bytes 65536 | tf_op jit(solution)/shard_map/finish0/pallas_call | solution.py:297
  35.5 1.3 %collective-permute-done.5 = f32[2,128,128]{2,1,0:T(8,128)S(1)} collective-permute-done((f32[2,128,128]{2,1,0:T(8,128)S(1)}, f32[2,128,128]{2,1,0:T(8,128)S(1)}, u32[]{:S(2)}, u32[]{:S(2)}) %collective-permute-start.5) | collective-permute-done | bytes 131104 | tf_op jit(solution)/shard_map/ppermute | solution.py:346
  36.9 0.2 collective-permute-start.8
  37.1 1.3 %finish1.1 = (bf16[1024,2048]{1,0:T(8,128)(2,1)}, f32[16,256]{1,0:T(8,128)S(1)}) custom-call(f32[1024,256]{1,0:T(8,128)S(1)} %get-tuple-element.154.local_ref, bf16[1024,256]{1,0:T(8,128)(2,1)S(1)} %get-tuple-element.155.gate_ref, bf16[1024,128]{1,0:T(8,128)(2,1)S(1)} %get-tuple-element.140.far_ref, ...), custom_call_target="tpu_custom_call", output_to_operand_aliasing={{0}: (6, {})} | custom-call | flops 1048576 | bytes 65536 | tf_op jit(solution)/shard_map/finish1/pallas_call | solution.py:297
  38.4 1.2 %collective-permute-done.10 = f32[2,128,128]{2,1,0:T(8,128)S(1)} collective-permute-done((f32[2,128,128]{2,1,0:T(8,128)S(1)}, f32[2,128,128]{2,1,0:T(8,128)S(1)}, u32[]{:S(2)}, u32[]{:S(2)}) %collective-permute-start.10) | collective-permute-done | bytes 131104 | tf_op jit(solution)/shard_map/ppermute | solution.py:346
  39.7 0.5 collective-permute-start.13
  40.2 1.3 %finish2.1 = (bf16[1024,2048]{1,0:T(8,128)(2,1)}, f32[16,256]{1,0:T(8,128)S(1)}) custom-call(f32[1024,256]{1,0:T(8,128)S(1)} %get-tuple-element.162.local_ref, bf16[1024,256]{1,0:T(8,128)(2,1)S(1)} %get-tuple-element.163.gate_ref, bf16[1024,128]{1,0:T(8,128)(2,1)S(1)} %get-tuple-element.140.far_ref, ...), custom_call_target="tpu_custom_call", output_to_operand_aliasing={{0}: (6, {})} | custom-call | flops 1048576 | bytes 65536 | tf_op jit(solution)/shard_map/finish2/pallas_call | solution.py:297
  41.5 0.9 %collective-permute-done.9 = f32[2,128,128]{2,1,0:T(8,128)S(1)} collective-permute-done((f32[2,128,128]{2,1,0:T(8,128)S(1)}, f32[2,128,128]{2,1,0:T(8,128)S(1)}, u32[]{:S(2)}, u32[]{:S(2)}) %collective-permute-start.9) | collective-permute-done | bytes 131104 | tf_op jit(solution)/shard_map/ppermute | solution.py:346
  42.5 1.2 %collective-permute-start.12 = (f32[2,128,128]{2,1,0:T(8,128)S(1)}, f32[2,128,128]{2,1,0:T(8,128)S(1)}, u32[]{:S(2)}, u32[]{:S(2)}) collective-permute-start(f32[2,128,128]{2,1,0:T(8,128)S(1)} %multiply_add_fusion.1), channel_id=1, source_target_pairs={{0,4},{4,8},{8,12},{12,0},{1,5},{5,9},{9,13},{13,1},{2,6},{6,10},{... | collective-permute-start | bytes 393224 | tf_op jit(solution)/shard_map/ppermute | solution.py:346
  43.7 1.3 %finish3.1 = (bf16[1024,2048]{1,0:T(8,128)(2,1)}, f32[16,256]{1,0:T(8,128)S(1)}) custom-call(f32[1024,256]{1,0:T(8,128)S(1)} %get-tuple-element.170.local_ref, bf16[1024,256]{1,0:T(8,128)(2,1)S(1)} %get-tuple-element.171.gate_ref, bf16[1024,128]{1,0:T(8,128)(2,1)S(1)} %get-tuple-element.140.far_ref, ...), custom_call_target="tpu_custom_call", output_to_operand_aliasing={{0}: (6, {})} | custom-call | flops 1048576 | bytes 65536 | tf_op jit(solution)/shard_map/finish3/pallas_call | solution.py:297
  45.0 0.3 collective-permute-done.8
  45.3 1.1 %collective-permute-start.11 = (f32[2,128,128]{2,1,0:T(8,128)S(1)}, f32[2,128,128]{2,1,0:T(8,128)S(1)}, u32[]{:S(2)}, u32[]{:S(2)}) collective-permute-start(f32[2,128,128]{2,1,0:T(8,128)S(1)} %multiply_add_fusion), channel_id=1, source_target_pairs={{0,4},{4,8},{8,12},{12,0},{1,5},{5,9},{9,13},{13,1},{2,6},{6,10},{... | collective-permute-start | bytes 393224 | tf_op jit(solution)/shard_map/ppermute | solution.py:346
  46.4 1.3 %finish4.1 = (bf16[1024,2048]{1,0:T(8,128)(2,1)}, f32[16,256]{1,0:T(8,128)S(1)}) custom-call(f32[1024,256]{1,0:T(8,128)S(1)} %get-tuple-element.182.local_ref, bf16[1024,256]{1,0:T(8,128)(2,1)S(1)} %get-tuple-element.183.gate_ref, bf16[1024,128]{1,0:T(8,128)(2,1)S(1)} %get-tuple-element.140.far_ref, ...), custom_call_target="tpu_custom_call", output_to_operand_aliasing={{0}: (6, {})} | custom-call | flops 1048576 | bytes 65536 | tf_op jit(solution)/shard_map/finish4/pallas_call | solution.py:297
  47.8 0.3 collective-permute-done.13
  48.1 1.3 %finish5.1 = (bf16[1024,2048]{1,0:T(8,128)(2,1)}, f32[16,256]{1,0:T(8,128)S(1)}) custom-call(f32[1024,256]{1,0:T(8,128)S(1)} %get-tuple-element.180.local_ref, bf16[1024,256]{1,0:T(8,128)(2,1)S(1)} %get-tuple-element.181.gate_ref, bf16[1024,128]{1,0:T(8,128)(2,1)S(1)} %get-tuple-element.140.far_ref, ...), custom_call_target="tpu_custom_call", output_to_operand_aliasing={{0}: (6, {})} | custom-call | flops 1048576 | bytes 65536 | tf_op jit(solution)/shard_map/finish5/pallas_call | solution.py:297
  49.4 1.5 %collective-permute-done.12 = f32[2,128,128]{2,1,0:T(8,128)S(1)} collective-permute-done((f32[2,128,128]{2,1,0:T(8,128)S(1)}, f32[2,128,128]{2,1,0:T(8,128)S(1)}, u32[]{:S(2)}, u32[]{:S(2)}) %collective-permute-start.12) | collective-permute-done | bytes 131104 | tf_op jit(solution)/shard_map/ppermute | solution.py:346
  51.0 1.3 %finish6.1 = (bf16[1024,2048]{1,0:T(8,128)(2,1)}, f32[16,256]{1,0:T(8,128)S(1)}) custom-call(f32[1024,256]{1,0:T(8,128)S(1)} %get-tuple-element.178.local_ref, bf16[1024,256]{1,0:T(8,128)(2,1)S(1)} %get-tuple-element.179.gate_ref, bf16[1024,128]{1,0:T(8,128)(2,1)S(1)} %get-tuple-element.140.far_ref, ...), custom_call_target="tpu_custom_call", output_to_operand_aliasing={{0}: (6, {})} | custom-call | flops 1048576 | bytes 65536 | tf_op jit(solution)/shard_map/finish6/pallas_call | solution.py:297
  52.3 0.5 collective-permute-done.11
  52.9 1.3 %finish7.1 = (bf16[1024,2048]{1,0:T(8,128)(2,1)}, f32[16,256]{1,0:T(8,128)S(1)}) custom-call(f32[1024,256]{1,0:T(8,128)S(1)} %get-tuple-element.138.local_ref, bf16[1024,256]{1,0:T(8,128)(2,1)S(1)} %get-tuple-element.139.gate_ref, bf16[1024,128]{1,0:T(8,128)(2,1)S(1)} %get-tuple-element.140.far_ref, ...), custom_call_target="tpu_custom_call", output_to_operand_aliasing={{0}: (6, {})} | custom-call | flops 1048576 | bytes 65536 | tf_op jit(solution)/shard_map/finish7/pallas_call | solution.py:297
  54.3 5.0 %collective-permute-done.14 = f32[16,2048]{1,0:T(8,128)S(1)} collective-permute-done((f32[16,2048]{1,0:T(8,128)S(1)}, f32[16,2048]{1,0:T(8,128)S(1)}, u32[]{:S(2)}, u32[]{:S(2)}) %collective-permute-start.14) | collective-permute-done | bytes 131104 | tf_op jit(solution)/shard_map/ppermute | solution.py:211
  59.2 0.8 %collective-permute-start.15 = (f32[16,2048]{1,0:T(8,128)S(1)}, f32[16,2048]{1,0:T(8,128)S(1)}, u32[]{:S(2)}, u32[]{:S(2)}) collective-permute-start(f32[16,2048]{1,0:T(8,128)S(1)} %add.101), channel_id=1, source_target_pairs={{0,8},{4,12},{8,0},{12,4},{1,9},{5,13},{9,1},{13,5},{2,10},{6,14},... | collective-permute-start | bytes 393224 | tf_op jit(solution)/shard_map/ppermute | solution.py:211
  60.0 6.1 %collective-permute-done.15 = f32[16,2048]{1,0:T(8,128)S(1)} collective-permute-done((f32[16,2048]{1,0:T(8,128)S(1)}, f32[16,2048]{1,0:T(8,128)S(1)}, u32[]{:S(2)}, u32[]{:S(2)}) %collective-permute-start.15) | collective-permute-done | bytes 131104 | tf_op jit(solution)/shard_map/ppermute | solution.py:211
  66.2 0.2 multiply_reduce_fusion.1
  66.4 1.5 %collective-permute-start.16 = (f32[16,2048]{1,0:T(8,128)S(1)}, f32[16,2048]{1,0:T(8,128)S(1)}, u32[]{:S(2)}, u32[]{:S(2)}) collective-permute-start(f32[16,2048]{1,0:T(8,128)S(1)} %get-tuple-element.214), channel_id=1, source_target_pairs={{0,2},{2,0},{1,3},{3,1},{4,6},{6,4},{5,7},{7,5},{8,10},{10,8},{9,1... | collective-permute-start | bytes 393224 | tf_op jit(solution)/shard_map/ppermute | solution.py:211
  67.9 0.1 copy.21
  67.9 0.2 fusion.11
  68.2 3.2 %collective-permute-done.16 = f32[16,2048]{1,0:T(8,128)S(1)} collective-permute-done((f32[16,2048]{1,0:T(8,128)S(1)}, f32[16,2048]{1,0:T(8,128)S(1)}, u32[]{:S(2)}, u32[]{:S(2)}) %collective-permute-start.16) | collective-permute-done | bytes 131104 | tf_op jit(solution)/shard_map/ppermute | solution.py:211
  71.4 0.1 multiply_reduce_fusion
  71.5 0.1 copy.22
  71.6 0.2 fusion.12
  71.8 0.1 pad_maximum_fusion
  72.0 1.1 %collective-permute-done.17 = f32[34,16]{0,1:T(8,128)S(1)} collective-permute-done((f32[34,16]{0,1:T(8,128)S(1)}, f32[34,16]{0,1:T(8,128)S(1)}, u32[]{:S(2)}, u32[]{:S(2)}) %collective-permute-start.17) | collective-permute-done | bytes 2208 | tf_op jit(solution)/shard_map/ppermute | solution.py:211
  73.2 0.2 fusion.2
  73.4 0.7 broadcast_multiply_fusion
  74.2 0.1 select_reduce_fusion.2
  74.3 0.5 add_subtract_fusion
  (51 shorter events, 1.2 us)
Async XLA Ops:
  0.6 0.8 %copy-start.5 = (f32[1,16,1024]{2,1,0:T(8,128)S(1)}, f32[1,16,1024]{2,1,0:T(8,128)}, u32[]{:S(2)}) copy-start(f32[1,16,1024]{2,1,0:T(8,128)} %param.13) | copy-start | bytes 196612
  1.5 0.7 copy-start.6
  2.1 0.9 %copy-start.3 = (bf16[1,1024,128]{2,1,0:T(8,128)(2,1)S(1)}, bf16[1,1024,128]{2,1,0:T(8,128)(2,1)}, u32[]{:S(2)}) copy-start(bf16[1,1024,128]{2,1,0:T(8,128)(2,1)} %param.11) | copy-start | bytes 786436
  2.1 1.0 %copy-start.4 = (bf16[1,1024,128]{2,1,0:T(8,128)(2,1)S(1)}, bf16[1,1024,128]{2,1,0:T(8,128)(2,1)}, u32[]{:S(2)}) copy-start(bf16[1,1024,128]{2,1,0:T(8,128)(2,1)} %param.12) | copy-start | bytes 786436
  2.1 1.0 %copy-start.7 = (s32[1,16]{1,0:T(1,128)S(1)}, s32[1,16]{1,0:T(1,128)}, u32[]{:S(2)}) copy-start(s32[1,16]{1,0:T(1,128)} %lengths_ref.1) | copy-start | bytes 196
  3.2 2.2 %copy-start = (bf16[1,1024,2048]{2,1,0:T(8,128)(2,1)S(1)}, bf16[1,1024,2048]{2,1,0:T(8,128)(2,1)}, u32[]{:S(2)}) copy-start(bf16[1,1024,2048]{2,1,0:T(8,128)(2,1)} %param.9) | copy-start | bytes 12582916
  3.2 3.5 %copy-start.1 = (bf16[1,1024,2048]{2,1,0:T(8,128)(2,1)S(1)}, bf16[1,1024,2048]{2,1,0:T(8,128)(2,1)}, u32[]{:S(2)}) copy-start(bf16[1,1024,2048]{2,1,0:T(8,128)(2,1)} %param.10) | copy-start | bytes 12582916
  7.7 9.5 %collective-permute-start = (f32[2,128,128]{2,1,0:T(8,128)S(1)}, f32[2,128,128]{2,1,0:T(8,128)S(1)}, u32[]{:S(2)}, u32[]{:S(2)}) collective-permute-start(f32[2,128,128]{2,1,0:T(8,128)S(1)} %get-tuple-element.115), channel_id=1, source_target_pairs={{0,4},{4,8},{8,12},{12,0},{1,5},{5,9},{9,13},{13,1},{2,6},{6,10},{... | collective-permute-start | bytes 393224 | tf_op jit(solution)/shard_map/ppermute | solution.py:346
  11.9 8.1 %collective-permute-start.1 = (f32[2,128,128]{2,1,0:T(8,128)S(1)}, f32[2,128,128]{2,1,0:T(8,128)S(1)}, u32[]{:S(2)}, u32[]{:S(2)}) collective-permute-start(f32[2,128,128]{2,1,0:T(8,128)S(1)} %get-tuple-element.119), channel_id=1, source_target_pairs={{0,4},{4,8},{8,12},{12,0},{1,5},{5,9},{9,13},{13,1},{2,6},{6,10},{... | collective-permute-start | bytes 393224 | tf_op jit(solution)/shard_map/ppermute | solution.py:346
  14.5 8.2 %collective-permute-start.2 = (f32[2,128,128]{2,1,0:T(8,128)S(1)}, f32[2,128,128]{2,1,0:T(8,128)S(1)}, u32[]{:S(2)}, u32[]{:S(2)}) collective-permute-start(f32[2,128,128]{2,1,0:T(8,128)S(1)} %get-tuple-element.122), channel_id=1, source_target_pairs={{0,4},{4,8},{8,12},{12,0},{1,5},{5,9},{9,13},{13,1},{2,6},{6,10},{... | collective-permute-start | bytes 393224 | tf_op jit(solution)/shard_map/ppermute | solution.py:346
  17.3 8.3 %collective-permute-start.3 = (f32[2,128,128]{2,1,0:T(8,128)S(1)}, f32[2,128,128]{2,1,0:T(8,128)S(1)}, u32[]{:S(2)}, u32[]{:S(2)}) collective-permute-start(f32[2,128,128]{2,1,0:T(8,128)S(1)} %multiply_add_fusion.10), channel_id=1, source_target_pairs={{0,4},{4,8},{8,12},{12,0},{1,5},{5,9},{9,13},{13,1},{2,6},{6,10},{... | collective-permute-start | bytes 393224 | tf_op jit(solution)/shard_map/ppermute | solution.py:346
  20.0 8.4 %collective-permute-start.4 = (f32[2,128,128]{2,1,0:T(8,128)S(1)}, f32[2,128,128]{2,1,0:T(8,128)S(1)}, u32[]{:S(2)}, u32[]{:S(2)}) collective-permute-start(f32[2,128,128]{2,1,0:T(8,128)S(1)} %multiply_add_fusion.9), channel_id=1, source_target_pairs={{0,4},{4,8},{8,12},{12,0},{1,5},{5,9},{9,13},{13,1},{2,6},{6,10},{... | collective-permute-start | bytes 393224 | tf_op jit(solution)/shard_map/ppermute | solution.py:346
  22.8 8.4 %collective-permute-start.7 = (f32[2,128,128]{2,1,0:T(8,128)S(1)}, f32[2,128,128]{2,1,0:T(8,128)S(1)}, u32[]{:S(2)}, u32[]{:S(2)}) collective-permute-start(f32[2,128,128]{2,1,0:T(8,128)S(1)} %multiply_add_fusion.8), channel_id=1, source_target_pairs={{0,4},{4,8},{8,12},{12,0},{1,5},{5,9},{9,13},{13,1},{2,6},{6,10},{... | collective-permute-start | bytes 393224 | tf_op jit(solution)/shard_map/ppermute | solution.py:346
  25.6 8.5 %copy-start.2 = (f32[2048]{0:T(1024)S(1)}, f32[2048]{0:T(1024)}, u32[]{:S(2)}) copy-start(f32[2048]{0:T(1024)} %param.15) | copy-start | bytes 24580
  25.6 8.4 %collective-permute-start.6 = (f32[2,128,128]{2,1,0:T(8,128)S(1)}, f32[2,128,128]{2,1,0:T(8,128)S(1)}, u32[]{:S(2)}, u32[]{:S(2)}) collective-permute-start(f32[2,128,128]{2,1,0:T(8,128)S(1)} %multiply_add_fusion.7), channel_id=1, source_target_pairs={{0,4},{4,8},{8,12},{12,0},{1,5},{5,9},{9,13},{13,1},{2,6},{6,10},{... | collective-permute-start | bytes 393224 | tf_op jit(solution)/shard_map/ppermute | solution.py:346
  28.4 8.4 %collective-permute-start.5 = (f32[2,128,128]{2,1,0:T(8,128)S(1)}, f32[2,128,128]{2,1,0:T(8,128)S(1)}, u32[]{:S(2)}, u32[]{:S(2)}) collective-permute-start(f32[2,128,128]{2,1,0:T(8,128)S(1)} %multiply_add_fusion.6), channel_id=1, source_target_pairs={{0,4},{4,8},{8,12},{12,0},{1,5},{5,9},{9,13},{13,1},{2,6},{6,10},{... | collective-permute-start | bytes 393224 | tf_op jit(solution)/shard_map/ppermute | solution.py:346
  31.2 8.4 %collective-permute-start.10 = (f32[2,128,128]{2,1,0:T(8,128)S(1)}, f32[2,128,128]{2,1,0:T(8,128)S(1)}, u32[]{:S(2)}, u32[]{:S(2)}) collective-permute-start(f32[2,128,128]{2,1,0:T(8,128)S(1)} %multiply_add_fusion.5), channel_id=1, source_target_pairs={{0,4},{4,8},{8,12},{12,0},{1,5},{5,9},{9,13},{13,1},{2,6},{6,10},{... | collective-permute-start | bytes 393224 | tf_op jit(solution)/shard_map/ppermute | solution.py:346
  34.1 8.4 %collective-permute-start.9 = (f32[2,128,128]{2,1,0:T(8,128)S(1)}, f32[2,128,128]{2,1,0:T(8,128)S(1)}, u32[]{:S(2)}, u32[]{:S(2)}) collective-permute-start(f32[2,128,128]{2,1,0:T(8,128)S(1)} %multiply_add_fusion.4), channel_id=1, source_target_pairs={{0,4},{4,8},{8,12},{12,0},{1,5},{5,9},{9,13},{13,1},{2,6},{6,10},{... | collective-permute-start | bytes 393224 | tf_op jit(solution)/shard_map/ppermute | solution.py:346
  36.9 8.4 %collective-permute-start.8 = (f32[2,128,128]{2,1,0:T(8,128)S(1)}, f32[2,128,128]{2,1,0:T(8,128)S(1)}, u32[]{:S(2)}, u32[]{:S(2)}) collective-permute-start(f32[2,128,128]{2,1,0:T(8,128)S(1)} %multiply_add_fusion.3), channel_id=1, source_target_pairs={{0,4},{4,8},{8,12},{12,0},{1,5},{5,9},{9,13},{13,1},{2,6},{6,10},{... | collective-permute-start | bytes 393224 | tf_op jit(solution)/shard_map/ppermute | solution.py:346
  39.7 8.4 %collective-permute-start.13 = (f32[2,128,128]{2,1,0:T(8,128)S(1)}, f32[2,128,128]{2,1,0:T(8,128)S(1)}, u32[]{:S(2)}, u32[]{:S(2)}) collective-permute-start(f32[2,128,128]{2,1,0:T(8,128)S(1)} %multiply_add_fusion.2), channel_id=1, source_target_pairs={{0,4},{4,8},{8,12},{12,0},{1,5},{5,9},{9,13},{13,1},{2,6},{6,10},{... | collective-permute-start | bytes 393224 | tf_op jit(solution)/shard_map/ppermute | solution.py:346
  42.5 8.5 %collective-permute-start.12 = (f32[2,128,128]{2,1,0:T(8,128)S(1)}, f32[2,128,128]{2,1,0:T(8,128)S(1)}, u32[]{:S(2)}, u32[]{:S(2)}) collective-permute-start(f32[2,128,128]{2,1,0:T(8,128)S(1)} %multiply_add_fusion.1), channel_id=1, source_target_pairs={{0,4},{4,8},{8,12},{12,0},{1,5},{5,9},{9,13},{13,1},{2,6},{6,10},{... | collective-permute-start | bytes 393224 | tf_op jit(solution)/shard_map/ppermute | solution.py:346
  45.3 7.5 %collective-permute-start.11 = (f32[2,128,128]{2,1,0:T(8,128)S(1)}, f32[2,128,128]{2,1,0:T(8,128)S(1)}, u32[]{:S(2)}, u32[]{:S(2)}) collective-permute-start(f32[2,128,128]{2,1,0:T(8,128)S(1)} %multiply_add_fusion), channel_id=1, source_target_pairs={{0,4},{4,8},{8,12},{12,0},{1,5},{5,9},{9,13},{13,1},{2,6},{6,10},{... | collective-permute-start | bytes 393224 | tf_op jit(solution)/shard_map/ppermute | solution.py:346
  52.3 21.9 %copy-start.8 = (s32[16]{0:T(128)S(1)}, s32[16]{0:T(128)}, u32[]{:S(2)}) copy-start(s32[16]{0:T(128)} %param.17) | copy-start | bytes 196
  54.2 5.0 %collective-permute-start.14 = (f32[16,2048]{1,0:T(8,128)S(1)}, f32[16,2048]{1,0:T(8,128)S(1)}, u32[]{:S(2)}, u32[]{:S(2)}) collective-permute-start(f32[16,2048]{1,0:T(8,128)S(1)} %constant_dynamic-update-slice_fusion), channel_id=1, source_target_pairs={{0,4},{4,0},{8,12},{12,8},{1,5},{5,1},{9,13},{13,9},{2,6},{6,2},{1... | collective-permute-start | bytes 393224 | tf_op jit(solution)/shard_map/ppermute | solution.py:211
  59.2 6.9 %collective-permute-start.15 = (f32[16,2048]{1,0:T(8,128)S(1)}, f32[16,2048]{1,0:T(8,128)S(1)}, u32[]{:S(2)}, u32[]{:S(2)}) collective-permute-start(f32[16,2048]{1,0:T(8,128)S(1)} %add.101), channel_id=1, source_target_pairs={{0,8},{4,12},{8,0},{12,4},{1,9},{5,13},{9,1},{13,5},{2,10},{6,14},... | collective-permute-start | bytes 393224 | tf_op jit(solution)/shard_map/ppermute | solution.py:211
  66.4 5.0 %collective-permute-start.16 = (f32[16,2048]{1,0:T(8,128)S(1)}, f32[16,2048]{1,0:T(8,128)S(1)}, u32[]{:S(2)}, u32[]{:S(2)}) collective-permute-start(f32[16,2048]{1,0:T(8,128)S(1)} %get-tuple-element.214), channel_id=1, source_target_pairs={{0,2},{2,0},{1,3},{3,1},{4,6},{6,4},{5,7},{7,5},{8,10},{10,8},{9,1... | collective-permute-start | bytes 393224 | tf_op jit(solution)/shard_map/ppermute | solution.py:211
  72.0 1.2 %collective-permute-start.17 = (f32[34,16]{0,1:T(8,128)S(1)}, f32[34,16]{0,1:T(8,128)S(1)}, u32[]{:S(2)}, u32[]{:S(2)}) collective-permute-start(f32[34,16]{0,1:T(8,128)S(1)} %pad_maximum_fusion), channel_id=1, source_target_pairs={{0,1},{1,0},{2,3},{3,2},{4,5},{5,4},{6,7},{7,6},{8,9},{9,8},{10,11... | collective-permute-start | bytes 6536 | tf_op jit(solution)/shard_map/ppermute | solution.py:211
